TPU v7x, 32 devices: a whole 2x2x4 slice. The times are simulated.
32 devices in a mesh: space: 16 (over z, y, x), sens: 2 (over core).
Axes of the slice: x: 2, y: 2, z: 4, core: 2. Of those that a mesh axis runs over, the one named last changes fastest.
Arguments:
- adjoint_end: float32 [16, 64, 64, 128], P('sens', 'space'), may hold values from -6 to 6
- checkpoints: float32 [8, 64, 64, 128], P('sens', 'space'), may hold values from 0.5 to 2
- dispersion: float32 [6, 64, 64, 128], P(None, 'space', 'sens'), as said below
- owner_steps: int32 [3], replicated, may hold values from 0 to 7, as said below
- sensor_cells: int32 [16], P('sens'), may hold values from 0 to 524287
- misfit: float32 [16, 3], P('sens'), may hold values from -6 to 6
- release_cells: int32 [128], replicated, may hold values from 0 to 524287
- release_steps: int32 [128], replicated, may hold values from 0 to 2
Outputs:
- adjoint: float32 [16, 64, 64, 128], P('sens', 'space')
- release_grad: float32 [16, 128], P('sens')
Inputs may be any that keep to these rules, and one draw needn't show every extreme that they name: `owner_steps`: the entries are different stored states; the first and the last stored state are always among them. `sensor_cells`: flat cell indices. `release_cells`: flat cell indices. `dispersion`: zz, yy and xx components are positive.
All inputs are finite; a program needn't handle non-finite values.
Results may differ from a plain program's by a relative error of at most 0.00002.
Values sent between devices are 32-bit elements; how exact they have to be, the bound alone decides.
No kernel may reach another device: no remote copies, remote signals or barrier semaphores. Data moves between devices by JAX's collectives and lax.ppermute only.
A program may use at most 128 MiB of HBM per device.

v0:
```python
import jax
import jax.numpy as jnp
from jax import lax
from jax.sharding import PartitionSpec as P

STEPS = 3


step_dt = 0.12


def extended(block, sides, width):
    for axis, dim in sides:
        count = lax.axis_size(axis)
        forward = [(i, i + 1) for i in range(count - 1)]
        backward = [(target, source) for source, target in forward]
        low = lax.ppermute(
            lax.slice_in_dim(block, block.shape[dim] - width, None, axis=dim), axis, forward
        )
        high = lax.ppermute(lax.slice_in_dim(block, 0, width, axis=dim), axis, backward)
        block = jnp.concatenate([low, block, high], axis=dim)
    return block


def broadcast(array, axis, root):
    mine = lax.axis_index(axis) == root
    return lax.psum(jnp.where(mine, array, jnp.zeros_like(array)), axis)


def retard_scale(conc):
    return step_dt / (1.0 + 0.5 * conc ** (-0.5))


def retard_slope(conc):
    retard = 1.0 + 0.5 * conc ** (-0.5)
    deriv = -0.25 * conc ** (-1.5)
    return -step_dt * deriv / (retard * retard)


def apply_op(field, tensor):
    depth = field.shape[1] - 2
    rows_y = field.shape[2]
    rows_x = field.shape[3]
    padded = jnp.pad(field, ((0, 0), (0, 0), (1, 1), (1, 1)))
    coeffs = jnp.pad(tensor, ((0, 0), (0, 0), (1, 1), (1, 1)))

    def at_shift(arr, shift):
        return arr[
            ...,
            1 + shift[0] : 1 + shift[0] + depth,
            1 + shift[1] : 1 + shift[1] + rows_y,
            1 + shift[2] : 1 + shift[2] + rows_x,
        ]

    units = [(1, 0, 0), (0, 1, 0), (0, 0, 1)]
    centre = (0, 0, 0)
    total = jnp.zeros((field.shape[0], depth, rows_y, rows_x), jnp.float32)
    for axis_id in range(3):
        plus = units[axis_id]
        minus = tuple((-v for v in plus))
        diag = coeffs[axis_id]
        a_plus = 0.5 * (at_shift(diag, centre) + at_shift(diag, plus))
        a_minus = 0.5 * (at_shift(diag, centre) + at_shift(diag, minus))
        total = total + a_plus * (at_shift(padded, plus) - at_shift(padded, centre))
        total = total - a_minus * (at_shift(padded, centre) - at_shift(padded, minus))
    for first, second, comp in ((0, 1, 3), (0, 2, 4), (1, 2, 5)):
        for outer, inner in ((first, second), (second, first)):
            unit_o = units[outer]
            unit_i = units[inner]
            for sign in (1, -1):
                spot = tuple((sign * v for v in unit_o))
                up_spot = tuple((spot[t] + unit_i[t] for t in range(3)))
                down_spot = tuple((spot[t] - unit_i[t] for t in range(3)))
                flux = at_shift(coeffs[comp], spot) * (
                    0.5 * (at_shift(padded, up_spot) - at_shift(padded, down_spot))
                )
                total = total + 0.5 * sign * flux
    return total


def add_misfit(field, column, sensor_cells, start_cell):
    count = field.shape[0]
    cells = field.shape[1] * field.shape[2] * field.shape[3]
    local = sensor_cells - start_cell
    positions = lax.broadcasted_iota(jnp.int32, (count, cells), 1)
    hit = positions == local[:, None]
    return field + jnp.where(hit, column[:, None], 0.0).reshape(field.shape)


def body(
    adjoint_end,
    checkpoints,
    dispersion,
    owner_steps,
    sensor_cells,
    misfit,
    release_cells,
    release_steps,
):
    own_sensors, depth, rows_y, rows_x = adjoint_end.shape
    slot_count = checkpoints.shape[0]
    cells = depth * rows_y * rows_x
    first_cell = lax.axis_index("space") * cells
    release_local = release_cells - first_cell
    release_inside = (release_local >= 0) & (release_local < cells)
    release_index = jnp.clip(release_local, 0, cells - 1)
    lam = adjoint_end
    partial_grad = jnp.zeros((own_sensors, release_cells.shape[0]), jnp.float32)
    whole = lax.all_gather(dispersion, "sens", axis=2, tiled=True)
    tensor = extended(whole, (("space", 1),), 1)
    for step in reversed(range(STEPS)):
        holder = owner_steps[step] // slot_count
        mine = lax.dynamic_index_in_dim(
            checkpoints, owner_steps[step] % slot_count, 0, keepdims=False
        )
        conc = broadcast(mine, "sens", holder)
        mixed = add_misfit(lam, misfit[:, step], sensor_cells, first_cell)
        scaled = retard_scale(conc) * mixed
        stacked = jnp.concatenate([conc[None], scaled], 0)
        rimmed = extended(stacked, (("space", 1),), 1)
        applied = apply_op(rimmed, tensor)
        lam = mixed + applied[1:] + retard_slope(conc) * applied[0] * mixed
        values = jnp.take(lam.reshape(own_sensors, cells), release_index, axis=1)
        keep = release_inside & (release_steps == step)
        partial_grad = partial_grad + jnp.where(keep[None, :], values, 0.0)
    release_grad = lax.psum(partial_grad, "space")
    return (lam, release_grad)


def solution(mesh):
    in_specs = (
        P("sens", "space", None, None),
        P("sens", "space", None, None),
        P(None, "space", "sens", None),
        P(),
        P("sens"),
        P("sens", None),
        P(),
        P(),
    )
    out_specs = (P("sens", "space", None, None), P("sens", None))
    return jax.shard_map(body, mesh=mesh, in_specs=in_specs, out_specs=out_specs, check_vma=False)
```

profile of v0, /device:TPU:0, one launch (start us, length us, event | category | flops | bytes accessed | tf_op | source)
XLA Modules:
  0.0 248.9 jit_solution(358271755512530131)
XLA Ops:
  7.2 2.8 %all_gather.3 = f32[6,4,64,128]{3,2,1,0:T(8,128)S(1)} all-gather(f32[6,4,32,128]{3,2,1,0:T(8,128)} %param.12), channel_id=1, replica_groups=mesh['space'=16,'sens'=2] {'sens'}, dimensions={2}, use_global_device_ids=true | all-gather | bytes 1179648 | tf_op jit(solution)/shard_map/all_gather | solution.py:109
  10.1 4.8 %collective-permute-start = (f32[6,1,64,128]{3,2,1,0:T(8,128)S(1)}, f32[6,1,64,128]{3,2,1,0:T(8,128)S(1)}, u32[]{:S(2)}, u32[]{:S(2)}) collective-permute-start(f32[6,1,64,128]{3,2,1,0:T(8,128)S(1)} %get-tuple-element.28), channel_id=1, source_target_pairs={{0,2},{2,4},{4,6},{6,8},{8,10},{10,12},{12,14},{14,16},{16,18},{18... | collective-permute-start | bytes 589832 | tf_op jit(solution)/shard_map/ppermute | solution.py:17
  14.8 1.3 collective-permute-start.1
  24.6 0.8 select_bitcast_fusion
  25.5 0.8 select_maximum_fusion.9
  26.2 1.2 slice_bitcast_fusion.5
  27.4 1.0 slice_multiply_fusion.11
  28.8 17.7 %all-reduce.7.cloned.1.call-done = (f32[4,64,128]{2,1,0:T(8,128)}, f32[4,64,128]{2,1,0:T(8,128)}, f32[4,64,128]{2,1,0:T(8,128)}) async-done(((f32[4,64,128]{2,1,0:T(8,128)}, f32[4,64,128]{2,1,0:T(8,128)}, f32[4,64,128]{2,1,0:T(8,128)}), (f32[4,64,128]{2,1,0:T(8,128)}, f32[4,64,128]{2,1,0:T(8,128)}, f32[4,64,128]{2,1,0:T(8,128)})) %all-reduce.7.cloned.1.call-update) | async-done | bytes 393232 | tf_op jit(solution)/shard_map/psum | solution.py:27
  46.5 1.0 fusion.107
  48.4 3.7 %collective-permute-start.3 = (f32[9,1,64,128]{3,2,1,0:T(8,128)S(1)}, f32[9,1,64,128]{3,2,1,0:T(8,128)S(1)}, u32[]{:S(2)}, u32[]{:S(2)}) collective-permute-start(f32[9,1,64,128]{3,2,1,0:T(8,128)S(1)} %get-tuple-element.26), channel_id=1, source_target_pairs={{0,2},{2,4},{4,6},{6,8},{8,10},{10,12},{12,14},{14,16},{16,18},{18... | collective-permute-start | bytes 884744 | tf_op jit(solution)/shard_map/ppermute | solution.py:17
  52.1 1.3 collective-permute-start.2
  53.9 11.3 %collective-permute-done.3 = f32[9,1,64,128]{3,2,1,0:T(8,128)S(1)} collective-permute-done((f32[9,1,64,128]{3,2,1,0:T(8,128)S(1)}, f32[9,1,64,128]{3,2,1,0:T(8,128)S(1)}, u32[]{:S(2)}, u32[]{:S(2)}) %collective-permute-start.3) | collective-permute-done | bytes 294944 | tf_op jit(solution)/shard_map/ppermute | solution.py:17
  65.1 1.9 collective-permute-done.2
  67.1 2.7 %select_maximum_fusion.6 = f32[9,6,66,130]{3,2,1,0:T(8,128)S(1)} fusion(f32[9,1,64,128]{3,2,1,0:T(8,128)S(1)} %collective-permute-done.2, f32[9,1,64,128]{3,2,1,0:T(8,128)S(1)} %collective-permute-done.3, f32[8,4,64,128]{3,2,1,0:T(8,128)S(1)} %fusion.89, f32[1,4,64,128]{3,2,1,0:T(8,128)S(1)} %bitcast.69), kind=kLoop, calls=%fused_computation.13 | loop fusion | flops 8339760 | bytes 3622752 | tf_op jit(solution)/shard_map/concatenate | solution.py:21
  69.9 4.7 %fusion.69 = f32[9,4,64,128]{3,2,1,0:T(8,128)S(1)} fusion(f32[9,6,66,130]{3,2,1,0:T(8,128)S(1)} %select_maximum_fusion.6, f32[9,1,64,128]{3,2,1,0:T(8,128)S(1)} %collective-permute-done.3, f32[8,4,64,128]{3,2,1,0:T(8,128)S(1)} %fusion.89, f32[1,4,64,128]{3,2,1,0:T(8,128)S(1)} %bitcast.70, f32[9,1,64,128]{3,2,1,0:T(8,128)S(1)} %collective-permute-done.2, ...), kind=kLoop, calls=%fused_computation.120 | loop fusion | flops 20643840 | bytes 24182784 | tf_op jit(solution)/shard_map/add | solution.py:77
  75.3 3.4 %collective-permute-start.5 = (f32[9,1,64,128]{3,2,1,0:T(8,128)S(1)}, f32[9,1,64,128]{3,2,1,0:T(8,128)S(1)}, u32[]{:S(2)}, u32[]{:S(2)}) collective-permute-start(f32[9,1,64,128]{3,2,1,0:T(8,128)S(1)} %get-tuple-element.24), channel_id=1, source_target_pairs={{0,2},{2,4},{4,6},{6,8},{8,10},{10,12},{12,14},{14,16},{16,18},{18... | collective-permute-start | bytes 884744 | tf_op jit(solution)/shard_map/ppermute | solution.py:17
  78.7 1.5 collective-permute-start.4
  80.9 10.0 %collective-permute-done.5 = f32[9,1,64,128]{3,2,1,0:T(8,128)S(1)} collective-permute-done((f32[9,1,64,128]{3,2,1,0:T(8,128)S(1)}, f32[9,1,64,128]{3,2,1,0:T(8,128)S(1)}, u32[]{:S(2)}, u32[]{:S(2)}) %collective-permute-start.5) | collective-permute-done | bytes 294944 | tf_op jit(solution)/shard_map/ppermute | solution.py:17
  91.6 2.7 %select_maximum_fusion.3 = f32[9,6,66,130]{3,2,1,0:T(8,128)S(1)} fusion(f32[9,1,64,128]{3,2,1,0:T(8,128)S(1)} %collective-permute-done.4, f32[9,1,64,128]{3,2,1,0:T(8,128)S(1)} %collective-permute-done.5, f32[8,4,64,128]{3,2,1,0:T(8,128)S(1)} %get-tuple-element.14, f32[1,4,64,128]{3,2,1,0:T(8,128)S(1)} %bitcast.66), kind=kLoop, calls=%fused_computation.10 | loop fusion | flops 8339760 | bytes 3622752 | tf_op jit(solution)/shard_map/concatenate | solution.py:21
  94.4 4.7 %fusion.44 = f32[9,4,64,128]{3,2,1,0:T(8,128)S(1)} fusion(f32[9,6,66,130]{3,2,1,0:T(8,128)S(1)} %select_maximum_fusion.3, f32[9,1,64,128]{3,2,1,0:T(8,128)S(1)} %collective-permute-done.5, f32[8,4,64,128]{3,2,1,0:T(8,128)S(1)} %get-tuple-element.14, f32[1,4,64,128]{3,2,1,0:T(8,128)S(1)} %bitcast.67, f32[9,1,64,128]{3,2,1,0:T(8,128)S(1)} %collective-permute-done.4, ...), kind=kLoop, calls=%fused_computation.87 | loop fusion | flops 20643840 | bytes 24182784 | tf_op jit(solution)/shard_map/add | solution.py:77
  99.8 0.8 fusion.91
  100.6 4.3 %collective-permute-start.7 = (f32[9,1,64,128]{3,2,1,0:T(8,128)}, f32[9,1,64,128]{3,2,1,0:T(8,128)}, u32[]{:S(2)}, u32[]{:S(2)}) collective-permute-start(f32[9,1,64,128]{3,2,1,0:T(8,128)} %get-tuple-element.22), channel_id=1, source_target_pairs={{0,2},{2,4},{4,6},{6,8},{8,10},{10,12},{12,14},{14,16},{16,18},{18... | collective-permute-start | bytes 884744 | tf_op jit(solution)/shard_map/ppermute | solution.py:17
  105.0 1.3 collective-permute-start.6
  106.8 8.7 %copy.10 = f32[8,4,64,128]{0,3,2,1:T(8,128)} copy(f32[8,4,64,128]{3,2,1,0:T(8,128)S(1)} %get-tuple-element.15) | data formatting | bytes 2097152 | tf_op jit(solution)/shard_map/add | solution.py:122
  115.5 7.0 %gather_fusion = f32[128,8]{1,0:T(8,128)} fusion(f32[8,32768]{0,1:T(8,128)} %bitcast.59, s32[1024]{0:T(1024)S(1)} %pad_clamp_fusion), kind=kCustom, calls=%fused_computation.clone | custom fusion | bytes 8704 | tf_op jit(solution)/shard_map/jit(_take)/gather | solution.py:123
  122.5 8.7 %copy.11 = f32[8,4,64,128]{0,3,2,1:T(8,128)} copy(f32[8,4,64,128]{3,2,1,0:T(8,128)S(1)} %get-tuple-element.13) | data formatting | bytes 2097152 | tf_op jit(solution)/shard_map/add | solution.py:122
  131.1 7.0 %gather_fusion.1 = f32[128,8]{1,0:T(8,128)} fusion(f32[8,32768]{0,1:T(8,128)} %bitcast.61, s32[1024]{0:T(1024)S(1)} %pad_clamp_fusion), kind=kCustom, calls=%fused_computation.1.clone | custom fusion | bytes 8704 | tf_op jit(solution)/shard_map/jit(_take)/gather | solution.py:123
  138.3 3.9 %select_maximum_fusion = f32[9,6,66,130]{3,2,1,0:T(8,128)S(1)} fusion(f32[9,1,64,128]{3,2,1,0:T(8,128)} %collective-permute-done.6, f32[9,1,64,128]{3,2,1,0:T(8,128)} %collective-permute-done.7, f32[8,4,64,128]{3,2,1,0:T(8,128)S(1)} %get-tuple-element.12, f32[1,4,64,128]{3,2,1,0:T(8,128)S(1)} %bitcast.63), kind=kLoop, calls=%fused_computation.7 | loop fusion | flops 8339760 | bytes 3622752 | tf_op jit(solution)/shard_map/concatenate | solution.py:21
  142.4 5.7 %fusion.19 = f32[9,4,64,128]{3,2,1,0:T(8,128)S(1)} fusion(f32[9,6,66,130]{3,2,1,0:T(8,128)S(1)} %select_maximum_fusion, f32[9,1,64,128]{3,2,1,0:T(8,128)} %collective-permute-done.7, f32[8,4,64,128]{3,2,1,0:T(8,128)S(1)} %get-tuple-element.12, f32[1,4,64,128]{3,2,1,0:T(8,128)S(1)} %bitcast.64, f32[9,1,64,128]{3,2,1,0:T(8,128)} %collective-permute-done.6, ...), kind=kLoop, calls=%fused_computation.54 | loop fusion | flops 20643840 | bytes 24182784 | tf_op jit(solution)/shard_map/add | solution.py:77
  148.6 8.7 %copy.12 = f32[8,4,64,128]{0,3,2,1:T(8,128)} copy(f32[8,4,64,128]{3,2,1,0:T(8,128)S(1)} %fusion.84) | data formatting | bytes 2097152 | tf_op jit(solution)/shard_map/add | solution.py:122
  157.4 6.4 %gather_fusion.2 = f32[128,8]{1,0:T(8,128)S(1)} fusion(f32[8,32768]{0,1:T(8,128)} %bitcast.60, s32[1024]{0:T(1024)S(1)} %pad_clamp_fusion), kind=kCustom, calls=%fused_computation.2.clone | custom fusion | bytes 8704 | tf_op jit(solution)/shard_map/jit(_take)/gather | solution.py:123
  164.0 77.5 %psum.31 = f32[8,128]{0,1:T(8,128)S(1)} all-reduce(f32[8,128]{0,1:T(8,128)S(1)} %fusion.108), channel_id=1, replica_groups=mesh['space'=16,'sens'=2] {'space'}, use_global_device_ids=true, to_apply=%region_3.5 | all-reduce | flops 1024 | bytes 8192 | tf_op jit(solution)/shard_map/psum | solution.py:126
  (152 shorter events, 7.1 us)
Async XLA Ops:
  7.2 17.4 %copy-start.50 = (f32[4,4,64,128]{3,2,1,0:T(8,128)S(1)}, f32[4,4,64,128]{3,2,1,0:T(8,128)}, u32[]{:S(2)}) copy-start(f32[4,4,64,128]{3,2,1,0:T(8,128)} %param.11) | copy-start | bytes 1572868
  7.2 39.3 %all-reduce.7.cloned.1.call-start = ((), (), s32[]{:S(2)}) async-start(), calls=%async_computation | async-start | bytes 786432 | tf_op jit(solution)/shard_map/psum | solution.py:27
  10.0 15.4 %copy-start.58 = (f32[8,3]{0,1:T(4,128)S(1)}, f32[8,3]{0,1:T(4,128)}, u32[]{:S(2)}) copy-start(f32[8,3]{0,1:T(4,128)} %param.15) | copy-start | bytes 292
  10.0 15.4 %copy-start.60 = (s32[8]{0:T(128)S(1)}, s32[8]{0:T(128)}, u32[]{:S(2)}) copy-start(s32[8]{0:T(128)} %param.14) | copy-start | bytes 100
  10.1 15.4 %collective-permute-start = (f32[6,1,64,128]{3,2,1,0:T(8,128)S(1)}, f32[6,1,64,128]{3,2,1,0:T(8,128)S(1)}, u32[]{:S(2)}, u32[]{:S(2)}) collective-permute-start(f32[6,1,64,128]{3,2,1,0:T(8,128)S(1)} %get-tuple-element.28), channel_id=1, source_target_pairs={{0,2},{2,4},{4,6},{6,8},{8,10},{10,12},{12,14},{14,16},{16,18},{18... | collective-permute-start | bytes 589832 | tf_op jit(solution)/shard_map/ppermute | solution.py:17
  14.8 10.6 %collective-permute-start.1 = (f32[6,1,64,128]{3,2,1,0:T(8,128)S(1)}, f32[6,1,64,128]{3,2,1,0:T(8,128)S(1)}, u32[]{:S(2)}, u32[]{:S(2)}) collective-permute-start(f32[6,1,64,128]{3,2,1,0:T(8,128)S(1)} %get-tuple-element.29), channel_id=1, source_target_pairs={{2,0},{4,2},{6,4},{8,6},{10,8},{12,10},{14,12},{16,14},{18,16},{20... | collective-permute-start | bytes 589832 | tf_op jit(solution)/shard_map/ppermute | solution.py:20
  28.4 41.3 %copy-start.33 = (f32[4,64,128]{2,1,0:T(8,128)}, f32[4,64,128]{2,1,0:T(8,128)S(1)}, u32[]{:S(2)}) copy-start(f32[4,64,128]{2,1,0:T(8,128)S(1)} %get-tuple-element.39) | copy-start | bytes 393220
  28.5 41.3 %copy-start.36 = (f32[4,64,128]{2,1,0:T(8,128)}, f32[4,64,128]{2,1,0:T(8,128)S(1)}, u32[]{:S(2)}) copy-start(f32[4,64,128]{2,1,0:T(8,128)S(1)} %get-tuple-element.40) | copy-start | bytes 393220
  28.5 41.3 %copy-start.39 = (f32[4,64,128]{2,1,0:T(8,128)}, f32[4,64,128]{2,1,0:T(8,128)S(1)}, u32[]{:S(2)}) copy-start(f32[4,64,128]{2,1,0:T(8,128)S(1)} %get-tuple-element.41) | copy-start | bytes 393220
  28.5 19.0 %copy-start.1 = (f32[8,4,64,128]{3,2,1,0:T(8,128)S(1)}, f32[8,4,64,128]{3,2,1,0:T(8,128)}, u32[]{:S(2)}) copy-start(f32[8,4,64,128]{3,2,1,0:T(8,128)} %param.10) | copy-start | bytes 3145732
  28.7 41.0 %copy-start.7 = (f32[4,64,128]{2,1,0:T(8,128)}, f32[4,64,128]{2,1,0:T(8,128)S(1)}, u32[]{:S(2)}) copy-start(f32[4,64,128]{2,1,0:T(8,128)S(1)} %get-tuple-element.49) | copy-start | bytes 393220
  28.8 41.0 %copy-start.10 = (f32[4,64,128]{2,1,0:T(8,128)}, f32[4,64,128]{2,1,0:T(8,128)S(1)}, u32[]{:S(2)}) copy-start(f32[4,64,128]{2,1,0:T(8,128)S(1)} %get-tuple-element.50) | copy-start | bytes 393220
  28.8 41.0 %copy-start.13 = (f32[4,64,128]{2,1,0:T(8,128)}, f32[4,64,128]{2,1,0:T(8,128)S(1)}, u32[]{:S(2)}) copy-start(f32[4,64,128]{2,1,0:T(8,128)S(1)} %get-tuple-element.61) | copy-start | bytes 393220
  28.8 41.0 %copy-start.16 = (f32[4,64,128]{2,1,0:T(8,128)}, f32[4,64,128]{2,1,0:T(8,128)S(1)}, u32[]{:S(2)}) copy-start(f32[4,64,128]{2,1,0:T(8,128)S(1)} %get-tuple-element.62) | copy-start | bytes 393220
  28.8 41.0 %copy-start.19 = (f32[4,64,128]{2,1,0:T(8,128)}, f32[4,64,128]{2,1,0:T(8,128)S(1)}, u32[]{:S(2)}) copy-start(f32[4,64,128]{2,1,0:T(8,128)S(1)} %get-tuple-element.63) | copy-start | bytes 393220
  28.8 41.0 %copy-start.22 = (f32[4,64,128]{2,1,0:T(8,128)}, f32[4,64,128]{2,1,0:T(8,128)S(1)}, u32[]{:S(2)}) copy-start(f32[4,64,128]{2,1,0:T(8,128)S(1)} %get-tuple-element.64) | copy-start | bytes 393220
  28.8 65.5 %copy-start.5 = (f32[4,64,128]{2,1,0:T(8,128)}, f32[4,64,128]{2,1,0:T(8,128)S(1)}, u32[]{:S(2)}) copy-start(f32[4,64,128]{2,1,0:T(8,128)S(1)} %get-tuple-element.48) | copy-start | bytes 393220
  48.4 16.7 %collective-permute-start.3 = (f32[9,1,64,128]{3,2,1,0:T(8,128)S(1)}, f32[9,1,64,128]{3,2,1,0:T(8,128)S(1)}, u32[]{:S(2)}, u32[]{:S(2)}) collective-permute-start(f32[9,1,64,128]{3,2,1,0:T(8,128)S(1)} %get-tuple-element.26), channel_id=1, source_target_pairs={{0,2},{2,4},{4,6},{6,8},{8,10},{10,12},{12,14},{14,16},{16,18},{18... | collective-permute-start | bytes 884744 | tf_op jit(solution)/shard_map/ppermute | solution.py:17
  52.1 14.9 %collective-permute-start.2 = (f32[9,1,64,128]{3,2,1,0:T(8,128)S(1)}, f32[9,1,64,128]{3,2,1,0:T(8,128)S(1)}, u32[]{:S(2)}, u32[]{:S(2)}) collective-permute-start(f32[9,1,64,128]{3,2,1,0:T(8,128)S(1)} %get-tuple-element.27), channel_id=1, source_target_pairs={{2,0},{4,2},{6,4},{8,6},{10,8},{12,10},{14,12},{16,14},{18,16},{20... | collective-permute-start | bytes 884744 | tf_op jit(solution)/shard_map/ppermute | solution.py:20
  53.7 40.6 %copy-start.25 = (f32[4,64,128]{2,1,0:T(8,128)}, f32[4,64,128]{2,1,0:T(8,128)S(1)}, u32[]{:S(2)}) copy-start(f32[4,64,128]{2,1,0:T(8,128)S(1)} %get-tuple-element.35) | copy-start | bytes 393220
  53.7 40.6 %copy-start.27 = (f32[4,64,128]{2,1,0:T(8,128)}, f32[4,64,128]{2,1,0:T(8,128)S(1)}, u32[]{:S(2)}) copy-start(f32[4,64,128]{2,1,0:T(8,128)S(1)} %get-tuple-element.36) | copy-start | bytes 393220
  53.8 40.6 %copy-start.29 = (f32[4,64,128]{2,1,0:T(8,128)}, f32[4,64,128]{2,1,0:T(8,128)S(1)}, u32[]{:S(2)}) copy-start(f32[4,64,128]{2,1,0:T(8,128)S(1)} %get-tuple-element.67) | copy-start | bytes 393220
  53.8 40.6 %copy-start.31 = (f32[4,64,128]{2,1,0:T(8,128)}, f32[4,64,128]{2,1,0:T(8,128)S(1)}, u32[]{:S(2)}) copy-start(f32[4,64,128]{2,1,0:T(8,128)S(1)} %get-tuple-element.68) | copy-start | bytes 393220
  53.9 16.0 %copy-start.42 = (f32[4,64,128]{2,1,0:T(8,128)S(1)}, f32[4,64,128]{2,1,0:T(8,128)}, u32[]{:S(2)}) copy-start(f32[4,64,128]{2,1,0:T(8,128)} %get-tuple-element.42) | copy-start | bytes 393220
  53.9 16.0 %copy-start.44 = (f32[4,64,128]{2,1,0:T(8,128)S(1)}, f32[4,64,128]{2,1,0:T(8,128)}, u32[]{:S(2)}) copy-start(f32[4,64,128]{2,1,0:T(8,128)} %get-tuple-element.65) | copy-start | bytes 393220
  53.9 16.0 %copy-start.46 = (f32[4,64,128]{2,1,0:T(8,128)S(1)}, f32[4,64,128]{2,1,0:T(8,128)}, u32[]{:S(2)}) copy-start(f32[4,64,128]{2,1,0:T(8,128)} %get-tuple-element.66) | copy-start | bytes 393220
  75.3 15.6 %collective-permute-start.5 = (f32[9,1,64,128]{3,2,1,0:T(8,128)S(1)}, f32[9,1,64,128]{3,2,1,0:T(8,128)S(1)}, u32[]{:S(2)}, u32[]{:S(2)}) collective-permute-start(f32[9,1,64,128]{3,2,1,0:T(8,128)S(1)} %get-tuple-element.24), channel_id=1, source_target_pairs={{0,2},{2,4},{4,6},{6,8},{8,10},{10,12},{12,14},{14,16},{16,18},{18... | collective-permute-start | bytes 884744 | tf_op jit(solution)/shard_map/ppermute | solution.py:17
  78.7 12.9 %collective-permute-start.4 = (f32[9,1,64,128]{3,2,1,0:T(8,128)S(1)}, f32[9,1,64,128]{3,2,1,0:T(8,128)S(1)}, u32[]{:S(2)}, u32[]{:S(2)}) collective-permute-start(f32[9,1,64,128]{3,2,1,0:T(8,128)S(1)} %get-tuple-element.25), channel_id=1, source_target_pairs={{2,0},{4,2},{6,4},{8,6},{10,8},{12,10},{14,12},{16,14},{18,16},{20... | collective-permute-start | bytes 884744 | tf_op jit(solution)/shard_map/ppermute | solution.py:20
  100.6 37.6 %collective-permute-start.7 = (f32[9,1,64,128]{3,2,1,0:T(8,128)}, f32[9,1,64,128]{3,2,1,0:T(8,128)}, u32[]{:S(2)}, u32[]{:S(2)}) collective-permute-start(f32[9,1,64,128]{3,2,1,0:T(8,128)} %get-tuple-element.22), channel_id=1, source_target_pairs={{0,2},{2,4},{4,6},{6,8},{8,10},{10,12},{12,14},{14,16},{16,18},{18... | collective-permute-start | bytes 884744 | tf_op jit(solution)/shard_map/ppermute | solution.py:17
  105.0 33.3 %collective-permute-start.6 = (f32[9,1,64,128]{3,2,1,0:T(8,128)}, f32[9,1,64,128]{3,2,1,0:T(8,128)}, u32[]{:S(2)}, u32[]{:S(2)}) collective-permute-start(f32[9,1,64,128]{3,2,1,0:T(8,128)} %get-tuple-element.23), channel_id=1, source_target_pairs={{2,0},{4,2},{6,4},{8,6},{10,8},{12,10},{14,12},{16,14},{18,16},{20... | collective-permute-start | bytes 884744 | tf_op jit(solution)/shard_map/ppermute | solution.py:20
  148.6 15.2 %copy-start.51 = (f32[128,8]{1,0:T(8,128)S(1)}, f32[128,8]{1,0:T(8,128)}, u32[]{:S(2)}) copy-start(f32[128,8]{1,0:T(8,128)} %gather_fusion) | copy-start | bytes 12292
  148.6 15.2 %copy-start.52 = (f32[128,8]{1,0:T(8,128)S(1)}, f32[128,8]{1,0:T(8,128)}, u32[]{:S(2)}) copy-start(f32[128,8]{1,0:T(8,128)} %gather_fusion.1) | copy-start | bytes 12292
  (38 other events, 287.9 us)
Sparse Core Ops, SparseCore 0:
  25.5 20.9 all-reduce.6
where the time goes:
time: 250 us; the launch traced here: 249 us
  blocking collectives  80.2 us (32%)
  local copies, waits for them, and re-layouts  49.8 us (20%)
  waiting for transfers between devices  41.6 us (17%)
  other arithmetic  32.7 us (13%)
  between operations  23 us (9%)
  starting transfers between devices  21.6 us (9%)
    psum x1, blocking collectives, body(): release_grad = lax.psum(partial_grad, 'space')  77.5 us
    add x3, local copies, waits for them, and re-layouts, body(): lam = mixed + applied[1:] + retard_slope(conc) * applied[0] * mixed  26 us
    ppermute x4, waiting for transfers between devices, extended(): lax.ppermute(lax.slice_in_dim(block, block.shape[dim] - width, None, axis...  21.2 us
    gather x3, local copies, waits for them, and re-layouts, body(): values = jnp.take(lam.reshape(own_sensors, cells), release_index, axis=1)  20.4 us
    psum x1, waiting for transfers between devices, broadcast(): return lax.psum(jnp.where(mine, array, jnp.zeros_like(array)), axis)  17.7 us
    ppermute x4, starting transfers between devices, extended(): lax.ppermute(lax.slice_in_dim(block, block.shape[dim] - width, None, axis...  16.2 us
    add x3, other arithmetic, apply_op(): total = total + 0.5 * sign * flux  15 us
    concatenate x4, other arithmetic, extended(): block = jnp.concatenate([low, block, high], axis=dim)  9.99 us
  transfers between devices with their start and end apart: 9, of which 5 were waited for; matrix products, arithmetic and copies ran while one was open for 15% of the time, Pallas kernels for 0%

commit v1 on v0

v1 whole, which is shorter than its diff:
```python
import functools

import jax
import jax.numpy as jnp
from jax import lax
from jax.experimental import pallas as pl
from jax.experimental.pallas import tpu as pltpu
from jax.sharding import PartitionSpec as P

STEPS = 3
DT = 0.12
PAD = 8
TILE = 8
CENTRE, ZP, ZM, YP, YM, ZPYP, ZPYM, ZMYP, ZMYM = range(9)
XP, XPZP, XPZM, XPYP, XPYM, XM, XMZP, XMZM, XMYP, XMYM = range(9, 19)
PLANES = 19
LOW = (ZM, ZMYP, ZMYM, XPZM, XMZM)
HIGH = (ZP, ZPYP, ZPYM, XPZP, XMZP)

VMEM = pl.BlockSpec(memory_space=pltpu.VMEM)
SMEM = pl.BlockSpec(memory_space=pltpu.SMEM)
ANY = pl.BlockSpec(memory_space=pl.ANY)


def f32(*shape):
    return jax.ShapeDtypeStruct(shape, jnp.float32)


def params(mib):
    return pltpu.CompilerParams(vmem_limit_bytes=mib * 1024 * 1024)


def cost(flops, moved):
    return pl.CostEstimate(flops=flops, bytes_accessed=moved, transcendentals=0)


def owned(owner_ref, slots):
    me = lax.axis_index("sens")
    o0, o1, o2 = (owner_ref[i] for i in range(3))
    own0 = lax.div(o0, slots) == me
    own1 = lax.div(o1, slots) == me
    first = jnp.where(own0, o0, jnp.where(own1, o1, o2))
    second = jnp.where(own0 & own1, o1, o2)
    return lax.rem(first, slots), lax.rem(second, slots)


def parity():
    return lax.rem(lax.axis_index("space"), 2)


def pack_kernel(owner, adj, ckpt, disp, lam_a, lam_b, small_a, small_b, states, sems):
    depth, rows_y = adj.shape[1], adj.shape[2]
    rows = disp.shape[2]
    even = parity() == 0
    z_a = jnp.where(even, depth - 1, 0)
    z_b = jnp.where(even, 0, depth - 1)
    held = owned(owner, ckpt.shape[0])
    moves = []
    for z, small in ((z_a, small_a), (z_b, small_b)):
        for j in range(2):
            moves.append((ckpt.at[held[j], z], small.at[pl.ds(j * rows_y, rows_y)]))
        for j, comp in enumerate((0, 3, 4)):
            moves.append((disp.at[comp, z], small.at[pl.ds(2 * rows_y + j * rows, rows)]))
    for j in range(2):
        moves.append((ckpt.at[held[j]], states.at[j]))
    moves.append((adj.at[:, z_a], lam_a))
    moves.append((adj.at[:, z_b], lam_b))
    copies = [pltpu.make_async_copy(s, d, sems.at[i]) for i, (s, d) in enumerate(moves)]
    for c in copies:
        c.start()
    for c in copies:
        c.wait()


def pack(owner, adj, ckpt, disp):
    own, depth, rows_y, rows_x = adj.shape
    rows = disp.shape[2]
    small = f32(2 * rows_y + 3 * rows, rows_x)
    return pl.pallas_call(
        pack_kernel,
        in_specs=[SMEM, ANY, ANY, ANY],
        out_specs=[ANY] * 5,
        out_shape=[f32(own, rows_y, rows_x)] * 2 + [small, small, f32(2, depth, rows_y, rows_x)],
        scratch_shapes=[pltpu.SemaphoreType.DMA((14,))],
        compiler_params=params(16),
        name="pack",
    )(owner, adj, ckpt, disp)


def lane_masks(shape):
    lanes = lax.broadcasted_iota(jnp.int32, shape, len(shape) - 1)
    return lanes >= 1, lanes < shape[-1] - 1


def before(value, keep):
    return jnp.where(keep, pltpu.roll(value, 1, axis=value.ndim - 1), 0.0)


def after(value, keep):
    return jnp.where(keep, pltpu.roll(value, value.shape[-1] - 1, axis=value.ndim - 1), 0.0)


def planes_at(window, keep_b, keep_a):
    def yy(dy):
        return window(1, 0, dy)

    c = [None] * PLANES
    zz, zzp, zzm = window(0, 0, 0), window(0, 1, 0), window(0, -1, 0)
    xx = window(2, 0, 0)
    c[ZP], c[ZM] = 0.5 * (zz + zzp), 0.5 * (zz + zzm)
    c[YP], c[YM] = 0.5 * (yy(0) + yy(1)), 0.5 * (yy(0) + yy(-1))
    xx_b, xx_a = before(xx, keep_b), after(xx, keep_a)
    c[XP] = jnp.where(keep_b, 0.5 * (xx_b + xx), 0.0)
    c[XM] = jnp.where(keep_a, 0.5 * (xx_a + xx), 0.0)
    c[CENTRE] = -(c[ZP] + c[ZM] + c[YP] + c[YM] + (xx + 0.5 * (xx_a + xx_b)))
    zp, zm, yp, ym = window(3, 1, 0), window(3, -1, 0), window(3, 0, 1), window(3, 0, -1)
    c[ZPYP], c[ZPYM] = 0.25 * (zp + yp), -0.25 * (zp + ym)
    c[ZMYP], c[ZMYM] = -0.25 * (zm + yp), 0.25 * (zm + ym)
    for comp, plus, minus, names in (
        (4, window(4, 1, 0), window(4, -1, 0), (XPZP, XPZM, XMZP, XMZM)),
        (5, window(5, 0, 1), window(5, 0, -1), (XPYP, XPYM, XMYP, XMYM)),
    ):
        here = window(comp, 0, 0)
        c[names[0]] = jnp.where(keep_b, 0.25 * (before(plus, keep_b) + here), 0.0)
        c[names[1]] = jnp.where(keep_b, -0.25 * (before(minus, keep_b) + here), 0.0)
        c[names[2]] = jnp.where(keep_a, -0.25 * (after(plus, keep_a) + here), 0.0)
        c[names[3]] = jnp.where(keep_a, 0.25 * (after(minus, keep_a) + here), 0.0)
    return c


def stencil(c, u):
    near = {(dz, dy): u(dz, dy) for dz in (-1, 0, 1) for dy in (-1, 0, 1)}
    here = c[CENTRE] * near[0, 0] + c[ZP] * near[1, 0] + c[ZM] * near[-1, 0]
    here += c[YP] * near[0, 1] + c[YM] * near[0, -1]
    here += c[ZPYP] * near[1, 1] + c[ZPYM] * near[1, -1]
    here += c[ZMYP] * near[-1, 1] + c[ZMYM] * near[-1, -1]
    right = c[XP] * near[0, 0] + c[XPZP] * near[1, 0] + c[XPZM] * near[-1, 0]
    right += c[XPYP] * near[0, 1] + c[XPYM] * near[0, -1]
    left = c[XM] * near[0, 0] + c[XMZP] * near[1, 0] + c[XMZM] * near[-1, 0]
    left += c[XMYP] * near[0, 1] + c[XMYM] * near[0, -1]
    width = here.shape[-1]
    return here + pltpu.roll(right, width - 1, axis=1) + pltpu.roll(left, 1, axis=1)


def scale_of(conc):
    root = jnp.sqrt(conc)
    return DT * root / (root + 0.5)


def slope_of(conc):
    root = jnp.sqrt(conc)
    return (0.25 * DT) / (root * (root + 0.5) * (root + 0.5))


def planes_kernel(count, slot_count, *refs):
    owner, cells = refs[:2]
    parts, states = refs[2 : 2 + count], refs[2 + count : 2 + 2 * count]
    small = refs[2 + 2 * count : 2 + 3 * count], refs[2 + 3 * count : 2 + 4 * count]
    coef, edge, gain, scale, rim, inside, full, conc = refs[2 + 4 * count :]
    depth, rows_y, rows_x = coef.shape[1:]
    rows = rows_y // count
    me = lax.axis_index("sens")
    even = parity() == 0
    z_a = jnp.where(even, depth + 1, 0)
    z_b = jnp.where(even, 0, depth + 1)
    inner = pl.ds(PAD, rows_y)

    blank = jnp.zeros((PAD, rows_x), jnp.float32)
    for ref in (full, conc):
        for i in range(ref.shape[0]):
            for z in range(depth + 2):
                ref[i, z, pl.ds(0, PAD)] = blank
                ref[i, z, pl.ds(PAD + rows_y, PAD)] = blank
    for side in range(2):
        for j in range(5):
            edge[side, j, pl.ds(0, PAD)] = blank
            edge[side, j, pl.ds(PAD + rows_y, PAD)] = blank
    for k in range(count):
        who = lax.rem(me - k + count, count)
        span = pl.ds(pl.multiple_of(PAD + who * rows, PAD), rows)
        for comp in range(6):
            for z in range(depth):
                full[comp, z + 1, span] = parts[k][comp, z]
        for j, comp in enumerate((0, 3, 4)):
            here = pl.ds(2 * rows_y + j * rows, rows)
            full[comp, z_a, span] = small[0][k][here]
            full[comp, z_b, span] = small[1][k][here]
    holders = [lax.div(owner[i], slot_count) for i in range(STEPS)]
    for i in range(STEPS):
        slot = jnp.int32(0)
        for j in range(i):
            slot += jnp.where(holders[j] == holders[i], 1, 0)
        slot = jnp.minimum(slot, 1)
        turn = lax.rem(me - holders[i] + count, count)
        for k in range(count):

            @pl.when(turn == k)
            def _(i=i, k=k, slot=slot):
                conc[i, pl.ds(1, depth), inner] = states[k][slot]
                span = pl.ds(pl.multiple_of(slot * rows_y, PAD), rows_y)
                conc[i, z_a, inner] = small[0][k][span]
                conc[i, z_b, inner] = small[1][k][span]

    plane = rows_y * rows_x
    start = lax.axis_index("space") * (depth * plane)

    def note(r, found):
        local = cells[r] - start

        @pl.when((local >= -plane) & (local < (depth + 1) * plane))
        def _():
            inside[found] = r

        return found + jnp.where((local >= -plane) & (local < (depth + 1) * plane), 1, 0)

    last = inside.shape[0] - 1
    inside[last] = lax.fori_loop(0, cells.shape[0], note, jnp.int32(0))

    keep_b, keep_a = lane_masks((TILE, rows_x))

    def layer(z, carry):
        for tile in range(rows_y // TILE):
            at = pl.ds(tile * TILE, TILE)

            def window(comp, dz, dy):
                return full[comp, z + 1 + dz, pl.ds(PAD + tile * TILE + dy, TILE)]

            c = planes_at(window, keep_b, keep_a)
            for j in range(PLANES):
                coef[j, z, at] = c[j]
            for i in range(STEPS):
                here = conc[i, z + 1, pl.ds(PAD + tile * TILE, TILE)]
                spread = stencil(
                    c, lambda dz, dy: conc[i, z + 1 + dz, pl.ds(PAD + tile * TILE + dy, TILE)]
                )
                scale[i, z, at] = scale_of(here)
                gain[i, z, at] = 1.0 + slope_of(here) * spread
        return carry

    lax.fori_loop(0, depth, layer, 0)
    for side, z, names in ((0, 0, LOW), (1, depth - 1, HIGH)):
        for j in range(5):
            edge[side, j, inner] = coef[names[j], z]
        rim[side] = scale_of(conc[STEPS - 1, side * (depth + 1), inner])


def planes(owner, cells, parts, states, small_a, small_b, slot_count):
    count = len(parts)
    depth, rows_y, rows_x = states[0].shape[1:]
    grown = rows_y + 2 * PAD
    return pl.pallas_call(
        functools.partial(planes_kernel, count, slot_count),
        in_specs=[SMEM, SMEM] + [VMEM] * (4 * count),
        out_specs=[VMEM] * 5 + [SMEM],
        out_shape=[
            f32(PLANES, depth, rows_y, rows_x),
            f32(2, 5, grown, rows_x),
            f32(STEPS, depth, rows_y, rows_x),
            f32(STEPS, depth, rows_y, rows_x),
            f32(2, rows_y, rows_x),
            jax.ShapeDtypeStruct((cells.shape[0] + 1,), jnp.int32),
        ],
        scratch_shapes=[
            pltpu.VMEM((6, depth + 2, grown, rows_x), jnp.float32),
            pltpu.VMEM((STEPS, depth + 2, grown, rows_x), jnp.float32),
        ],
        compiler_params=params(24),
        cost_estimate=cost(20_000_000, 6_000_000),
        name="planes",
    )(owner, cells, *parts, *states, *small_a, *small_b)


def spot(cell, start, rows_y, rows_x):
    local = cell - start
    lifted = local + rows_y * rows_x
    z = lax.div(lifted, rows_y * rows_x) - 1
    y = lax.div(lax.rem(lifted, rows_y * rows_x), rows_x)
    return lifted, z, y, lax.rem(lifted, rows_x)


def main_kernel(step, *refs):
    first, last = step == STEPS - 1, step == 0
    refs = list(refs)
    sensors, misfit = refs.pop(0), refs.pop(0)
    if not first:
        cells, steps, inside, grad_in = (refs.pop(0) for _ in range(4))
        lam_edges = refs.pop(0)
    lam, coef, gain, scale = (refs.pop(0) for _ in range(4))
    if last:
        planes_out = refs.pop(0)
    part, part_edges = refs.pop(0), refs.pop(0)
    if not first:
        grad = refs.pop(0)
    v, mu = refs.pop(0), refs.pop(0)
    if last:
        ghost, total = refs
    elif not first:
        total = grad
    own, depth, rows_y, rows_x = mu.shape
    plane = rows_y * rows_x
    start = lax.axis_index("space") * (depth * plane)
    lanes = lax.broadcasted_iota(jnp.int32, (1, rows_x), 1)

    for k in range(own):
        for z in range(depth):
            if first or 0 < z < depth - 1:
                mu[k, z] = lam[k, z]
            else:
                mu[k, z] = lam_edges[min(z, 1), k]

    def take(source, z, y, x, r):
        row = source(z, y)
        value = jnp.sum(jnp.where(lanes == x, row, 0.0), axis=-1, keepdims=True)
        slots = lax.broadcasted_iota(jnp.int32, (own, total.shape[1]), 1)
        total[...] += jnp.where(slots == r, value, 0.0)

    def collect(wanted, own_rows, ghost_rows):
        def visit(i, carry):
            r = inside[i]
            _, z, y, x = spot(cells[r], start, rows_y, rows_x)
            fits = steps[r] == wanted
            mine = (z >= 0) & (z < depth)

            @pl.when(fits & mine)
            def _():
                take(own_rows, z, y, x, r)

            if ghost_rows is not None:

                @pl.when(fits & jnp.logical_not(mine))
                def _():
                    take(ghost_rows, jnp.where(z < 0, 0, 1), y, x, r)

            return carry

        lax.fori_loop(0, inside[inside.shape[0] - 1], visit, 0)

    if not first:
        total[...] = grad_in[...]
        collect(step + 1, lambda z, y: mu[:, z, pl.ds(y, 1), :].reshape(own, rows_x), None)

    for k in range(own):
        lifted, z, y, x = spot(sensors[k], start, rows_y, rows_x)

        @pl.when((lifted >= plane) & (lifted < (depth + 1) * plane))
        def _(k=k, z=z, y=y, x=x):
            mu[k, z, pl.ds(y, 1), :] += jnp.where(lanes == x, misfit[k, step], 0.0)

    blank = jnp.zeros((PAD, rows_x), jnp.float32)
    void = jnp.zeros((rows_y + 2 * PAD, rows_x), jnp.float32)
    for k in range(own):
        v[k, 0] = void
        v[k, depth + 1] = void
        for z in range(depth):
            v[k, z + 1, pl.ds(0, PAD)] = blank
            v[k, z + 1, pl.ds(PAD + rows_y, PAD)] = blank
            v[k, z + 1, pl.ds(PAD, rows_y)] = scale[0, z] * mu[k, z]

    def layer(z, carry):
        for tile in range(rows_y // TILE):
            at = pl.ds(tile * TILE, TILE)
            c = [coef[j, z, at] for j in range(PLANES)]
            keep = gain[0, z, at]
            for k in range(own):
                spread = stencil(
                    c, lambda dz, dy: v[k, z + 1 + dz, pl.ds(PAD + tile * TILE + dy, TILE)]
                )
                part[k, z, at] = mu[k, z, at] * keep + spread
        return carry

    lax.fori_loop(0, depth, layer, 0)
    for k in range(own):
        part_edges[0, k] = part[k, 0]
        part_edges[1, k] = part[k, depth - 1]

    if last:
        def field(k, carry):
            for side in range(2):
                z = 1 + side * (depth - 1)
                for tile in range(rows_y // TILE):
                    base = PAD + tile * TILE
                    here = v[k, z, pl.ds(base, TILE)]
                    down, up = pl.ds(base - 1, TILE), pl.ds(base + 1, TILE)
                    mid = pl.ds(base, TILE)
                    value = planes_out[side, 0, mid] * here
                    value += planes_out[side, 1, down] * v[k, z, down]
                    value += planes_out[side, 2, up] * v[k, z, up]
                    value += planes_out[side, 3, mid] * pltpu.roll(here, 1, axis=1)
                    value += planes_out[side, 4, mid] * pltpu.roll(here, rows_x - 1, axis=1)
                    ghost[side, k, pl.ds(tile * TILE, TILE)] = value
            return carry

        lax.fori_loop(0, own, field, 0)
        collect(
            0,
            lambda z, y: part[:, z, pl.ds(y, 1), :].reshape(own, rows_x),
            lambda z, y: ghost[z, :, pl.ds(y, 1), :].reshape(own, rows_x),
        )
        for i in range(grad.shape[0]):
            grad[i] = total[...]


def main(step, sensors, misfit, lam, lam_edges, planes_all, release, copies):
    first, last = step == STEPS - 1, step == 0
    coef, edge, gain, scale = planes_all
    own, depth, rows_y, rows_x = lam.shape
    grown = rows_y + 2 * PAD
    one = pl.BlockSpec((1, depth, rows_y, rows_x), lambda i: (step, 0, 0, 0))

    def whole(x):
        return pl.BlockSpec(x.shape, lambda i: (0,) * len(x.shape))

    args, specs = [sensors, misfit], [SMEM, SMEM]
    if not first:
        cells, steps, inside, grad_in = release
        args += [cells, steps, inside, grad_in, lam_edges]
        specs += [SMEM, SMEM, SMEM, whole(grad_in), whole(lam_edges)]
    args += [lam, coef, gain, scale]
    specs += [whole(lam), whole(coef), one, one]
    outs = [f32(own, depth, rows_y, rows_x), f32(2, own, rows_y, rows_x)]
    scratch = [
        pltpu.VMEM((own, depth + 2, grown, rows_x), jnp.float32),
        pltpu.VMEM((own, depth, rows_y, rows_x), jnp.float32),
    ]
    if last:
        args.append(edge)
        specs.append(whole(edge))
        outs.append(f32(copies, *grad_in.shape))
        scratch.append(pltpu.VMEM((2, own, rows_y, rows_x), jnp.float32))
        scratch.append(pltpu.VMEM(grad_in.shape, jnp.float32))
    elif not first:
        outs.append(f32(*grad_in.shape))
    return pl.pallas_call(
        functools.partial(main_kernel, step),
        grid=(1,),
        in_specs=specs,
        out_specs=[whole(o) for o in outs],
        out_shape=outs,
        scratch_shapes=scratch,
        compiler_params=params(40),
        cost_estimate=cost(40_000_000, 6_000_000),
        name=f"step{step}",
    )(*args)


def rim_kernel(step, *refs):
    first, last = step == STEPS - 1, step == 0
    refs = list(refs)
    sensors, misfit = refs.pop(0), refs.pop(0)
    part_edges, got_a, got_b, edge = (refs.pop(0) for _ in range(4))
    if first:
        rim = refs.pop(0)
    if last:
        grads, _, out, grad, vh, lam, sems = refs
    else:
        scale, lam, send_a, send_b, vh, w = refs
    own, rows_y, rows_x = got_a.shape
    depth = scale.shape[1] if not last else out.shape[1]
    plane = rows_y * rows_x
    start = lax.axis_index("space") * (depth * plane)
    lanes = lax.broadcasted_iota(jnp.int32, (1, rows_x), 1)
    inner = pl.ds(PAD, rows_y)
    side_a = 1 - parity()
    side_b = parity()

    blank = jnp.zeros((PAD, rows_x), jnp.float32)
    for k in range(own):
        for side in range(2):
            vh[side, k, pl.ds(0, PAD)] = blank
            vh[side, k, pl.ds(PAD + rows_y, PAD)] = blank
        vh[side_a, k, inner] = got_a[k]
        vh[side_b, k, inner] = got_b[k]
    if first:
        for k in range(own):
            lifted, z, y, x = spot(sensors[k], start, rows_y, rows_x)
            below = (lifted >= 0) & (lifted < plane)
            above = (lifted >= (depth + 1) * plane) & (lifted < (depth + 2) * plane)

            @pl.when(below | above)
            def _(k=k, above=above, y=y, x=x):
                side = jnp.where(above, 1, 0)
                vh[side, k, pl.ds(PAD + y, 1), :] += jnp.where(lanes == x, misfit[k, step], 0.0)

        for side in range(2):
            for k in range(own):
                vh[side, k, inner] = vh[side, k, inner] * rim[side]

    for side in range(2):
        for tile in range(rows_y // TILE):
            at = pl.ds(tile * TILE, TILE)
            base = PAD + tile * TILE
            c = [edge[side, j, pl.ds(base, TILE)] for j in range(5)]
            if not last:
                z = side * (depth - 1)
                gain = scale[0, z, at]
            for k in range(own):
                here = vh[side, k, pl.ds(base, TILE)]
                value = part_edges[side, k, at] + c[0] * here
                value += c[1] * vh[side, k, pl.ds(base + 1, TILE)]
                value += c[2] * vh[side, k, pl.ds(base - 1, TILE)]
                value += pltpu.roll(c[3] * here, rows_x - 1, axis=1)
                value += pltpu.roll(c[4] * here, 1, axis=1)
                lam[side, k, at] = value
                if not last:
                    w[side, k, at] = gain * value
    if last:
        copies = [
            pltpu.make_async_copy(lam.at[side], out.at[:, side * (depth - 1)], sems.at[side])
            for side in range(2)
        ]
        for c in copies:
            c.start()
        total = grads[0]
        for i in range(1, grads.shape[0]):
            total += grads[i]
        grad[...] = total
        for c in copies:
            c.wait()
        return
    for k in range(own):
        lifted, z, y, x = spot(sensors[k], start, rows_y, rows_x)
        here = (lifted >= plane) & (lifted < (depth + 1) * plane)

        @pl.when(here & ((z == 0) | (z == depth - 1)))
        def _(k=k, z=z, y=y, x=x):
            side = jnp.where(z == 0, 0, 1)
            add = jnp.where(lanes == x, misfit[k, step - 1], 0.0)
            w[side, k, pl.ds(y, 1), :] += add * scale[0, z, pl.ds(y, 1), :]

    for k in range(own):
        send_a[k] = w[side_a, k]
        send_b[k] = w[side_b, k]


def rim_step(step, sensors, misfit, part, part_edges, got_a, got_b, planes_all, rim, grads):
    first, last = step == STEPS - 1, step == 0
    _, edge, _, scale = planes_all
    own, rows_y, rows_x = got_a.shape
    depth = part.shape[1]
    grown = rows_y + 2 * PAD

    def whole(x):
        return pl.BlockSpec(x.shape, lambda i: (0,) * len(x.shape))

    args = [sensors, misfit, part_edges, got_a, got_b, edge]
    specs = [SMEM, SMEM] + [whole(x) for x in args[2:]]
    if first:
        args.append(rim)
        specs.append(whole(rim))
    field = f32(own, rows_y, rows_x)
    halo = pltpu.VMEM((2, own, grown, rows_x), jnp.float32)
    both = pltpu.VMEM((2, own, rows_y, rows_x), jnp.float32)
    aliases = {}
    if last:
        aliases = {len(args) + 1: 0}
        args += [grads, part]
        specs += [whole(grads), ANY]
        outs = [f32(*part.shape), f32(*grads.shape[1:])]
        out_specs = [ANY, whole(outs[1])]
        scratch = [halo, both, pltpu.SemaphoreType.DMA((2,))]
    else:
        args.append(scale)
        specs.append(pl.BlockSpec((1, depth, rows_y, rows_x), lambda i: (step - 1, 0, 0, 0)))
        outs = [f32(2, own, rows_y, rows_x), field, field]
        out_specs = [whole(o) for o in outs]
        scratch = [halo, both]
    return pl.pallas_call(
        functools.partial(rim_kernel, step),
        grid=(1,),
        in_specs=specs,
        out_specs=out_specs,
        out_shape=outs,
        scratch_shapes=scratch,
        input_output_aliases=aliases,
        compiler_params=params(24),
        cost_estimate=cost(4_000_000, 3_000_000),
        name=f"rim{step}",
    )(*args)


def turned(array, axis):
    count = lax.axis_size(axis)
    return [array] + [
        lax.ppermute(array, axis, [(i, (i + k) % count) for i in range(count)])
        for k in range(1, count)
    ]


def body(
    adjoint_end,
    checkpoints,
    dispersion,
    owner_steps,
    sensor_cells,
    misfit,
    release_cells,
    release_steps,
):
    own, depth, rows_y, rows_x = adjoint_end.shape
    slabs = lax.axis_size("space")
    pairs_a = [(i, i ^ 1) for i in range(slabs)]
    pairs_b = [(i, ((i + 1) ^ 1) - 1) for i in range(1, slabs - 1)]

    def swap(a, b):
        return lax.ppermute(a, "space", pairs_a), lax.ppermute(b, "space", pairs_b)

    send_a, send_b, small_a, small_b, states = pack(
        owner_steps, adjoint_end, checkpoints, dispersion
    )
    small_a, small_b = swap(small_a, small_b)
    got_a, got_b = swap(send_a, send_b)
    parts = turned(dispersion, "sens")
    states = turned(states, "sens")
    small_a, small_b = turned(small_a, "sens"), turned(small_b, "sens")
    coef, edge, gain, scale, rim, inside = planes(
        owner_steps, release_cells, parts, states, small_a, small_b, checkpoints.shape[0]
    )
    planes_all = (coef, edge, gain, scale)
    part, part_edges = main(
        2, sensor_cells, misfit, adjoint_end, None, planes_all, None, slabs
    )
    edges, send_a, send_b = rim_step(
        2, sensor_cells, misfit, part, part_edges, got_a, got_b, planes_all, rim, None
    )
    grad = jnp.zeros((own, release_cells.shape[0]), jnp.float32)
    for step in (1, 0):
        got_a, got_b = swap(send_a, send_b)
        release = (release_cells, release_steps, inside, grad)
        part, part_edges, grad = main(
            step, sensor_cells, misfit, part, edges, planes_all, release, slabs
        )
        if step == 0:
            grad = lax.all_to_all(grad, "space", 0, 0, tiled=True)
        edges, *rest = rim_step(
            step, sensor_cells, misfit, part, part_edges, got_a, got_b, planes_all, rim, grad
        )
        if step:
            send_a, send_b = rest
    return edges, rest[0]


def solution(mesh):
    in_specs = (
        P("sens", "space", None, None),
        P("sens", "space", None, None),
        P(None, "space", "sens", None),
        P(),
        P("sens"),
        P("sens", None),
        P(),
        P(),
    )
    out_specs = (P("sens", "space", None, None), P("sens", None))
    return jax.shard_map(body, mesh=mesh, in_specs=in_specs, out_specs=out_specs, check_vma=False)
```

time: 250 us -> 71.5 us (0.29)
  blocking collectives: 80.2 us -> 15.4 us
  local copies, waits for them, and re-layouts: 49.8 us -> 7 us
  other arithmetic: 32.7 us -> 0 us
  waiting for transfers between devices: 41.6 us -> 10.5 us
  between operations: 23 us -> 0.79 us
  Pallas kernels: 0 us -> 20.4 us
  starting transfers between devices: 21.6 us -> 17.2 us
    psum x1 -> x0, blocking collectives: 77.5 us -> none  [body(): release_grad = lax.psum(partial_grad, 'space')]
    add x3 -> x0, local copies, waits for them, and re-layouts: 26 us -> none  [body(): lam = mixed + applied[1:] + retard_slope(conc) * applied[0] * mixed]
    pallas_call x0 -> x8, Pallas kernels: none -> 20.4 us  [the longest x3 10.4 us: main(): pl.pallas_call(functools.partial(main_kernel, step), grid=(1,), in_specs=...]
    gather x3 -> x0, local copies, waits for them, and re-layouts: 20.4 us -> none  [body(): values = jnp.take(lam.reshape(own_sensors, cells), release_index, axis=1)]
    psum x1 -> x0, waiting for transfers between devices: 17.7 us -> none  [broadcast(): return lax.psum(jnp.where(mine, array, jnp.zeros_like(array)), axis)]
    add x5 -> x0, other arithmetic: 15.6 us -> none  [the longest x3 15 us: apply_op(): total = total + 0.5 * sign * flux]
    all_to_all x0 -> x1, blocking collectives: none -> 15.4 us  [body(): grad = lax.all_to_all(grad, 'space', 0, 0, tiled=True)]
    ppermute x8 -> x12, waiting for transfers between devices: 23.9 us -> 10.5 us  [the longest x4 8.92 us: swap(): lax.ppermute(a, 'space', pairs_a)]
  transfers between devices with their start and end apart: 9 -> 12, of which waited for: 5 -> 4; matrix products, arithmetic and copies ran while one was open for 15% -> 1% of each run, Pallas kernels for 0% -> 22%
where the time goes in v1:
time: 71.5 us; the launch traced here: 71.3 us
  Pallas kernels  20.4 us (29%)
  starting transfers between devices  17.2 us (24%)
  blocking collectives  15.4 us (22%)
  waiting for transfers between devices  10.5 us (15%)
  local copies, waits for them, and re-layouts  7 us (10%)
  between operations  0.79 us (1%)
    all_to_all x1, blocking collectives, body(): grad = lax.all_to_all(grad, 'space', 0, 0, tiled=True)  15.4 us
    ppermute x4, starting transfers between devices, swap(): lax.ppermute(a, 'space', pairs_a)  13.3 us
    pallas_call x3, Pallas kernels, main(): pl.pallas_call(functools.partial(main_kernel, step), grid=(1,), in_specs=...  10.4 us
    ppermute x4, waiting for transfers between devices, swap(): lax.ppermute(a, 'space', pairs_a)  8.92 us
    unnamed x23, local copies, waits for them, and re-layouts  7 us
    pallas_call x3, Pallas kernels, rim_step(): pl.pallas_call(functools.partial(rim_kernel, step), grid=(1,), in_specs=s...  4.83 us
    pallas_call x1, Pallas kernels, planes(): pl.pallas_call(functools.partial(planes_kernel, count, slot_count), in_sp...  3.8 us
    ppermute x4, starting transfers between devices, swap(): lax.ppermute(b, 'space', pairs_b)  2.65 us
  transfers between devices with their start and end apart: 12, of which 4 were waited for; matrix products, arithmetic and copies ran while one was open for 1% of the time, Pallas kernels for 22%

profile of v1, /device:TPU:0, one launch (start us, length us, event | category | flops | bytes accessed | tf_op | source)
XLA Modules:
  0.0 71.3 jit_solution(1257674949841800413)
XLA Ops:
  0.6 0.5 collective-permute-start
  1.1 1.2 %copy-done = f32[8,4,64,128]{3,2,1,0:T(8,128)S(1)} copy-done((f32[8,4,64,128]{3,2,1,0:T(8,128)S(1)}, f32[8,4,64,128]{3,2,1,0:T(8,128)}, u32[]{:S(2)}) %copy-start) | copy-done | bytes 1048600
  2.4 1.0 %copy-done.2 = f32[6,4,32,128]{3,2,1,0:T(8,128)S(1)} copy-done((f32[6,4,32,128]{3,2,1,0:T(8,128)S(1)}, f32[6,4,32,128]{3,2,1,0:T(8,128)}, u32[]{:S(2)}) %copy-start.2) | copy-done | bytes 393240
  3.4 1.0 %copy-done.4 = f32[4,4,64,128]{3,2,1,0:T(8,128)S(1)} copy-done((f32[4,4,64,128]{3,2,1,0:T(8,128)S(1)}, f32[4,4,64,128]{3,2,1,0:T(8,128)}, u32[]{:S(2)}) %copy-start.4) | copy-done | bytes 524312
  4.4 0.7 copy-done.8
  5.1 1.4 %pack.1 = (f32[8,64,128]{2,1,0:T(8,128)S(1)}, f32[8,64,128]{2,1,0:T(8,128)S(1)}, f32[224,128]{1,0:T(8,128)S(1)}, f32[224,128]{1,0:T(8,128)S(1)}, f32[2,4,64,128]{3,2,1,0:T(8,128)S(1)}) custom-call(s32[3]{0:T(128)S(1)} %copy-done.8, f32[8,4,64,128]{3,2,1,0:T(8,128)S(1)} %copy-done, f32[4,4,64,128]{3,2,1,0:T(8,128)S(1)} %copy-done.4, ...), custom_call_target="tpu_custom_call" | custom-call | tf_op jit(solution)/shard_map/pack/pallas_call | solution.py:79
  6.5 2.6 %collective-permute-start.2 = (f32[224,128]{1,0:T(8,128)S(1)}, f32[224,128]{1,0:T(8,128)S(1)}, u32[]{:S(2)}, u32[]{:S(2)}) collective-permute-start(f32[224,128]{1,0:T(8,128)S(1)} %get-tuple-element.28), channel_id=1, source_target_pairs={{0,2},{2,0},{4,6},{6,4},{8,10},{10,8},{12,14},{14,12},{16,18},{18,... | collective-permute-start | bytes 344072 | tf_op jit(solution)/shard_map/ppermute | solution.py:605
  9.0 0.7 collective-permute-start.4
  9.7 0.3 collective-permute-start.1
  10.0 4.1 %collective-permute-start.6 = (f32[8,64,128]{2,1,0:T(8,128)S(1)}, f32[8,64,128]{2,1,0:T(8,128)S(1)}, u32[]{:S(2)}, u32[]{:S(2)}) collective-permute-start(f32[8,64,128]{2,1,0:T(8,128)S(1)} %get-tuple-element.35), channel_id=1, source_target_pairs={{0,2},{2,0},{4,6},{6,4},{8,10},{10,8},{12,14},{14,12},{16,18},{18,... | collective-permute-start | bytes 786440 | tf_op jit(solution)/shard_map/ppermute | solution.py:605
  14.1 0.7 collective-permute-start.7
  14.8 0.2 collective-permute-start.3
  15.0 1.2 %collective-permute-done.3.refs_7_ = f32[224,128]{1,0:T(8,128)S(1)} collective-permute-done((f32[224,128]{1,0:T(8,128)S(1)}, f32[224,128]{1,0:T(8,128)S(1)}, u32[]{:S(2)}, u32[]{:S(2)}) %collective-permute-start.3) | collective-permute-done | bytes 114720 | tf_op jit(solution)/shard_map/ppermute | solution.py:584
  16.3 0.8 %copy.16.refs_1_ = f32[8,3]{1,0:T(8,128)S(1)} copy(f32[8,3]{0,1:T(4,128)} %param.13) | data formatting | bytes 192 | tf_op args[5]
  17.1 0.4 collective-permute-done.5.refs_9_
  17.5 1.0 %copy-done.3 = f32[6,4,32,128]{3,2,1,0:T(8,128)S(1)} copy-done((f32[6,4,32,128]{3,2,1,0:T(8,128)S(1)}, f32[6,4,32,128]{3,2,1,0:T(8,128)}, u32[]{:S(2)}) %copy-start.3) | copy-done | bytes 393240
  18.5 0.7 copy-done.6
  19.1 0.7 copy-done.9
  19.8 3.8 %planes.1 = (f32[19,4,64,128]{3,2,1,0:T(8,128)S(1)}, f32[2,5,80,128]{3,2,1,0:T(8,128)S(1)}, f32[3,4,64,128]{3,2,1,0:T(8,128)S(1)}, f32[3,4,64,128]{3,2,1,0:T(8,1...) custom-call(s32[3]{0:T(128)S(1)} %copy-done.9, s32[128]{0:T(128)S(1)} %copy-done.6, f32[6,4,32,128]{3,2,1,0:T(8,128)S(1)} %copy-done.3, ...), custom_call_target="tpu_custom_call" | custom-call | flops 20000000 | bytes 6000000 | tf_op jit(solution)/shard_map/planes/pallas_call | solution.py:251
  23.6 2.6 %step2.1 = (f32[8,4,64,128]{3,2,1,0:T(8,128)S(1)}, f32[2,8,64,128]{3,2,1,0:T(8,128)S(1)}) custom-call(s32[8]{0:T(128)S(1)} %copy-done.5, f32[8,3]{1,0:T(8,128)S(1)} %copy.16.refs_1_, f32[8,4,64,128]{3,2,1,0:T(8,128)S(1)} %copy-done.1, f32[19,4,64,128]{3,2,1,0:T(8,128)S(1)} %get-tuple-element.31.refs_3_.refs_8_, ...), custom_call_target="tpu_custom_call" | custom-call | flops 40000000 | bytes 6000000 | tf_op jit(solution)/shard_map/step2/pallas_call | solution.py:433
  26.2 1.1 %collective-permute-done.6.refs_3_ = f32[8,64,128]{2,1,0:T(8,128)S(1)} collective-permute-done((f32[8,64,128]{2,1,0:T(8,128)S(1)}, f32[8,64,128]{2,1,0:T(8,128)S(1)}, u32[]{:S(2)}, u32[]{:S(2)}) %collective-permute-start.6) | collective-permute-done | bytes 262176 | tf_op jit(solution)/shard_map/ppermute | solution.py:605
  27.3 1.3 %rim2.1 = (f32[2,8,64,128]{3,2,1,0:T(8,128)S(1)}, f32[8,64,128]{2,1,0:T(8,128)S(1)}, f32[8,64,128]{2,1,0:T(8,128)S(1)}) custom-call(s32[8]{0:T(128)S(1)} %copy-done.5, f32[8,3]{1,0:T(8,128)S(1)} %copy.16.refs_1_, f32[2,8,64,128]{3,2,1,0:T(8,128)S(1)} %get-tuple-element.34.refs_2_, f32[8,64,128]{2,1,0:T(8,128)S(1)} %collective-permute-done.6.refs_3_, ...), custom_call_target="tpu_custom_call" | custom-call | flops 4000000 | bytes 3000000 | tf_op jit(solution)/shard_map/rim2/pallas_call | solution.py:567
  28.6 3.2 %collective-permute-start.8 = (f32[8,64,128]{2,1,0:T(8,128)S(1)}, f32[8,64,128]{2,1,0:T(8,128)S(1)}, u32[]{:S(2)}, u32[]{:S(2)}) collective-permute-start(f32[8,64,128]{2,1,0:T(8,128)S(1)} %get-tuple-element.43), channel_id=1, source_target_pairs={{0,2},{2,0},{4,6},{6,4},{8,10},{10,8},{12,14},{14,12},{16,18},{18,... | collective-permute-start | bytes 786440 | tf_op jit(solution)/shard_map/ppermute | solution.py:605
  31.8 0.7 collective-permute-start.9
  32.5 3.0 %step1.1 = (f32[8,4,64,128]{3,2,1,0:T(8,128)S(1)}, f32[2,8,64,128]{3,2,1,0:T(8,128)S(1)}, f32[8,128]{1,0:T(8,128)S(1)}) custom-call(s32[8]{0:T(128)S(1)} %copy-done.5, f32[8,3]{1,0:T(8,128)S(1)} %copy.16.refs_1_, s32[128]{0:T(128)S(1)} %copy-done.7, s32[128]{0:T(128)S(1)} %copy-done.10, s32[129]{0:T(256)S(1)} %get-tuple-element.30.refs_4_, ...), custom_call_target="tpu_custom_call" | custom-call | flops 40000000 | bytes 6000000 | tf_op jit(solution)/shard_map/step1/pallas_call | solution.py:433
  35.5 7.8 %collective-permute-done.8.refs_3_ = f32[8,64,128]{2,1,0:T(8,128)S(1)} collective-permute-done((f32[8,64,128]{2,1,0:T(8,128)S(1)}, f32[8,64,128]{2,1,0:T(8,128)S(1)}, u32[]{:S(2)}, u32[]{:S(2)}) %collective-permute-start.8) | collective-permute-done | bytes 262176 | tf_op jit(solution)/shard_map/ppermute | solution.py:605
  43.3 1.2 %rim1.1 = (f32[2,8,64,128]{3,2,1,0:T(8,128)S(1)}, f32[8,64,128]{2,1,0:T(8,128)S(1)}, f32[8,64,128]{2,1,0:T(8,128)S(1)}) custom-call(s32[8]{0:T(128)S(1)} %copy-done.5, f32[8,3]{1,0:T(8,128)S(1)} %copy.16.refs_1_, f32[2,8,64,128]{3,2,1,0:T(8,128)S(1)} %get-tuple-element.42.refs_2_, f32[8,64,128]{2,1,0:T(8,128)S(1)} %collective-permute-done.8.refs_3_, ...), custom_call_target="tpu_custom_call" | custom-call | flops 4000000 | bytes 3000000 | tf_op jit(solution)/shard_map/rim1/pallas_call | solution.py:567
  44.5 3.5 %collective-permute-start.10 = (f32[8,64,128]{2,1,0:T(8,128)S(1)}, f32[8,64,128]{2,1,0:T(8,128)S(1)}, u32[]{:S(2)}, u32[]{:S(2)}) collective-permute-start(f32[8,64,128]{2,1,0:T(8,128)S(1)} %get-tuple-element.48), channel_id=1, source_target_pairs={{0,2},{2,0},{4,6},{6,4},{8,10},{10,8},{12,14},{14,12},{16,18},{18,... | collective-permute-start | bytes 786440 | tf_op jit(solution)/shard_map/ppermute | solution.py:605
  48.0 0.7 collective-permute-start.11
  48.6 4.8 %step0.1 = (f32[8,4,64,128]{3,2,1,0:T(8,128)}, f32[2,8,64,128]{3,2,1,0:T(8,128)S(1)}, f32[16,8,128]{2,1,0:T(8,128)S(1)}) custom-call(s32[8]{0:T(128)S(1)} %copy-done.5, f32[8,3]{1,0:T(8,128)S(1)} %copy.16.refs_1_, s32[128]{0:T(128)S(1)} %copy-done.7, s32[128]{0:T(128)S(1)} %copy-done.10, s32[129]{0:T(256)S(1)} %get-tuple-element.30.refs_4_, ...), custom_call_target="tpu_custom_call" | custom-call | flops 40000000 | bytes 6000000 | tf_op jit(solution)/shard_map/step0/pallas_call | solution.py:433
  53.5 15.4 %all_to_all.5.refs_6_ = f32[16,8,128]{2,1,0:T(8,128)S(1)} all-to-all(f32[16,8,128]{2,1,0:T(8,128)S(1)} %get-tuple-element.50), channel_id=1, replica_groups=mesh['space'=16,'sens'=2] {'space'}, dimensions={0} | all-to-all | bytes 131072 | tf_op jit(solution)/shard_map/all_to_all | solution.py:633
  68.9 2.4 %rim0.1 = (f32[8,4,64,128]{3,2,1,0:T(8,128)}, f32[8,128]{1,0:T(8,128)}) custom-call(s32[8]{0:T(128)S(1)} %copy-done.5, f32[8,3]{1,0:T(8,128)S(1)} %copy.16.refs_1_, f32[2,8,64,128]{3,2,1,0:T(8,128)S(1)} %get-tuple-element.47.refs_2_, f32[8,64,128]{2,1,0:T(8,128)S(1)} %collective-permute-done.10.refs_3_, ...), custom_call_target="tpu_custom_call", output_to_operand_aliasing={{0}: (7, {})} | custom-call | flops 4000000 | bytes 3000000 | tf_op jit(solution)/shard_map/rim0/pallas_call | solution.py:567
  (25 shorter events, 0.2 us)
Async XLA Ops:
  0.6 16.8 %collective-permute-start = (f32[6,4,32,128]{3,2,1,0:T(8,128)}, f32[6,4,32,128]{3,2,1,0:T(8,128)S(1)}, u32[]{:S(2)}, u32[]{:S(2)}) collective-permute-start(f32[6,4,32,128]{3,2,1,0:T(8,128)} %refs_2_.4), channel_id=1, source_target_pairs={{0,1},{1,0},{2,3},{3,2},{4,5},{5,4},{6,7},{7,6},{8,9},{9,8},{10,11... | collective-permute-start | bytes 1179656 | tf_op jit(solution)/shard_map/ppermute | solution.py:584
  1.1 1.2 %copy-start = (f32[8,4,64,128]{3,2,1,0:T(8,128)S(1)}, f32[8,4,64,128]{3,2,1,0:T(8,128)}, u32[]{:S(2)}) copy-start(f32[8,4,64,128]{3,2,1,0:T(8,128)} %refs_2_.5) | copy-start | bytes 3145732
  2.4 1.0 %copy-start.2 = (f32[6,4,32,128]{3,2,1,0:T(8,128)S(1)}, f32[6,4,32,128]{3,2,1,0:T(8,128)}, u32[]{:S(2)}) copy-start(f32[6,4,32,128]{3,2,1,0:T(8,128)} %refs_2_.4) | copy-start | bytes 1179652
  3.4 1.0 %copy-start.4 = (f32[4,4,64,128]{3,2,1,0:T(8,128)S(1)}, f32[4,4,64,128]{3,2,1,0:T(8,128)}, u32[]{:S(2)}) copy-start(f32[4,4,64,128]{3,2,1,0:T(8,128)} %ckpt.1) | copy-start | bytes 1572868
  4.4 0.7 copy-start.8
  5.1 18.5 %copy-start.1 = (f32[8,4,64,128]{3,2,1,0:T(8,128)S(1)}, f32[8,4,64,128]{3,2,1,0:T(8,128)}, u32[]{:S(2)}) copy-start(f32[8,4,64,128]{3,2,1,0:T(8,128)} %refs_2_.5) | copy-start | bytes 3145732
  5.1 18.5 %copy-start.5 = (s32[8]{0:T(128)S(1)}, s32[8]{0:T(128)}, u32[]{:S(2)}) copy-start(s32[8]{0:T(128)} %refs_0_.13) | copy-start | bytes 100
  6.5 7.6 %collective-permute-start.2 = (f32[224,128]{1,0:T(8,128)S(1)}, f32[224,128]{1,0:T(8,128)S(1)}, u32[]{:S(2)}, u32[]{:S(2)}) collective-permute-start(f32[224,128]{1,0:T(8,128)S(1)} %get-tuple-element.28), channel_id=1, source_target_pairs={{0,2},{2,0},{4,6},{6,4},{8,10},{10,8},{12,14},{14,12},{16,18},{18,... | collective-permute-start | bytes 344072 | tf_op jit(solution)/shard_map/ppermute | solution.py:605
  9.0 5.7 %collective-permute-start.4 = (f32[224,128]{1,0:T(8,128)S(1)}, f32[224,128]{1,0:T(8,128)S(1)}, u32[]{:S(2)}, u32[]{:S(2)}) collective-permute-start(f32[224,128]{1,0:T(8,128)S(1)} %get-tuple-element.29), channel_id=1, source_target_pairs={{2,4},{4,2},{6,8},{8,6},{10,12},{12,10},{14,16},{16,14},{18,20},{2... | collective-permute-start | bytes 344072 | tf_op jit(solution)/shard_map/ppermute | solution.py:605
  9.7 7.8 %collective-permute-start.1 = (f32[2,4,64,128]{3,2,1,0:T(8,128)S(1)}, f32[2,4,64,128]{3,2,1,0:T(8,128)S(1)}, u32[]{:S(2)}, u32[]{:S(2)}) collective-permute-start(f32[2,4,64,128]{3,2,1,0:T(8,128)S(1)} %get-tuple-element.27.refs_4_), channel_id=1, source_target_pairs={{0,1},{1,0},{2,3},{3,2},{4,5},{5,4},{6,7},{7,6},{8,9},{9,8},{10,11... | collective-permute-start | bytes 786440 | tf_op jit(solution)/shard_map/ppermute | solution.py:584
  10.0 17.4 %collective-permute-start.6 = (f32[8,64,128]{2,1,0:T(8,128)S(1)}, f32[8,64,128]{2,1,0:T(8,128)S(1)}, u32[]{:S(2)}, u32[]{:S(2)}) collective-permute-start(f32[8,64,128]{2,1,0:T(8,128)S(1)} %get-tuple-element.35), channel_id=1, source_target_pairs={{0,2},{2,0},{4,6},{6,4},{8,10},{10,8},{12,14},{14,12},{16,18},{18,... | collective-permute-start | bytes 786440 | tf_op jit(solution)/shard_map/ppermute | solution.py:605
  14.1 13.3 %collective-permute-start.7 = (f32[8,64,128]{2,1,0:T(8,128)S(1)}, f32[8,64,128]{2,1,0:T(8,128)S(1)}, u32[]{:S(2)}, u32[]{:S(2)}) collective-permute-start(f32[8,64,128]{2,1,0:T(8,128)S(1)} %get-tuple-element.36), channel_id=1, source_target_pairs={{2,4},{4,2},{6,8},{8,6},{10,12},{12,10},{14,16},{16,14},{18,20},{2... | collective-permute-start | bytes 786440 | tf_op jit(solution)/shard_map/ppermute | solution.py:605
  14.8 1.4 %collective-permute-start.3 = (f32[224,128]{1,0:T(8,128)S(1)}, f32[224,128]{1,0:T(8,128)S(1)}, u32[]{:S(2)}, u32[]{:S(2)}) collective-permute-start(f32[224,128]{1,0:T(8,128)S(1)} %collective-permute-done.2.refs_6_), channel_id=1, source_target_pairs={{0,1},{1,0},{2,3},{3,2},{4,5},{5,4},{6,7},{7,6},{8,9},{9,8},{10,11... | collective-permute-start | bytes 344072 | tf_op jit(solution)/shard_map/ppermute | solution.py:584
  16.1 1.3 %collective-permute-start.5 = (f32[224,128]{1,0:T(8,128)S(1)}, f32[224,128]{1,0:T(8,128)S(1)}, u32[]{:S(2)}, u32[]{:S(2)}) collective-permute-start(f32[224,128]{1,0:T(8,128)S(1)} %collective-permute-done.4.refs_8_), channel_id=1, source_target_pairs={{0,1},{1,0},{2,3},{3,2},{4,5},{5,4},{6,7},{7,6},{8,9},{9,8},{10,11... | collective-permute-start | bytes 344072 | tf_op jit(solution)/shard_map/ppermute | solution.py:584
  17.5 1.0 %copy-start.3 = (f32[6,4,32,128]{3,2,1,0:T(8,128)S(1)}, f32[6,4,32,128]{3,2,1,0:T(8,128)}, u32[]{:S(2)}) copy-start(f32[6,4,32,128]{3,2,1,0:T(8,128)} %refs_2_.4) | copy-start | bytes 1179652
  18.5 0.7 copy-start.6
  19.1 0.7 copy-start.9
  23.6 8.9 %copy-start.7 = (s32[128]{0:T(128)S(1)}, s32[128]{0:T(128)}, u32[]{:S(2)}) copy-start(s32[128]{0:T(128)} %refs_2_.7) | copy-start | bytes 1540
  23.6 8.9 %copy-start.10 = (s32[128]{0:T(128)S(1)}, s32[128]{0:T(128)}, u32[]{:S(2)}) copy-start(s32[128]{0:T(128)} %refs_3_.3) | copy-start | bytes 1540
  28.6 14.7 %collective-permute-start.8 = (f32[8,64,128]{2,1,0:T(8,128)S(1)}, f32[8,64,128]{2,1,0:T(8,128)S(1)}, u32[]{:S(2)}, u32[]{:S(2)}) collective-permute-start(f32[8,64,128]{2,1,0:T(8,128)S(1)} %get-tuple-element.43), channel_id=1, source_target_pairs={{0,2},{2,0},{4,6},{6,4},{8,10},{10,8},{12,14},{14,12},{16,18},{18,... | collective-permute-start | bytes 786440 | tf_op jit(solution)/shard_map/ppermute | solution.py:605
  31.8 11.5 %collective-permute-start.9 = (f32[8,64,128]{2,1,0:T(8,128)S(1)}, f32[8,64,128]{2,1,0:T(8,128)S(1)}, u32[]{:S(2)}, u32[]{:S(2)}) collective-permute-start(f32[8,64,128]{2,1,0:T(8,128)S(1)} %get-tuple-element.44), channel_id=1, source_target_pairs={{2,4},{4,2},{6,8},{8,6},{10,12},{12,10},{14,16},{16,14},{18,20},{2... | collective-permute-start | bytes 786440 | tf_op jit(solution)/shard_map/ppermute | solution.py:605
  44.5 24.4 %collective-permute-start.10 = (f32[8,64,128]{2,1,0:T(8,128)S(1)}, f32[8,64,128]{2,1,0:T(8,128)S(1)}, u32[]{:S(2)}, u32[]{:S(2)}) collective-permute-start(f32[8,64,128]{2,1,0:T(8,128)S(1)} %get-tuple-element.48), channel_id=1, source_target_pairs={{0,2},{2,0},{4,6},{6,4},{8,10},{10,8},{12,14},{14,12},{16,18},{18,... | collective-permute-start | bytes 786440 | tf_op jit(solution)/shard_map/ppermute | solution.py:605
  48.0 20.9 %collective-permute-start.11 = (f32[8,64,128]{2,1,0:T(8,128)S(1)}, f32[8,64,128]{2,1,0:T(8,128)S(1)}, u32[]{:S(2)}, u32[]{:S(2)}) collective-permute-start(f32[8,64,128]{2,1,0:T(8,128)S(1)} %get-tuple-element.49), channel_id=1, source_target_pairs={{2,4},{4,2},{6,8},{8,6},{10,12},{12,10},{14,16},{16,14},{18,20},{2... | collective-permute-start | bytes 786440 | tf_op jit(solution)/shard_map/ppermute | solution.py:605

commit v2 on v0

v2 whole, which is shorter than its diff:
```python
import functools

import jax
import jax.numpy as jnp
from jax import lax
from jax.experimental import pallas as pl
from jax.experimental.pallas import tpu as pltpu
from jax.sharding import PartitionSpec as P

STEPS = 3
DT = 0.12
PAD = 8
TILE = 8
CENTRE, ZP, ZM, YP, YM, ZPYP, ZPYM, ZMYP, ZMYM = range(9)
XP, XPZP, XPZM, XPYP, XPYM, XM, XMZP, XMZM, XMYP, XMYM = range(9, 19)
PLANES = 19
LOW = (ZM, ZMYP, ZMYM, XPZM, XMZM)
HIGH = (ZP, ZPYP, ZPYM, XPZP, XMZP)

VMEM = pl.BlockSpec(memory_space=pltpu.VMEM)
SMEM = pl.BlockSpec(memory_space=pltpu.SMEM)
ANY = pl.BlockSpec(memory_space=pl.ANY)


def f32(*shape):
    return jax.ShapeDtypeStruct(shape, jnp.float32)


def params(mib):
    return pltpu.CompilerParams(vmem_limit_bytes=mib * 1024 * 1024)


def cost(flops, moved):
    return pl.CostEstimate(flops=flops, bytes_accessed=moved, transcendentals=0)


def owned(owner_ref, slots):
    me = lax.axis_index("sens")
    o0, o1, o2 = (owner_ref[i] for i in range(3))
    own0 = lax.div(o0, slots) == me
    own1 = lax.div(o1, slots) == me
    first = jnp.where(own0, o0, jnp.where(own1, o1, o2))
    second = jnp.where(own0 & own1, o1, o2)
    return lax.rem(first, slots), lax.rem(second, slots)


def parity():
    return lax.rem(lax.axis_index("space"), 2)


def spot(cell, start, rows_y, rows_x):
    local = cell - start
    lifted = local + rows_y * rows_x
    z = lax.div(lifted, rows_y * rows_x) - 1
    y = lax.div(lax.rem(lifted, rows_y * rows_x), rows_x)
    return lifted, z, y, lax.rem(lifted, rows_x)


def pack_kernel(
    owner, sensors, misfit, adj, ckpt, disp, lam_a, lam_b, small_a, small_b, sems
):
    own, depth, rows_y, rows_x = adj.shape
    rows = disp.shape[2]
    plane = rows_y * rows_x
    start = lax.axis_index("space") * (depth * plane)
    even = parity() == 0
    z_a = jnp.where(even, depth - 1, 0)
    z_b = jnp.where(even, 0, depth - 1)
    held = owned(owner, ckpt.shape[0])
    moves = [(adj.at[:, z_a], lam_a), (adj.at[:, z_b], lam_b)]
    for z, small in ((z_a, small_a), (z_b, small_b)):
        for j in range(2):
            moves.append((ckpt.at[held[j], z], small.at[pl.ds(j * rows_y, rows_y)]))
        for j, comp in enumerate((0, 3, 4)):
            moves.append((disp.at[comp, z], small.at[pl.ds(2 * rows_y + j * rows, rows)]))
    copies = [pltpu.make_async_copy(s, d, sems.at[i]) for i, (s, d) in enumerate(moves)]
    for c in copies:
        c.start()

    lanes = lax.broadcasted_iota(jnp.int32, (1, rows_x), 1)
    for c in copies[:2]:
        c.wait()
    for k in range(own):
        lifted, z, y, x = spot(sensors[k], start, rows_y, rows_x)
        mine = (lifted >= plane) & (lifted < (depth + 1) * plane)

        for edge, lam in ((z_a, lam_a), (z_b, lam_b)):

            @pl.when(mine & (z == edge))
            def _(k=k, y=y, x=x, lam=lam):
                lam[k, pl.ds(y, 1), :] += jnp.where(lanes == x, misfit[STEPS - 1, k], 0.0)

    for c in copies[2:]:
        c.wait()


def pack(owner, sensors, misfit, adj, ckpt, disp):
    own, depth, rows_y, rows_x = adj.shape
    rows = disp.shape[2]
    small = f32(2 * rows_y + 3 * rows, rows_x)
    return pl.pallas_call(
        pack_kernel,
        in_specs=[SMEM] * 3 + [ANY] * 3,
        out_specs=[VMEM] * 4,
        out_shape=[f32(own, rows_y, rows_x)] * 2 + [small, small],
        scratch_shapes=[pltpu.SemaphoreType.DMA((12,))],
        compiler_params=params(60),
        cost_estimate=cost(1000, 1000),
        name="pack",
    )(owner, sensors, misfit, adj, ckpt, disp)


def lane_masks(shape):
    lanes = lax.broadcasted_iota(jnp.int32, shape, len(shape) - 1)
    return lanes >= 1, lanes < shape[-1] - 1


def before(value, keep):
    return jnp.where(keep, pltpu.roll(value, 1, axis=value.ndim - 1), 0.0)


def after(value, keep):
    return jnp.where(keep, pltpu.roll(value, value.shape[-1] - 1, axis=value.ndim - 1), 0.0)


def planes_at(window, keep_b, keep_a):
    def yy(dy):
        return window(1, 0, dy)

    c = [None] * PLANES
    zz, zzp, zzm = window(0, 0, 0), window(0, 1, 0), window(0, -1, 0)
    xx = window(2, 0, 0)
    c[ZP], c[ZM] = 0.5 * (zz + zzp), 0.5 * (zz + zzm)
    c[YP], c[YM] = 0.5 * (yy(0) + yy(1)), 0.5 * (yy(0) + yy(-1))
    xx_b, xx_a = before(xx, keep_b), after(xx, keep_a)
    c[XP] = jnp.where(keep_b, 0.5 * (xx_b + xx), 0.0)
    c[XM] = jnp.where(keep_a, 0.5 * (xx_a + xx), 0.0)
    c[CENTRE] = -(c[ZP] + c[ZM] + c[YP] + c[YM] + (xx + 0.5 * (xx_a + xx_b)))
    zp, zm, yp, ym = window(3, 1, 0), window(3, -1, 0), window(3, 0, 1), window(3, 0, -1)
    c[ZPYP], c[ZPYM] = 0.25 * (zp + yp), -0.25 * (zp + ym)
    c[ZMYP], c[ZMYM] = -0.25 * (zm + yp), 0.25 * (zm + ym)
    for comp, plus, minus, names in (
        (4, window(4, 1, 0), window(4, -1, 0), (XPZP, XPZM, XMZP, XMZM)),
        (5, window(5, 0, 1), window(5, 0, -1), (XPYP, XPYM, XMYP, XMYM)),
    ):
        here = window(comp, 0, 0)
        c[names[0]] = jnp.where(keep_b, 0.25 * (before(plus, keep_b) + here), 0.0)
        c[names[1]] = jnp.where(keep_b, -0.25 * (before(minus, keep_b) + here), 0.0)
        c[names[2]] = jnp.where(keep_a, -0.25 * (after(plus, keep_a) + here), 0.0)
        c[names[3]] = jnp.where(keep_a, 0.25 * (after(minus, keep_a) + here), 0.0)
    return c


def stencil(c, u):
    near = {(dz, dy): u(dz, dy) for dz in (-1, 0, 1) for dy in (-1, 0, 1)}
    here = c[CENTRE] * near[0, 0] + c[ZP] * near[1, 0] + c[ZM] * near[-1, 0]
    here += c[YP] * near[0, 1] + c[YM] * near[0, -1]
    here += c[ZPYP] * near[1, 1] + c[ZPYM] * near[1, -1]
    here += c[ZMYP] * near[-1, 1] + c[ZMYM] * near[-1, -1]
    right = c[XP] * near[0, 0] + c[XPZP] * near[1, 0] + c[XPZM] * near[-1, 0]
    right += c[XPYP] * near[0, 1] + c[XPYM] * near[0, -1]
    left = c[XM] * near[0, 0] + c[XMZP] * near[1, 0] + c[XMZM] * near[-1, 0]
    left += c[XMYP] * near[0, 1] + c[XMYM] * near[0, -1]
    width = here.shape[-1]
    return here + pltpu.roll(right, width - 1, axis=1) + pltpu.roll(left, 1, axis=1)


def scale_of(conc):
    root = jnp.sqrt(conc)
    return DT * root / (root + 0.5)


def slope_of(conc):
    root = jnp.sqrt(conc)
    return (0.25 * DT) / (root * (root + 0.5) * (root + 0.5))


def planes_kernel(count, *refs):
    owner = refs[0]
    parts, states = refs[1 : 1 + count], refs[1 + count : 1 + 2 * count]
    coef, gain, scale, ends, full, conc = refs[1 + 2 * count :]
    depth, rows_y, rows_x = coef.shape[1:]
    rows = rows_y // count
    slots = states[0].shape[0]
    me = lax.axis_index("sens")
    inner = pl.ds(PAD, rows_y)

    blank = jnp.zeros((PAD, rows_x), jnp.float32)
    void = jnp.zeros((rows_y + 2 * PAD, rows_x), jnp.float32)
    for ref in (full, conc):
        for i in range(ref.shape[0]):
            ref[i, 0] = void
            ref[i, depth + 1] = void
            for z in range(depth):
                ref[i, z + 1, pl.ds(0, PAD)] = blank
                ref[i, z + 1, pl.ds(PAD + rows_y, PAD)] = blank
    for k in range(count):
        who = lax.rem(me - k + count, count)
        span = pl.ds(pl.multiple_of(PAD + who * rows, PAD), rows)
        for comp in range(6):
            for z in range(depth):
                full[comp, z + 1, span] = parts[k][comp, z]
    for i in range(STEPS):
        turn = lax.rem(me - lax.div(owner[i], slots) + count, count)
        slot = lax.rem(owner[i], slots)
        for k in range(count):

            @pl.when(turn == k)
            def _(i=i, k=k, slot=slot):
                conc[i, pl.ds(1, depth), inner] = states[k][slot]

        for side in range(2):
            ends[i, side] = conc[i, 1 + side * (depth - 1), inner]

    keep_b, keep_a = lane_masks((TILE, rows_x))

    def layer(z, carry):
        for tile in range(rows_y // TILE):
            at = pl.ds(tile * TILE, TILE)

            def window(comp, dz, dy):
                return full[comp, z + 1 + dz, pl.ds(PAD + tile * TILE + dy, TILE)]

            c = planes_at(window, keep_b, keep_a)
            for j in range(PLANES):
                coef[j, z, at] = c[j]
            for i in range(STEPS):
                here = conc[i, z + 1, pl.ds(PAD + tile * TILE, TILE)]
                spread = stencil(
                    c, lambda dz, dy: conc[i, z + 1 + dz, pl.ds(PAD + tile * TILE + dy, TILE)]
                )
                scale[i, z, at] = scale_of(here)
                gain[i, z, at] = 1.0 + slope_of(here) * spread
        return carry

    lax.fori_loop(0, depth, layer, 0)


def planes(owner, parts, states):
    count = len(parts)
    depth, rows_y, rows_x = states[0].shape[1:]
    grown = rows_y + 2 * PAD
    return pl.pallas_call(
        functools.partial(planes_kernel, count),
        in_specs=[SMEM] + [VMEM] * (2 * count),
        out_specs=[VMEM] * 4,
        out_shape=[
            f32(PLANES, depth, rows_y, rows_x),
            f32(STEPS, depth, rows_y, rows_x),
            f32(STEPS, depth, rows_y, rows_x),
            f32(STEPS, 2, rows_y, rows_x),
        ],
        scratch_shapes=[
            pltpu.VMEM((6, depth + 2, grown, rows_x), jnp.float32),
            pltpu.VMEM((STEPS, depth + 2, grown, rows_x), jnp.float32),
        ],
        compiler_params=params(24),
        cost_estimate=cost(2_000_000_000, 60_000_000),
        name="planes",
    )(owner, *parts, *states)


def ends_kernel(count, slots, *refs):
    owner, coef, ends = refs[:3]
    small = refs[3 : 3 + count], refs[3 + count : 3 + 2 * count]
    edge, edge_raw, corr, tensor, conc = refs[3 + 2 * count :]
    depth, rows_y, rows_x = coef.shape[1:]
    rows = rows_y // count
    me = lax.axis_index("sens")
    side_a = 1 - parity()
    inner = pl.ds(PAD, rows_y)
    blank = jnp.zeros((PAD, rows_x), jnp.float32)
    for side in range(2):
        for i in range(STEPS):
            conc[side, i, pl.ds(0, PAD)] = blank
            conc[side, i, pl.ds(PAD + rows_y, PAD)] = blank
    for k in range(count):
        who = lax.rem(me - k + count, count)
        span = pl.ds(pl.multiple_of(who * rows, PAD), rows)
        for j in range(3):
            here = pl.ds(2 * rows_y + j * rows, rows)
            tensor[side_a, j, span] = small[0][k][here]
            tensor[1 - side_a, j, span] = small[1][k][here]
    holders = [lax.div(owner[i], slots) for i in range(STEPS)]
    for i in range(STEPS):
        slot = jnp.int32(0)
        for j in range(i):
            slot += jnp.where(holders[j] == holders[i], 1, 0)
        slot = jnp.minimum(slot, 1)
        turn = lax.rem(me - holders[i] + count, count)
        for k in range(count):

            @pl.when(turn == k)
            def _(i=i, k=k, slot=slot):
                span = pl.ds(pl.multiple_of(slot * rows_y, PAD), rows_y)
                conc[side_a, i, inner] = small[0][k][span]
                conc[1 - side_a, i, inner] = small[1][k][span]

    keep_b, keep_a = lane_masks((TILE, rows_x))
    ys = lax.broadcasted_iota(jnp.int32, (TILE, rows_x), 0)
    for side, z, names in ((0, 0, LOW), (1, depth - 1, HIGH)):
        sign = 2 * side - 1
        for tile in range(rows_y // TILE):
            at = pl.ds(tile * TILE, TILE)
            zz, zy, zx = (tensor[side, j, at] for j in range(3))
            e = [coef[names[j], z, at] for j in range(5)]
            e[0] += 0.5 * zz
            e[1] += (0.25 * sign) * zy
            e[2] -= (0.25 * sign) * zy
            e[3] += (0.25 * sign) * before(zx, keep_b)
            e[4] -= (0.25 * sign) * after(zx, keep_a)
            if tile == rows_y // TILE - 1:
                e[1] = jnp.where(ys < TILE - 1, e[1], 0.0)
            if tile == 0:
                e[2] = jnp.where(ys > 0, e[2], 0.0)
            near = [
                [conc[side, i, pl.ds(PAD + tile * TILE + d, TILE)] for d in (0, 1, -1)]
                for i in range(STEPS)
            ]
            for j in range(5):
                edge[side, j, at] = e[j]
                edge_raw[side, j, at] = e[j] * scale_of(near[STEPS - 1][(0, 1, 2, 0, 0)[j]])
            for i in range(STEPS):
                here, up, down = near[i]
                own = ends[i, side, at]
                spread = e[0] * here + e[1] * up + e[2] * down - 0.5 * zz * own
                spread += pltpu.roll(e[3] * here, rows_x - 1, axis=1)
                spread += pltpu.roll(e[4] * here, 1, axis=1)
                gain, scale = slope_of(own) * spread, scale_of(own)
                if i == STEPS - 1:
                    corr[i, side, at] = gain - 0.5 * zz * scale
                else:
                    corr[i, side, at] = gain / scale - 0.5 * zz


def ends_call(owner, coef, ends, small_a, small_b, slots):
    count = len(small_a)
    _, _, rows_y, rows_x = coef.shape
    return pl.pallas_call(
        functools.partial(ends_kernel, count, slots),
        in_specs=[SMEM] + [VMEM] * (2 + 2 * count),
        out_specs=[VMEM] * 3,
        out_shape=[
            f32(2, 5, rows_y, rows_x),
            f32(2, 5, rows_y, rows_x),
            f32(STEPS, 2, rows_y, rows_x),
        ],
        scratch_shapes=[
            pltpu.VMEM((2, 3, rows_y, rows_x), jnp.float32),
            pltpu.VMEM((2, STEPS, rows_y + 2 * PAD, rows_x), jnp.float32),
        ],
        compiler_params=params(16),
        cost_estimate=cost(1_000_000, 1_000_000),
        name="ends",
    )(owner, coef, ends, *small_a, *small_b)


def gather_field(first, lam, lam_a, lam_b, mu):
    own, depth = mu.shape[:2]
    for k in range(own):
        for z in range(depth):
            if first or 0 < z < depth - 1:
                mu[k, z] = lam[k, z]
    if not first:
        z_a = jnp.where(parity() == 0, depth - 1, 0)
        for k in range(own):
            mu[k, z_a] = lam_a[k]
            mu[k, depth - 1 - z_a] = lam_b[k]


def add_misfit(step, sensors, misfit, mu):
    own, depth, rows_y, rows_x = mu.shape
    plane = rows_y * rows_x
    start = lax.axis_index("space") * (depth * plane)
    lanes = lax.broadcasted_iota(jnp.int32, (1, rows_x), 1)
    for k in range(own):
        lifted, z, y, x = spot(sensors[k], start, rows_y, rows_x)

        @pl.when((lifted >= plane) & (lifted < (depth + 1) * plane))
        def _(k=k, z=z, y=y, x=x):
            mu[k, z, pl.ds(y, 1), :] += jnp.where(lanes == x, misfit[step, k], 0.0)


def scale_field(scale, step, mu, v):
    own, depth, rows_y, rows_x = mu.shape
    blank = jnp.zeros((PAD, rows_x), jnp.float32)
    void = jnp.zeros((rows_y + 2 * PAD, rows_x), jnp.float32)
    for k in range(own):
        v[k, 0] = void
        v[k, depth + 1] = void
        for z in range(depth):
            v[k, z + 1, pl.ds(0, PAD)] = blank
            v[k, z + 1, pl.ds(PAD + rows_y, PAD)] = blank
            v[k, z + 1, pl.ds(PAD, rows_y)] = scale[step, z] * mu[k, z]


def spread_field(coef, gain, step, mu, v, part, part_edges=None):
    own, depth, rows_y, rows_x = mu.shape

    def layer(z, carry):
        for tile in range(rows_y // TILE):
            at = pl.ds(tile * TILE, TILE)
            c = [coef[j, z, at] for j in range(PLANES)]
            keep = gain[step, z, at]
            for k in range(own):
                spread = stencil(
                    c, lambda dz, dy: v[k, z + 1 + dz, pl.ds(PAD + tile * TILE + dy, TILE)]
                )
                part[k, z, at] = mu[k, z, at] * keep + spread
        return carry

    lax.fori_loop(0, depth, layer, 0)
    if part_edges is not None:
        for k in range(own):
            part_edges[0, k] = part[k, 0]
            part_edges[1, k] = part[k, depth - 1]


def collect(wanted, release, shape, total, own_row, near_row=None):
    cells, steps, inside = release
    own, depth, rows_y, rows_x = shape
    start = lax.axis_index("space") * (depth * rows_y * rows_x)
    lanes = lax.broadcasted_iota(jnp.int32, (1, rows_x), 1)
    slots = lax.broadcasted_iota(jnp.int32, (own, total.shape[1]), 1)

    def take(r, x, row):
        value = jnp.sum(jnp.where(lanes == x, row, 0.0), axis=-1, keepdims=True)
        total[...] += jnp.where(slots == r, value, 0.0)

    def visit(i, carry):
        r = inside[i]
        _, z, y, x = spot(cells[r], start, rows_y, rows_x)
        fits = steps[r] == wanted
        mine = (z >= 0) & (z < depth)

        @pl.when(fits & mine)
        def _():
            take(r, x, own_row(z, y))

        if near_row is not None:

            @pl.when(fits & jnp.logical_not(mine))
            def _():
                take(r, x, near_row(jnp.where(z < 0, 0, 1), y))

        return carry

    lax.fori_loop(0, inside[inside.shape[0] - 1], visit, 0)


def list_releases(cells, shape, inside):
    own, depth, rows_y, rows_x = shape
    plane = rows_y * rows_x
    start = lax.axis_index("space") * (depth * plane)

    def note(r, found):
        local = cells[r] - start
        near = (local >= -plane) & (local < (depth + 1) * plane)

        @pl.when(near)
        def _():
            inside[found] = r

        return found + jnp.where(near, 1, 0)

    inside[inside.shape[0] - 1] = lax.fori_loop(0, cells.shape[0], note, jnp.int32(0))


def rows_of(ref, *index):
    row = ref[(slice(None), *index, slice(None))]
    return row.reshape(row.shape[0], row.shape[-1])


def first_kernel(sensors, misfit, lam, coef, gain, scale, part, part_edges, v, mu):
    gather_field(True, lam, None, None, mu)
    add_misfit(STEPS - 1, sensors, misfit, mu)
    scale_field(scale, STEPS - 1, mu, v)
    spread_field(coef, gain, STEPS - 1, mu, v, part, part_edges)


def middle_kernel(
    step, sensors, misfit, cells, steps, lam, lam_a, lam_b, coef, gain, scale, part, part_edges, grad, inside, v, mu
):
    gather_field(False, lam, lam_a, lam_b, mu)
    grad[...] = jnp.zeros_like(grad)
    list_releases(cells, mu.shape, inside)
    collect(
        step + 1, (cells, steps, inside), mu.shape, grad, lambda z, y: rows_of(mu, z, pl.ds(y, 1))
    )
    add_misfit(step, sensors, misfit, mu)
    scale_field(scale, step, mu, v)
    spread_field(coef, gain, step, mu, v, part, part_edges)


def front_kernel(
    sensors, misfit, cells, steps, inside, grad_in, lam, lam_a, lam_b, coef, edge, corr, gain, scale, grads, mu, v, total
):
    own, depth, rows_y, rows_x = mu.shape
    gather_field(False, lam, lam_a, lam_b, mu)
    total[...] = grad_in[...]
    release = (cells, steps, inside)
    collect(1, release, mu.shape, total, lambda z, y: rows_of(mu, z, pl.ds(y, 1)))
    add_misfit(0, sensors, misfit, mu)
    scale_field(scale, 0, mu, v)

    def own_row(z, y):
        at = pl.ds(y, 1)
        c = [coef[j, z, at] for j in range(PLANES)]
        spread = stencil(c, lambda dz, dy: rows_of(v, z + 1 + dz, pl.ds(PAD + y + dy, 1)))
        at_edge = (z == 0) | (z == depth - 1)
        miss = jnp.where(at_edge, corr[0, jnp.where(z == 0, 0, 1), at], 0.0)
        return rows_of(mu, z, at) * gain[0, z, at] + spread + miss * rows_of(v, z + 1, pl.ds(PAD + y, 1))

    def near_row(side, y):
        z = 1 + side * (depth - 1)
        here, down, up = (rows_of(v, z, pl.ds(PAD + y + d, 1)) for d in (0, -1, 1))
        at = pl.ds(y, 1)
        value = edge[side, 0, at] * here
        value += edge[side, 1, pl.ds(jnp.maximum(y - 1, 0), 1)] * down
        value += edge[side, 2, pl.ds(jnp.minimum(y + 1, rows_y - 1), 1)] * up
        value += edge[side, 3, at] * pltpu.roll(here, 1, axis=1)
        value += edge[side, 4, at] * pltpu.roll(here, rows_x - 1, axis=1)
        return value

    collect(0, release, mu.shape, total, own_row, near_row)
    for i in range(grads.shape[0]):
        grads[i] = total[...]


def field_call(kernel, name, args, specs, outs, scratch, flops, listed=0):
    return pl.pallas_call(
        kernel,
        in_specs=specs,
        out_specs=[VMEM] * len(outs) + [SMEM] * (listed > 0),
        out_shape=outs + [jax.ShapeDtypeStruct((listed,), jnp.int32)] * (listed > 0),
        scratch_shapes=[pltpu.VMEM(o.shape, jnp.float32) for o in scratch],
        compiler_params=params(32),
        cost_estimate=cost(flops, 4_000_000),
        name=name,
    )(*args)


def met(got, k, tile, tiles):
    here = got[k, pl.ds(tile * TILE, TILE)]
    if tile == tiles - 1:
        up = pltpu.roll(here, TILE - 1, axis=0)
    else:
        up = got[k, pl.ds(tile * TILE + 1, TILE)]
    if tile == 0:
        down = pltpu.roll(here, 1, axis=0)
    else:
        down = got[k, pl.ds(tile * TILE - 1, TILE)]
    return here, up, down


def from_met(c, here, up, down):
    width = here.shape[-1]
    value = c[0] * here + c[1] * up + c[2] * down
    value += pltpu.roll(c[3] * here, width - 1, axis=1)
    return value + pltpu.roll(c[4] * here, 1, axis=1)


def rim_kernel(step, late, sensors, misfit, part_edges, got, sent, edge, corr, scale, lam, send):
    depth = scale.shape[1]
    own, rows_y, rows_x = got.shape
    tiles = rows_y // TILE
    side = parity() if late else 1 - parity()
    z = side * (depth - 1)
    for tile in range(tiles):
        at = pl.ds(tile * TILE, TILE)
        c = [edge[side, j, at] for j in range(5)]
        miss = corr[step, side, at]
        gain = scale[step - 1, z, at]
        for k in range(own):
            value = part_edges[side, k, at] + miss * sent[k, at]
            value += from_met(c, *met(got, k, tile, tiles))
            lam[k, at] = value
            send[k, at] = gain * value
    plane = rows_y * rows_x
    start = lax.axis_index("space") * (depth * plane)
    lanes = lax.broadcasted_iota(jnp.int32, (1, rows_x), 1)
    for k in range(own):
        lifted, at_z, y, x = spot(sensors[k], start, rows_y, rows_x)
        here = (lifted >= plane) & (lifted < (depth + 1) * plane)

        @pl.when(here & (at_z == z))
        def _(k=k, y=y, x=x):
            add = jnp.where(lanes == x, misfit[step - 1, k], 0.0)
            send[k, pl.ds(y, 1), :] += add * scale[step - 1, z, pl.ds(y, 1), :]


def rim(step, late, sensors, misfit, part_edges, got, sent, edge, corr, scale):
    return pl.pallas_call(
        functools.partial(rim_kernel, step, late),
        in_specs=[SMEM] * 2 + [VMEM] * 6,
        out_specs=[VMEM] * 2,
        out_shape=[f32(*got.shape)] * 2,
        compiler_params=params(16),
        cost_estimate=cost(2_000_000, 1_500_000),
        name=f"rim{step}{'b' if late else 'a'}",
    )(sensors, misfit, part_edges, got, sent, edge, corr, scale)


def last_kernel(mu, v, coef, gain, got_a, got_b, edge, corr, grads, out, grad, part, sems):
    own, depth, rows_y, rows_x = mu.shape
    tiles = rows_y // TILE
    spread_field(coef, gain, 0, mu, v, part)
    copies = [
        pltpu.make_async_copy(part.at[:, z], out.at[:, z], sems.at[z]) for z in range(depth)
    ]
    for c in copies[1:-1]:
        c.start()
    total = grads[0]
    for i in range(1, grads.shape[0]):
        total += grads[i]
    grad[...] = total
    side_a = 1 - parity()
    for got, side in ((got_a, side_a), (got_b, 1 - side_a)):
        z = side * (depth - 1)
        for tile in range(tiles):
            at = pl.ds(tile * TILE, TILE)
            c = [edge[side, j, at] for j in range(5)]
            miss = corr[0, side, at]
            for k in range(own):
                value = part[k, z, at] + miss * v[k, z + 1, pl.ds(PAD + tile * TILE, TILE)]
                part[k, z, at] = value + from_met(c, *met(got, k, tile, tiles))
    for c in (copies[0], copies[-1]):
        c.start()
    for c in copies:
        c.wait()


def last_call(mu, v, coef, gain, got_a, got_b, edge, corr, grads):
    return pl.pallas_call(
        last_kernel,
        in_specs=[VMEM] * 9,
        out_specs=[ANY, VMEM],
        out_shape=[f32(*mu.shape), f32(*grads.shape[1:])],
        scratch_shapes=[
            pltpu.VMEM(mu.shape, jnp.float32),
            pltpu.SemaphoreType.DMA((mu.shape[1],)),
        ],
        compiler_params=params(16),
        cost_estimate=cost(40_000_000, 6_000_000),
        name="step0",
    )(mu, v, coef, gain, got_a, got_b, edge, corr, grads)


def turned(array, axis):
    count = lax.axis_size(axis)
    return [array] + [
        lax.ppermute(array, axis, [(i, (i + k) % count) for i in range(count)])
        for k in range(1, count)
    ]


def body(
    adjoint_end,
    checkpoints,
    dispersion,
    owner_steps,
    sensor_cells,
    misfit,
    release_cells,
    release_steps,
):
    own, depth, rows_y, rows_x = adjoint_end.shape
    slabs = lax.axis_size("space")
    pairs_a = [(i, i ^ 1) for i in range(slabs)]
    pairs_b = [(i, ((i + 1) ^ 1) - 1) for i in range(1, slabs - 1)]
    misfit = misfit.T

    def swap_a(x):
        return lax.ppermute(x, "space", pairs_a)

    def swap_b(x):
        return lax.ppermute(x, "space", pairs_b)

    parts, states = turned(dispersion, "sens"), turned(checkpoints, "sens")
    sent_a, sent_b, small_a, small_b = pack(
        owner_steps, sensor_cells, misfit, adjoint_end, checkpoints, dispersion
    )
    small_a, small_b = swap_a(small_a), swap_b(small_b)
    parts, states, sent_a, sent_b = lax.optimization_barrier((parts, states, sent_a, sent_b))
    got_a, got_b = swap_a(sent_a), swap_b(sent_b)
    small_a, small_b, parts = lax.optimization_barrier((small_a, small_b, parts))
    small_a, small_b = turned(small_a, "sens"), turned(small_b, "sens")
    coef, gain, scale, ends = planes(owner_steps, parts, states)

    field = f32(own, depth, rows_y, rows_x)
    edges = f32(2, own, rows_y, rows_x)
    tall = f32(own, depth + 2, rows_y + 2 * PAD, rows_x)
    kept = f32(own, release_cells.shape[0])
    sensors = (sensor_cells, misfit)
    release = (release_cells, release_steps)

    part, part_edges = field_call(
        first_kernel,
        "step2",
        (*sensors, adjoint_end, coef, gain, scale),
        [SMEM] * 2 + [VMEM, VMEM, VMEM, VMEM],
        [field, edges],
        [tall, field],
        40_000_000,
    )
    small_a, small_b, part_edges = lax.optimization_barrier((small_a, small_b, part_edges))
    edge, edge_raw, corr = ends_call(
        owner_steps, coef, ends, small_a, small_b, checkpoints.shape[0]
    )
    lam_b, send_b = rim(2, True, *sensors, part_edges, got_b, sent_b, edge_raw, corr, scale)
    got_b = swap_b(send_b)
    lam_a, send_a = rim(2, False, *sensors, part_edges, got_a, sent_a, edge_raw, corr, scale)
    got_a = swap_a(send_a)
    part, part_edges, grad, inside = field_call(
        functools.partial(middle_kernel, 1),
        "step1",
        (*sensors, *release, part, lam_a, lam_b, coef, gain, scale),
        [SMEM] * 4 + [VMEM] * 6,
        [field, edges, kept],
        [tall, field],
        40_000_000,
        release_cells.shape[0] + 1,
    )
    sent_a, sent_b = send_a, send_b
    lam_b, send_b = rim(1, True, *sensors, part_edges, got_b, sent_b, edge, corr, scale)
    got_b = swap_b(send_b)
    lam_a, send_a = rim(1, False, *sensors, part_edges, got_a, sent_a, edge, corr, scale)
    got_a = swap_a(send_a)
    grads, mu, v = field_call(
        front_kernel,
        "front0",
        (*sensors, *release, inside, grad, part, lam_a, lam_b, coef, edge, corr, gain, scale),
        [SMEM] * 5 + [VMEM] * 9,
        [f32(slabs, *kept.shape), field, tall],
        [kept],
        10_000_000,
    )
    grads = lax.all_to_all(grads, "space", 0, 0, tiled=True)
    grads, mu, v = lax.optimization_barrier((grads, mu, v))
    return tuple(last_call(mu, v, coef, gain, got_a, got_b, edge, corr, grads))


def solution(mesh):
    in_specs = (
        P("sens", "space", None, None),
        P("sens", "space", None, None),
        P(None, "space", "sens", None),
        P(),
        P("sens"),
        P("sens", None),
        P(),
        P(),
    )
    out_specs = (P("sens", "space", None, None), P("sens", None))
    return jax.shard_map(body, mesh=mesh, in_specs=in_specs, out_specs=out_specs, check_vma=False)
```

time: 250 us -> 63.7 us (0.25)
  blocking collectives: 80.2 us -> 13.3 us
  local copies, waits for them, and re-layouts: 49.8 us -> 2.74 us
  waiting for transfers between devices: 41.6 us -> 6.13 us
  other arithmetic: 32.7 us -> 0 us
  Pallas kernels: 0 us -> 22.2 us
  between operations: 23 us -> 0.89 us
  starting transfers between devices: 21.6 us -> 18.2 us
    psum x1 -> x0, blocking collectives: 77.5 us -> none  [body(): release_grad = lax.psum(partial_grad, 'space')]
    add x3 -> x0, local copies, waits for them, and re-layouts: 26 us -> none  [body(): lam = mixed + applied[1:] + retard_slope(conc) * applied[0] * mixed]
    pallas_call x0 -> x11, Pallas kernels: none -> 22.2 us  [the longest x3 9.49 us: field_call(): pl.pallas_call(kernel, in_specs=specs, out_specs=[VMEM] * len(outs) + [SM...]
    gather x3 -> x0, local copies, waits for them, and re-layouts: 20.4 us -> none  [body(): values = jnp.take(lam.reshape(own_sensors, cells), release_index, axis=1)]
    ppermute x8 -> x12, waiting for transfers between devices: 23.9 us -> 6.13 us  [the longest x4 6.11 us: swap_a(): return lax.ppermute(x, 'space', pairs_a)]
    psum x1 -> x0, waiting for transfers between devices: 17.7 us -> none  [broadcast(): return lax.psum(jnp.where(mine, array, jnp.zeros_like(array)), axis)]
    add x5 -> x0, other arithmetic: 15.6 us -> none  [the longest x3 15 us: apply_op(): total = total + 0.5 * sign * flux]
    all_to_all x0 -> x1, blocking collectives: none -> 13.3 us  [body(): grads = lax.all_to_all(grads, 'space', 0, 0, tiled=True)]
  transfers between devices with their start and end apart: 9 -> 12, of which waited for: 5 -> 2; matrix products, arithmetic and copies ran while one was open for 15% -> 0% of each run, Pallas kernels for 0% -> 30%
where the time goes in v2:
time: 63.7 us; the launch traced here: 63.5 us
  Pallas kernels  22.2 us (35%)
  starting transfers between devices  18.2 us (29%)
  blocking collectives  13.3 us (21%)
  waiting for transfers between devices  6.13 us (10%)
  local copies, waits for them, and re-layouts  2.74 us (4%)
  between operations  0.89 us (1%)
    ppermute x4, starting transfers between devices, swap_a(): return lax.ppermute(x, 'space', pairs_a)  14.3 us
    all_to_all x1, blocking collectives, body(): grads = lax.all_to_all(grads, 'space', 0, 0, tiled=True)  13.3 us
    pallas_call x3, Pallas kernels, field_call(): pl.pallas_call(kernel, in_specs=specs, out_specs=[VMEM] * len(outs) + [SM...  9.49 us
    ppermute x4, waiting for transfers between devices, swap_a(): return lax.ppermute(x, 'space', pairs_a)  6.11 us
    pallas_call x4, Pallas kernels, rim(): pl.pallas_call(functools.partial(rim_kernel, step, late), in_specs=[SMEM]...  3.64 us
    pallas_call x1, Pallas kernels, last_call(): pl.pallas_call(last_kernel, in_specs=[VMEM] * 9, out_specs=[ANY, VMEM], o...  3.32 us
    ppermute x4, starting transfers between devices, swap_b(): return lax.ppermute(x, 'space', pairs_b)  2.82 us
    unnamed x22, local copies, waits for them, and re-layouts  2.74 us
  transfers between devices with their start and end apart: 12, of which 2 were waited for; matrix products, arithmetic and copies ran while one was open for 0% of the time, Pallas kernels for 30%

profile of v2, /device:TPU:0, one launch (start us, length us, event | category | flops | bytes accessed | tf_op | source)
XLA Modules:
  0.0 63.5 jit_solution(11187170349356695420)
XLA Ops:
  0.6 0.5 collective-permute-start.3
  1.1 0.1 collective-permute-start.2
  1.2 2.7 %pack.1 = (f32[8,64,128]{2,1,0:T(8,128)}, f32[8,64,128]{2,1,0:T(8,128)}, f32[224,128]{1,0:T(8,128)}, f32[224,128]{1,0:T(8,128)}) custom-call(s32[3]{0:T(128)} %refs_0_.3, s32[8]{0:T(128)} %sensors.15, f32[3,8]{1,0:T(4,128)} %bitcast.1, f32[8,4,64,128]{3,2,1,0:T(8,128)} %lam.1, f32[4,4,64,128]{3,2,1,0:T(8,128)} %refs_3_, f32[6,4,32,128]{3,2,1,0:T(8,128)} %refs_1_), custom_call_target="tpu_custom_call" | custom-call | flops 1000 | bytes 1000 | tf_op jit(solution)/shard_map/pack/pallas_call | solution.py:101
  4.0 3.0 %collective-permute-start = (f32[224,128]{1,0:T(8,128)}, f32[224,128]{1,0:T(8,128)S(1)}, u32[]{:S(2)}, u32[]{:S(2)}) collective-permute-start(f32[224,128]{1,0:T(8,128)} %get-tuple-element.48), channel_id=1, source_target_pairs={{0,2},{2,0},{4,6},{6,4},{8,10},{10,8},{12,14},{14,12},{16,18},{18,... | collective-permute-start | bytes 344072 | tf_op jit(solution)/shard_map/ppermute | solution.py:674
  6.9 0.7 %collective-permute-start.1 = (f32[224,128]{1,0:T(8,128)}, f32[224,128]{1,0:T(8,128)S(1)}, u32[]{:S(2)}, u32[]{:S(2)}) collective-permute-start(f32[224,128]{1,0:T(8,128)} %get-tuple-element.49), channel_id=1, source_target_pairs={{2,4},{4,2},{6,8},{8,6},{10,12},{12,10},{14,16},{16,14},{18,20},{2... | collective-permute-start | bytes 344072 | tf_op jit(solution)/shard_map/ppermute | solution.py:677
  7.6 0.0 copy-start.5
  7.6 0.0 copy-start.6
  7.7 0.0 copy-start
  7.7 0.8 %collective-permute-start.7 = (f32[8,64,128]{2,1,0:T(8,128)}, f32[8,64,128]{2,1,0:T(8,128)S(1)}, u32[]{:S(2)}, u32[]{:S(2)}) collective-permute-start(f32[8,64,128]{2,1,0:T(8,128)} %get-tuple-element.75.sent), channel_id=1, source_target_pairs={{2,4},{4,2},{6,8},{8,6},{10,12},{12,10},{14,16},{16,14},{18,20},{2... | collective-permute-start | bytes 786440 | tf_op jit(solution)/shard_map/ppermute | solution.py:677
  8.5 5.5 %collective-permute-start.6 = (f32[8,64,128]{2,1,0:T(8,128)}, f32[8,64,128]{2,1,0:T(8,128)S(1)}, u32[]{:S(2)}, u32[]{:S(2)}) collective-permute-start(f32[8,64,128]{2,1,0:T(8,128)} %get-tuple-element.66.sent), channel_id=1, source_target_pairs={{0,2},{2,0},{4,6},{6,4},{8,10},{10,8},{12,14},{14,12},{16,18},{18,... | collective-permute-start | bytes 786440 | tf_op jit(solution)/shard_map/ppermute | solution.py:674
  14.0 0.5 collective-permute-start.5
  14.5 1.0 %copy-done.1 = f32[4,4,64,128]{3,2,1,0:T(8,128)S(1)} copy-done((f32[4,4,64,128]{3,2,1,0:T(8,128)S(1)}, f32[4,4,64,128]{3,2,1,0:T(8,128)}, u32[]{:S(2)}) %copy-start.1) | copy-done | bytes 524312
  15.6 1.0 %copy-done.2 = f32[6,4,32,128]{3,2,1,0:T(8,128)S(1)} copy-done((f32[6,4,32,128]{3,2,1,0:T(8,128)S(1)}, f32[6,4,32,128]{3,2,1,0:T(8,128)}, u32[]{:S(2)}) %copy-start.2) | copy-done | bytes 393240
  16.6 0.7 %copy-done.7 = s32[3]{0:T(128)S(1)} copy-done((s32[3]{0:T(128)S(1)}, s32[3]{0:T(128)}, u32[]{:S(2)}) %copy-start.7) | copy-done | bytes 36
  17.2 2.0 %planes.1 = (f32[19,4,64,128]{3,2,1,0:T(8,128)S(1)}, f32[3,4,64,128]{3,2,1,0:T(8,128)S(1)}, f32[3,4,64,128]{3,2,1,0:T(8,128)S(1)}, f32[3,2,64,128]{3,2,1,0:T(8,128)S(1)}) custom-call(s32[3]{0:T(128)S(1)} %copy-done.7, f32[6,4,32,128]{3,2,1,0:T(8,128)S(1)} %copy-done.2, f32[6,4,32,128]{3,2,1,0:T(8,128)S(1)} %collective-permute-done.2.refs_2_, ...), custom_call_target="tpu_custom_call" | custom-call | flops 2000000000 | bytes 60000000 | tf_op jit(solution)/shard_map/planes/pallas_call | solution.py:243
  19.3 2.4 %step2.1 = (f32[8,4,64,128]{3,2,1,0:T(8,128)S(1)}, f32[2,8,64,128]{3,2,1,0:T(8,128)S(1)}) custom-call(s32[8]{0:T(128)S(1)} %copy-done.6, f32[3,8]{1,0:T(4,128)S(1)} %bitcast.2, f32[8,4,64,128]{3,2,1,0:T(8,128)S(1)} %copy-done, f32[19,4,64,128]{3,2,1,0:T(8,128)S(1)} %get-tuple-element.58.coef.refs_1_, f32[3,4,64,128]{3,2,1,0:T(8,128)S(1)} %get-tuple-element.59.gain, ...), custom_call_target="tpu_custom_call" | custom-call | flops 40000000 | bytes 4000000 | tf_op jit(solution)/shard_map/step2/pallas_call | solution.py:531
  21.8 1.0 %ends.1 = (f32[2,5,64,128]{3,2,1,0:T(8,128)S(1)}, f32[2,5,64,128]{3,2,1,0:T(8,128)S(1)}, f32[3,2,64,128]{3,2,1,0:T(8,128)S(1)}) custom-call(s32[3]{0:T(128)S(1)} %copy-done.8, f32[19,4,64,128]{3,2,1,0:T(8,128)S(1)} %get-tuple-element.58.coef.refs_1_, f32[3,2,64,128]{3,2,1,0:T(8,128)S(1)} %get-tuple-element.67.refs_2_, ...), custom_call_target="tpu_custom_call" | custom-call | flops 1000000 | bytes 1000000 | tf_op jit(solution)/shard_map/ends/pallas_call | solution.py:339
  22.8 0.0 copy-start.10
  22.8 0.9 %rim2b.1 = (f32[8,64,128]{2,1,0:T(8,128)S(1)}, f32[8,64,128]{2,1,0:T(8,128)S(1)}) custom-call(s32[8]{0:T(128)S(1)} %copy-done.6, f32[3,8]{1,0:T(4,128)S(1)} %bitcast.3, f32[2,8,64,128]{3,2,1,0:T(8,128)S(1)} %get-tuple-element.65.part_edges, f32[8,64,128]{2,1,0:T(8,128)S(1)} %collective-permute-done.7.got, f32[8,64,128]{2,1,0:T(8,128)S(1)} %copy-done.4, ...), custom_call_target="tpu_custom_call" | custom-call | flops 2000000 | bytes 1500000 | tf_op jit(solution)/shard_map/rim2b/pallas_call | solution.py:593
  23.8 0.7 %collective-permute-start.9 = (f32[8,64,128]{2,1,0:T(8,128)S(1)}, f32[8,64,128]{2,1,0:T(8,128)S(1)}, u32[]{:S(2)}, u32[]{:S(2)}) collective-permute-start(f32[8,64,128]{2,1,0:T(8,128)S(1)} %get-tuple-element.84.sent), channel_id=1, source_target_pairs={{2,4},{4,2},{6,8},{8,6},{10,12},{12,10},{14,16},{16,14},{18,20},{2... | collective-permute-start | bytes 786440 | tf_op jit(solution)/shard_map/ppermute | solution.py:677
  24.5 1.6 %collective-permute-done.6.got = f32[8,64,128]{2,1,0:T(8,128)S(1)} collective-permute-done((f32[8,64,128]{2,1,0:T(8,128)}, f32[8,64,128]{2,1,0:T(8,128)S(1)}, u32[]{:S(2)}, u32[]{:S(2)}) %collective-permute-start.6) | collective-permute-done | bytes 262176 | tf_op jit(solution)/shard_map/ppermute | solution.py:674
  26.1 0.9 %rim2a.1 = (f32[8,64,128]{2,1,0:T(8,128)S(1)}, f32[8,64,128]{2,1,0:T(8,128)S(1)}) custom-call(s32[8]{0:T(128)S(1)} %copy-done.6, f32[3,8]{1,0:T(4,128)S(1)} %bitcast.4, f32[2,8,64,128]{3,2,1,0:T(8,128)S(1)} %get-tuple-element.65.part_edges, f32[8,64,128]{2,1,0:T(8,128)S(1)} %collective-permute-done.6.got, f32[8,64,128]{2,1,0:T(8,128)S(1)} %copy-done.3, ...), custom_call_target="tpu_custom_call" | custom-call | flops 2000000 | bytes 1500000 | tf_op jit(solution)/shard_map/rim2a/pallas_call | solution.py:593
  27.0 4.0 %collective-permute-start.8 = (f32[8,64,128]{2,1,0:T(8,128)S(1)}, f32[8,64,128]{2,1,0:T(8,128)S(1)}, u32[]{:S(2)}, u32[]{:S(2)}) collective-permute-start(f32[8,64,128]{2,1,0:T(8,128)S(1)} %get-tuple-element.81.sent), channel_id=1, source_target_pairs={{0,2},{2,0},{4,6},{6,4},{8,10},{10,8},{12,14},{14,12},{16,18},{18,... | collective-permute-start | bytes 786440 | tf_op jit(solution)/shard_map/ppermute | solution.py:674
  31.0 4.8 %step1.1 = (f32[8,4,64,128]{3,2,1,0:T(8,128)S(1)}, f32[2,8,64,128]{3,2,1,0:T(8,128)S(1)}, f32[8,128]{1,0:T(8,128)S(1)}, s32[129]{0:T(256)S(1)}) custom-call(s32[8]{0:T(128)S(1)} %copy-done.6, f32[3,8]{1,0:T(4,128)S(1)} %bitcast.5, s32[128]{0:T(128)S(1)} %copy-done.9, s32[128]{0:T(128)S(1)} %copy-done.10, f32[8,4,64,128]{3,2,1,0:T(8,128)S(1)} %get-tuple-element.61.lam, ...), custom_call_target="tpu_custom_call" | custom-call | flops 40000000 | bytes 4000000 | tf_op jit(solution)/shard_map/step1/pallas_call | solution.py:531
  35.8 0.9 %rim1b.1 = (f32[8,64,128]{2,1,0:T(8,128)S(1)}, f32[8,64,128]{2,1,0:T(8,128)S(1)}) custom-call(s32[8]{0:T(128)S(1)} %copy-done.6, f32[3,8]{1,0:T(4,128)S(1)} %bitcast.6, f32[2,8,64,128]{3,2,1,0:T(8,128)S(1)} %get-tuple-element.80.part_edges, f32[8,64,128]{2,1,0:T(8,128)S(1)} %collective-permute-done.9.got, f32[8,64,128]{2,1,0:T(8,128)S(1)} %get-tuple-element.84.sent, ...), custom_call_target="tpu_custom_call" | custom-call | flops 2000000 | bytes 1500000 | tf_op jit(solution)/shard_map/rim1b/pallas_call | solution.py:593
  36.7 0.7 %collective-permute-start.11 = (f32[8,64,128]{2,1,0:T(8,128)S(1)}, f32[8,64,128]{2,1,0:T(8,128)S(1)}, u32[]{:S(2)}, u32[]{:S(2)}) collective-permute-start(f32[8,64,128]{2,1,0:T(8,128)S(1)} %get-tuple-element.92), channel_id=1, source_target_pairs={{2,4},{4,2},{6,8},{8,6},{10,12},{12,10},{14,16},{16,14},{18,20},{2... | collective-permute-start | bytes 786440 | tf_op jit(solution)/shard_map/ppermute | solution.py:677
  37.4 4.5 %collective-permute-done.8.got = f32[8,64,128]{2,1,0:T(8,128)S(1)} collective-permute-done((f32[8,64,128]{2,1,0:T(8,128)S(1)}, f32[8,64,128]{2,1,0:T(8,128)S(1)}, u32[]{:S(2)}, u32[]{:S(2)}) %collective-permute-start.8) | collective-permute-done | bytes 262176 | tf_op jit(solution)/shard_map/ppermute | solution.py:674
  41.9 0.9 %rim1a.1 = (f32[8,64,128]{2,1,0:T(8,128)S(1)}, f32[8,64,128]{2,1,0:T(8,128)S(1)}) custom-call(s32[8]{0:T(128)S(1)} %copy-done.6, f32[3,8]{1,0:T(4,128)S(1)} %bitcast.7, f32[2,8,64,128]{3,2,1,0:T(8,128)S(1)} %get-tuple-element.80.part_edges, f32[8,64,128]{2,1,0:T(8,128)S(1)} %collective-permute-done.8.got, f32[8,64,128]{2,1,0:T(8,128)S(1)} %get-tuple-element.81.sent, ...), custom_call_target="tpu_custom_call" | custom-call | flops 2000000 | bytes 1500000 | tf_op jit(solution)/shard_map/rim1a/pallas_call | solution.py:593
  42.8 1.7 %collective-permute-start.10 = (f32[8,64,128]{2,1,0:T(8,128)S(1)}, f32[8,64,128]{2,1,0:T(8,128)S(1)}, u32[]{:S(2)}, u32[]{:S(2)}) collective-permute-start(f32[8,64,128]{2,1,0:T(8,128)S(1)} %get-tuple-element.91), channel_id=1, source_target_pairs={{0,2},{2,0},{4,6},{6,4},{8,10},{10,8},{12,14},{14,12},{16,18},{18,... | collective-permute-start | bytes 786440 | tf_op jit(solution)/shard_map/ppermute | solution.py:674
  44.5 2.3 %front0.1 = (f32[16,8,128]{2,1,0:T(8,128)S(1)}, f32[8,4,64,128]{3,2,1,0:T(8,128)S(1)}, f32[8,6,80,128]{3,2,1,0:T(8,128)S(1)}) custom-call(s32[8]{0:T(128)S(1)} %copy-done.6, f32[3,8]{1,0:T(4,128)S(1)} %bitcast.8, s32[128]{0:T(128)S(1)} %copy-done.9, s32[128]{0:T(128)S(1)} %copy-done.10, s32[129]{0:T(256)S(1)} %get-tuple-element.77.inside, ...), custom_call_target="tpu_custom_call" | custom-call | flops 10000000 | bytes 4000000 | tf_op jit(solution)/shard_map/front0/pallas_call | solution.py:531
  46.8 13.3 %all_to_all.5.grads = f32[16,8,128]{2,1,0:T(8,128)S(1)} all-to-all(f32[16,8,128]{2,1,0:T(8,128)S(1)} %get-tuple-element.86), channel_id=1, replica_groups=mesh['space'=16,'sens'=2] {'space'}, dimensions={0} | all-to-all | bytes 131072 | tf_op jit(solution)/shard_map/all_to_all | solution.py:738
  60.1 3.3 %step0.1 = (f32[8,4,64,128]{3,2,1,0:T(8,128)}, f32[8,128]{1,0:T(8,128)}) custom-call(f32[8,4,64,128]{3,2,1,0:T(8,128)S(1)} %get-tuple-element.89.mu, f32[8,6,80,128]{3,2,1,0:T(8,128)S(1)} %get-tuple-element.90.v, f32[19,4,64,128]{3,2,1,0:T(8,128)S(1)} %get-tuple-element.58.coef.refs_1_, f32[3,4,64,128]{3,2,1,0:T(8,128)S(1)} %get-tuple-element.59.gain, ...), custom_call_target="tpu_custom_call" | custom-call | flops 40000000 | bytes 6000000 | tf_op jit(solution)/shard_map/step0/pallas_call | solution.py:634
  (26 shorter events, 0.1 us)
Async XLA Ops:
  0.6 7.0 %collective-permute-start.3 = (f32[4,4,64,128]{3,2,1,0:T(8,128)}, f32[4,4,64,128]{3,2,1,0:T(8,128)S(1)}, u32[]{:S(2)}, u32[]{:S(2)}) collective-permute-start(f32[4,4,64,128]{3,2,1,0:T(8,128)} %refs_3_), channel_id=1, source_target_pairs={{0,1},{1,0},{2,3},{3,2},{4,5},{5,4},{6,7},{7,6},{8,9},{9,8},{10,11... | collective-permute-start | bytes 1572872 | tf_op jit(solution)/shard_map/ppermute | solution.py:652
  1.1 6.5 %collective-permute-start.2 = (f32[6,4,32,128]{3,2,1,0:T(8,128)}, f32[6,4,32,128]{3,2,1,0:T(8,128)S(1)}, u32[]{:S(2)}, u32[]{:S(2)}) collective-permute-start(f32[6,4,32,128]{3,2,1,0:T(8,128)} %refs_1_), channel_id=1, source_target_pairs={{0,1},{1,0},{2,3},{3,2},{4,5},{5,4},{6,7},{7,6},{8,9},{9,8},{10,11... | collective-permute-start | bytes 1179656 | tf_op jit(solution)/shard_map/ppermute | solution.py:652
  4.0 10.0 %collective-permute-start = (f32[224,128]{1,0:T(8,128)}, f32[224,128]{1,0:T(8,128)S(1)}, u32[]{:S(2)}, u32[]{:S(2)}) collective-permute-start(f32[224,128]{1,0:T(8,128)} %get-tuple-element.48), channel_id=1, source_target_pairs={{0,2},{2,0},{4,6},{6,4},{8,10},{10,8},{12,14},{14,12},{16,18},{18,... | collective-permute-start | bytes 344072 | tf_op jit(solution)/shard_map/ppermute | solution.py:674
  6.9 7.1 %collective-permute-start.1 = (f32[224,128]{1,0:T(8,128)}, f32[224,128]{1,0:T(8,128)S(1)}, u32[]{:S(2)}, u32[]{:S(2)}) collective-permute-start(f32[224,128]{1,0:T(8,128)} %get-tuple-element.49), channel_id=1, source_target_pairs={{2,4},{4,2},{6,8},{8,6},{10,12},{12,10},{14,16},{16,14},{18,20},{2... | collective-permute-start | bytes 344072 | tf_op jit(solution)/shard_map/ppermute | solution.py:677
  7.6 11.7 %copy-start.5 = (f32[8,3]{0,1:T(4,128)S(1)}, f32[8,3]{0,1:T(4,128)}, u32[]{:S(2)}) copy-start(f32[8,3]{0,1:T(4,128)} %param.13) | copy-start | bytes 292
  7.6 11.7 %copy-start.6 = (s32[8]{0:T(128)S(1)}, s32[8]{0:T(128)}, u32[]{:S(2)}) copy-start(s32[8]{0:T(128)} %sensors.15) | copy-start | bytes 100
  7.7 11.7 %copy-start = (f32[8,4,64,128]{3,2,1,0:T(8,128)S(1)}, f32[8,4,64,128]{3,2,1,0:T(8,128)}, u32[]{:S(2)}) copy-start(f32[8,4,64,128]{3,2,1,0:T(8,128)} %lam.1) | copy-start | bytes 3145732
  7.7 15.2 %collective-permute-start.7 = (f32[8,64,128]{2,1,0:T(8,128)}, f32[8,64,128]{2,1,0:T(8,128)S(1)}, u32[]{:S(2)}, u32[]{:S(2)}) collective-permute-start(f32[8,64,128]{2,1,0:T(8,128)} %get-tuple-element.75.sent), channel_id=1, source_target_pairs={{2,4},{4,2},{6,8},{8,6},{10,12},{12,10},{14,16},{16,14},{18,20},{2... | collective-permute-start | bytes 786440 | tf_op jit(solution)/shard_map/ppermute | solution.py:677
  8.5 17.6 %collective-permute-start.6 = (f32[8,64,128]{2,1,0:T(8,128)}, f32[8,64,128]{2,1,0:T(8,128)S(1)}, u32[]{:S(2)}, u32[]{:S(2)}) collective-permute-start(f32[8,64,128]{2,1,0:T(8,128)} %get-tuple-element.66.sent), channel_id=1, source_target_pairs={{0,2},{2,0},{4,6},{6,4},{8,10},{10,8},{12,14},{14,12},{16,18},{18,... | collective-permute-start | bytes 786440 | tf_op jit(solution)/shard_map/ppermute | solution.py:674
  14.0 7.8 %collective-permute-start.4 = (f32[224,128]{1,0:T(8,128)S(1)}, f32[224,128]{1,0:T(8,128)S(1)}, u32[]{:S(2)}, u32[]{:S(2)}) collective-permute-start(f32[224,128]{1,0:T(8,128)S(1)} %collective-permute-done.refs_3_), channel_id=1, source_target_pairs={{0,1},{1,0},{2,3},{3,2},{4,5},{5,4},{6,7},{7,6},{8,9},{9,8},{10,11... | collective-permute-start | bytes 344072 | tf_op jit(solution)/shard_map/ppermute | solution.py:652
  14.0 7.8 %collective-permute-start.5 = (f32[224,128]{1,0:T(8,128)S(1)}, f32[224,128]{1,0:T(8,128)S(1)}, u32[]{:S(2)}, u32[]{:S(2)}) collective-permute-start(f32[224,128]{1,0:T(8,128)S(1)} %collective-permute-done.1.refs_5_), channel_id=1, source_target_pairs={{0,1},{1,0},{2,3},{3,2},{4,5},{5,4},{6,7},{7,6},{8,9},{9,8},{10,11... | collective-permute-start | bytes 344072 | tf_op jit(solution)/shard_map/ppermute | solution.py:652
  14.5 1.0 %copy-start.1 = (f32[4,4,64,128]{3,2,1,0:T(8,128)S(1)}, f32[4,4,64,128]{3,2,1,0:T(8,128)}, u32[]{:S(2)}) copy-start(f32[4,4,64,128]{3,2,1,0:T(8,128)} %refs_3_) | copy-start | bytes 1572868
  15.6 1.0 %copy-start.2 = (f32[6,4,32,128]{3,2,1,0:T(8,128)S(1)}, f32[6,4,32,128]{3,2,1,0:T(8,128)}, u32[]{:S(2)}) copy-start(f32[6,4,32,128]{3,2,1,0:T(8,128)} %refs_1_) | copy-start | bytes 1179652
  16.6 0.7 %copy-start.7 = (s32[3]{0:T(128)S(1)}, s32[3]{0:T(128)}, u32[]{:S(2)}) copy-start(s32[3]{0:T(128)} %refs_0_.3) | copy-start | bytes 40
  19.3 2.5 %copy-start.8 = (s32[3]{0:T(128)S(1)}, s32[3]{0:T(128)}, u32[]{:S(2)}) copy-start(s32[3]{0:T(128)} %refs_0_.3) | copy-start | bytes 40
  21.8 1.1 %copy-start.4 = (f32[8,64,128]{2,1,0:T(8,128)S(1)}, f32[8,64,128]{2,1,0:T(8,128)}, u32[]{:S(2)}) copy-start(f32[8,64,128]{2,1,0:T(8,128)} %get-tuple-element.75.sent) | copy-start | bytes 786436
  21.8 4.3 %copy-start.3 = (f32[8,64,128]{2,1,0:T(8,128)S(1)}, f32[8,64,128]{2,1,0:T(8,128)}, u32[]{:S(2)}) copy-start(f32[8,64,128]{2,1,0:T(8,128)} %get-tuple-element.66.sent) | copy-start | bytes 786436
  22.8 8.2 %copy-start.9 = (s32[128]{0:T(128)S(1)}, s32[128]{0:T(128)}, u32[]{:S(2)}) copy-start(s32[128]{0:T(128)} %cells.3) | copy-start | bytes 1540
  22.8 8.2 %copy-start.10 = (s32[128]{0:T(128)S(1)}, s32[128]{0:T(128)}, u32[]{:S(2)}) copy-start(s32[128]{0:T(128)} %steps.3) | copy-start | bytes 1540
  23.8 12.0 %collective-permute-start.9 = (f32[8,64,128]{2,1,0:T(8,128)S(1)}, f32[8,64,128]{2,1,0:T(8,128)S(1)}, u32[]{:S(2)}, u32[]{:S(2)}) collective-permute-start(f32[8,64,128]{2,1,0:T(8,128)S(1)} %get-tuple-element.84.sent), channel_id=1, source_target_pairs={{2,4},{4,2},{6,8},{8,6},{10,12},{12,10},{14,16},{16,14},{18,20},{2... | collective-permute-start | bytes 786440 | tf_op jit(solution)/shard_map/ppermute | solution.py:677
  27.0 14.9 %collective-permute-start.8 = (f32[8,64,128]{2,1,0:T(8,128)S(1)}, f32[8,64,128]{2,1,0:T(8,128)S(1)}, u32[]{:S(2)}, u32[]{:S(2)}) collective-permute-start(f32[8,64,128]{2,1,0:T(8,128)S(1)} %get-tuple-element.81.sent), channel_id=1, source_target_pairs={{0,2},{2,0},{4,6},{6,4},{8,10},{10,8},{12,14},{14,12},{16,18},{18,... | collective-permute-start | bytes 786440 | tf_op jit(solution)/shard_map/ppermute | solution.py:674
  36.7 23.4 %collective-permute-start.11 = (f32[8,64,128]{2,1,0:T(8,128)S(1)}, f32[8,64,128]{2,1,0:T(8,128)S(1)}, u32[]{:S(2)}, u32[]{:S(2)}) collective-permute-start(f32[8,64,128]{2,1,0:T(8,128)S(1)} %get-tuple-element.92), channel_id=1, source_target_pairs={{2,4},{4,2},{6,8},{8,6},{10,12},{12,10},{14,16},{16,14},{18,20},{2... | collective-permute-start | bytes 786440 | tf_op jit(solution)/shard_map/ppermute | solution.py:677
  42.8 17.3 %collective-permute-start.10 = (f32[8,64,128]{2,1,0:T(8,128)S(1)}, f32[8,64,128]{2,1,0:T(8,128)S(1)}, u32[]{:S(2)}, u32[]{:S(2)}) collective-permute-start(f32[8,64,128]{2,1,0:T(8,128)S(1)} %get-tuple-element.91), channel_id=1, source_target_pairs={{0,2},{2,0},{4,6},{6,4},{8,10},{10,8},{12,14},{14,12},{16,18},{18,... | collective-permute-start | bytes 786440 | tf_op jit(solution)/shard_map/ppermute | solution.py:674

commit v3 on v2

--- a/solution.py
+++ b/solution.py
@@ -16,6 +16,7 @@
 PLANES = 19
 LOW = (ZM, ZMYP, ZMYM, XPZM, XMZM)
 HIGH = (ZP, ZPYP, ZPYM, XPZP, XMZP)
+IN_LAYER = (CENTRE, YP, YM, XP, XPYP, XPYM, XM, XMYP, XMYM)
 
 VMEM = pl.BlockSpec(memory_space=pltpu.VMEM)
 SMEM = pl.BlockSpec(memory_space=pltpu.SMEM)
@@ -105,7 +106,7 @@
         out_shape=[f32(own, rows_y, rows_x)] * 2 + [small, small],
         scratch_shapes=[pltpu.SemaphoreType.DMA((12,))],
         compiler_params=params(60),
-        cost_estimate=cost(1000, 1000),
+        cost_estimate=cost(20_000_000_000, 60_000_000),
         name="pack",
     )(owner, sensors, misfit, adj, ckpt, disp)
 
@@ -368,7 +369,7 @@
             mu[k, depth - 1 - z_a] = lam_b[k]
 
 
-def add_misfit(step, sensors, misfit, mu):
+def add_misfit(step, sensors, misfit, mu, skip=0):
     own, depth, rows_y, rows_x = mu.shape
     plane = rows_y * rows_x
     start = lax.axis_index("space") * (depth * plane)
@@ -376,7 +377,7 @@
     for k in range(own):
         lifted, z, y, x = spot(sensors[k], start, rows_y, rows_x)
 
-        @pl.when((lifted >= plane) & (lifted < (depth + 1) * plane))
+        @pl.when((lifted >= (1 + skip) * plane) & (lifted < (depth + 1 - skip) * plane))
         def _(k=k, z=z, y=y, x=x):
             mu[k, z, pl.ds(y, 1), :] += jnp.where(lanes == x, misfit[step, k], 0.0)
 
@@ -416,32 +417,30 @@
             part_edges[1, k] = part[k, depth - 1]
 
 
-def collect(wanted, release, shape, total, own_row, near_row=None):
+def taker(total, own, rows_x):
+    lanes = lax.broadcasted_iota(jnp.int32, (1, rows_x), 1)
+    slots = lax.broadcasted_iota(jnp.int32, (own, total.shape[1]), 1)
+
+    def take(r, x, row):
+        value = jnp.sum(jnp.where(lanes == x, row, 0.0), axis=-1, keepdims=True)
+        total[...] += jnp.where(slots == r, value, 0.0)
+
+    return take
+
+
+def collect(wanted, release, shape, total, own_row):
     cells, steps, inside = release
     own, depth, rows_y, rows_x = shape
     start = lax.axis_index("space") * (depth * rows_y * rows_x)
-    lanes = lax.broadcasted_iota(jnp.int32, (1, rows_x), 1)
-    slots = lax.broadcasted_iota(jnp.int32, (own, total.shape[1]), 1)
-
-    def take(r, x, row):
-        value = jnp.sum(jnp.where(lanes == x, row, 0.0), axis=-1, keepdims=True)
-        total[...] += jnp.where(slots == r, value, 0.0)
+    take = taker(total, own, rows_x)
 
     def visit(i, carry):
         r = inside[i]
         _, z, y, x = spot(cells[r], start, rows_y, rows_x)
-        fits = steps[r] == wanted
-        mine = (z >= 0) & (z < depth)
-
-        @pl.when(fits & mine)
+
+        @pl.when((steps[r] == wanted) & (z >= 0) & (z < depth))
         def _():
             take(r, x, own_row(z, y))
-
-        if near_row is not None:
-
-            @pl.when(fits & jnp.logical_not(mine))
-            def _():
-                take(r, x, near_row(jnp.where(z < 0, 0, 1), y))
 
         return carry
 
@@ -455,13 +454,8 @@
 
     def note(r, found):
         local = cells[r] - start
-        near = (local >= -plane) & (local < (depth + 1) * plane)
-
-        @pl.when(near)
-        def _():
-            inside[found] = r
-
-        return found + jnp.where(near, 1, 0)
+        inside[found] = r
+        return found + jnp.where((local >= -plane) & (local < (depth + 1) * plane), 1, 0)
 
     inside[inside.shape[0] - 1] = lax.fori_loop(0, cells.shape[0], note, jnp.int32(0))
 
@@ -479,50 +473,105 @@
 
 
 def middle_kernel(
-    step, sensors, misfit, cells, steps, lam, lam_a, lam_b, coef, gain, scale, part, part_edges, grad, inside, v, mu
+    sensors, misfit, cells, steps, lam, lam_a, lam_b, coef, gain, scale, base, part_edges, grad, inside, v, mu, part
 ):
+    own, depth, rows_y, rows_x = mu.shape
     gather_field(False, lam, lam_a, lam_b, mu)
     grad[...] = jnp.zeros_like(grad)
     list_releases(cells, mu.shape, inside)
-    collect(
-        step + 1, (cells, steps, inside), mu.shape, grad, lambda z, y: rows_of(mu, z, pl.ds(y, 1))
-    )
-    add_misfit(step, sensors, misfit, mu)
-    scale_field(scale, step, mu, v)
-    spread_field(coef, gain, step, mu, v, part, part_edges)
-
-
-def front_kernel(
-    sensors, misfit, cells, steps, inside, grad_in, lam, lam_a, lam_b, coef, edge, corr, gain, scale, grads, mu, v, total
-):
-    own, depth, rows_y, rows_x = mu.shape
-    gather_field(False, lam, lam_a, lam_b, mu)
-    total[...] = grad_in[...]
     release = (cells, steps, inside)
-    collect(1, release, mu.shape, total, lambda z, y: rows_of(mu, z, pl.ds(y, 1)))
-    add_misfit(0, sensors, misfit, mu)
+    collect(2, release, mu.shape, grad, lambda z, y: rows_of(mu, z, pl.ds(y, 1)))
+    add_misfit(1, sensors, misfit, mu)
+    scale_field(scale, 1, mu, v)
+    spread_field(coef, gain, 1, mu, v, part, part_edges)
+
+    void = jnp.zeros((rows_y, rows_x), jnp.float32)
+    for k in range(own):
+        mu[k, 0] = void
+        mu[k, depth - 1] = void
+        for z in range(1, depth - 1):
+            mu[k, z] = part[k, z]
+    collect(1, release, mu.shape, grad, lambda z, y: rows_of(mu, z, pl.ds(y, 1)))
+    add_misfit(0, sensors, misfit, mu, 1)
     scale_field(scale, 0, mu, v)
+    spread_field(coef, gain, 0, mu, v, base)
 
     def own_row(z, y):
         at = pl.ds(y, 1)
         c = [coef[j, z, at] for j in range(PLANES)]
         spread = stencil(c, lambda dz, dy: rows_of(v, z + 1 + dz, pl.ds(PAD + y + dy, 1)))
-        at_edge = (z == 0) | (z == depth - 1)
-        miss = jnp.where(at_edge, corr[0, jnp.where(z == 0, 0, 1), at], 0.0)
-        return rows_of(mu, z, at) * gain[0, z, at] + spread + miss * rows_of(v, z + 1, pl.ds(PAD + y, 1))
-
-    def near_row(side, y):
-        z = 1 + side * (depth - 1)
-        here, down, up = (rows_of(v, z, pl.ds(PAD + y + d, 1)) for d in (0, -1, 1))
+        return rows_of(mu, z, at) * gain[0, z, at] + spread
+
+    collect(0, release, mu.shape, grad, own_row)
+
+
+def in_layer(c, here, up, down):
+    width = here.shape[-1]
+    value = c[0] * here + c[1] * up + c[2] * down
+    right = c[3] * here + c[4] * up + c[5] * down
+    left = c[6] * here + c[7] * up + c[8] * down
+    return value + pltpu.roll(right, width - 1, axis=1) + pltpu.roll(left, 1, axis=1)
+
+
+def front_kernel(
+    cells, steps, inside, grad_in, lam_a, lam_b, sent_a, sent_b, coef, edge, corr, gain, scale, grads, ve, total
+):
+    own, rows_y, rows_x = lam_a.shape
+    depth = coef.shape[1]
+    start = lax.axis_index("space") * (depth * rows_y * rows_x)
+    side_a = 1 - parity()
+    blank = jnp.zeros((PAD, rows_x), jnp.float32)
+    for k in range(own):
+        for side in range(2):
+            ve[side, k, pl.ds(0, PAD)] = blank
+            ve[side, k, pl.ds(PAD + rows_y, PAD)] = blank
+        ve[side_a, k, pl.ds(PAD, rows_y)] = sent_a[k]
+        ve[1 - side_a, k, pl.ds(PAD, rows_y)] = sent_b[k]
+    total[...] = grad_in[...]
+    take = taker(total, own, rows_x)
+
+    def visit(i, carry):
+        r = inside[i]
+        _, z, y, x = spot(cells[r], start, rows_y, rows_x)
+        step = steps[r]
         at = pl.ds(y, 1)
-        value = edge[side, 0, at] * here
-        value += edge[side, 1, pl.ds(jnp.maximum(y - 1, 0), 1)] * down
-        value += edge[side, 2, pl.ds(jnp.minimum(y + 1, rows_y - 1), 1)] * up
-        value += edge[side, 3, at] * pltpu.roll(here, 1, axis=1)
-        value += edge[side, 4, at] * pltpu.roll(here, rows_x - 1, axis=1)
-        return value
-
-    collect(0, release, mu.shape, total, own_row, near_row)
+        for lam, side in ((lam_a, side_a), (lam_b, 1 - side_a)):
+
+            @pl.when((step == 1) & (z == side * (depth - 1)))
+            def _(lam=lam):
+                take(r, x, rows_of(lam, at))
+
+        for side, names in ((0, LOW), (1, HIGH)):
+            out = 2 * side - 1
+            end = side * (depth - 1)
+
+            def near(side=side):
+                return [rows_of(ve.at[side], pl.ds(PAD + y + d, 1)) for d in (0, 1, -1)]
+
+            @pl.when((step == 0) & (z == end))
+            def _(side=side, end=end, near=near):
+                here, up, down = near()
+                value = in_layer([coef[j, end, at] for j in IN_LAYER], here, up, down)
+                keep = gain[0, end, at] / scale[0, end, at] + corr[0, side, at]
+                take(r, x, value + keep * here)
+
+            @pl.when((step == 0) & (z == end - out))
+            def _(end=end, out=out, names=names, near=near):
+                take(r, x, from_met([coef[j, end - out, at] for j in names], *near()))
+
+            @pl.when((step == 0) & (z == end + out))
+            def _(side=side, near=near):
+                here, up, down = near()
+                value = edge[side, 0, at] * here
+                value += edge[side, 1, pl.ds(jnp.maximum(y - 1, 0), 1)] * down
+                value += edge[side, 2, pl.ds(jnp.minimum(y + 1, rows_y - 1), 1)] * up
+                value += edge[side, 3, at] * pltpu.roll(here, 1, axis=1)
+                value += edge[side, 4, at] * pltpu.roll(here, rows_x - 1, axis=1)
+                take(r, x, value)
+
+        return carry
+
+    lax.fori_loop(0, inside[inside.shape[0] - 1], visit, 0)
     for i in range(grads.shape[0]):
         grads[i] = total[...]
 
@@ -601,49 +650,56 @@
     )(sensors, misfit, part_edges, got, sent, edge, corr, scale)
 
 
-def last_kernel(mu, v, coef, gain, got_a, got_b, edge, corr, grads, out, grad, part, sems):
-    own, depth, rows_y, rows_x = mu.shape
+def last_kernel(base, ve, coef, gain, scale, got_a, got_b, edge, corr, grads, out, grad, part, sems):
+    own, depth, rows_y, rows_x = base.shape
     tiles = rows_y // TILE
-    spread_field(coef, gain, 0, mu, v, part)
     copies = [
-        pltpu.make_async_copy(part.at[:, z], out.at[:, z], sems.at[z]) for z in range(depth)
+        pltpu.make_async_copy(base.at[:, z], out.at[:, z], sems.at[z]) for z in range(2, depth - 2)
     ]
-    for c in copies[1:-1]:
+    for c in copies:
         c.start()
+    side_a = 1 - parity()
+    for turn, (got, side) in enumerate(((got_b, 1 - side_a), (got_a, side_a))):
+        end = side * (depth - 1)
+        inner = end + 1 - 2 * side
+        for tile in range(tiles):
+            at = pl.ds(tile * TILE, TILE)
+            ce = [coef[j, end, at] for j in IN_LAYER]
+            ci = [coef[jnp.where(side == 0, low, high), inner, at] for low, high in zip(LOW, HIGH)]
+            cm = [edge[side, j, at] for j in range(5)]
+            keep = gain[0, end, at] / scale[0, end, at] + corr[0, side, at]
+            for k in range(own):
+                here, up, down = (
+                    ve[side, k, pl.ds(PAD + tile * TILE + d, TILE)] for d in (0, 1, -1)
+                )
+                value = base[k, end, at] + keep * here + in_layer(ce, here, up, down)
+                part[k, end, at] = value + from_met(cm, *met(got, k, tile, tiles))
+                part[k, inner, at] = base[k, inner, at] + from_met(ci, here, up, down)
+        for z, sem in ((end, turn), (inner, depth - 1 - turn)):
+            copies.append(pltpu.make_async_copy(part.at[:, z], out.at[:, z], sems.at[sem]))
+            copies[-1].start()
     total = grads[0]
     for i in range(1, grads.shape[0]):
         total += grads[i]
     grad[...] = total
-    side_a = 1 - parity()
-    for got, side in ((got_a, side_a), (got_b, 1 - side_a)):
-        z = side * (depth - 1)
-        for tile in range(tiles):
-            at = pl.ds(tile * TILE, TILE)
-            c = [edge[side, j, at] for j in range(5)]
-            miss = corr[0, side, at]
-            for k in range(own):
-                value = part[k, z, at] + miss * v[k, z + 1, pl.ds(PAD + tile * TILE, TILE)]
-                part[k, z, at] = value + from_met(c, *met(got, k, tile, tiles))
-    for c in (copies[0], copies[-1]):
-        c.start()
     for c in copies:
         c.wait()
 
 
-def last_call(mu, v, coef, gain, got_a, got_b, edge, corr, grads):
+def last_call(base, ve, coef, gain, scale, got_a, got_b, edge, corr, grads):
     return pl.pallas_call(
         last_kernel,
-        in_specs=[VMEM] * 9,
+        in_specs=[VMEM] * 10,
         out_specs=[ANY, VMEM],
-        out_shape=[f32(*mu.shape), f32(*grads.shape[1:])],
+        out_shape=[f32(*base.shape), f32(*grads.shape[1:])],
         scratch_shapes=[
-            pltpu.VMEM(mu.shape, jnp.float32),
-            pltpu.SemaphoreType.DMA((mu.shape[1],)),
+            pltpu.VMEM(base.shape, jnp.float32),
+            pltpu.SemaphoreType.DMA((base.shape[1],)),
         ],
         compiler_params=params(16),
-        cost_estimate=cost(40_000_000, 6_000_000),
+        cost_estimate=cost(10_000_000, 6_000_000),
         name="step0",
-    )(mu, v, coef, gain, got_a, got_b, edge, corr, grads)
+    )(base, ve, coef, gain, scale, got_a, got_b, edge, corr, grads)
 
 
 def turned(array, axis):
@@ -711,13 +767,13 @@
     got_b = swap_b(send_b)
     lam_a, send_a = rim(2, False, *sensors, part_edges, got_a, sent_a, edge_raw, corr, scale)
     got_a = swap_a(send_a)
-    part, part_edges, grad, inside = field_call(
-        functools.partial(middle_kernel, 1),
+    base, part_edges, grad, inside = field_call(
+        middle_kernel,
         "step1",
         (*sensors, *release, part, lam_a, lam_b, coef, gain, scale),
         [SMEM] * 4 + [VMEM] * 6,
         [field, edges, kept],
-        [tall, field],
+        [tall, field, field],
         40_000_000,
         release_cells.shape[0] + 1,
     )
@@ -726,18 +782,19 @@
     got_b = swap_b(send_b)
     lam_a, send_a = rim(1, False, *sensors, part_edges, got_a, sent_a, edge, corr, scale)
     got_a = swap_a(send_a)
-    grads, mu, v = field_call(
+    halo = f32(2, own, rows_y + 2 * PAD, rows_x)
+    grads, ve = field_call(
         front_kernel,
         "front0",
-        (*sensors, *release, inside, grad, part, lam_a, lam_b, coef, edge, corr, gain, scale),
-        [SMEM] * 5 + [VMEM] * 9,
-        [f32(slabs, *kept.shape), field, tall],
+        (*release, inside, grad, lam_a, lam_b, send_a, send_b, coef, edge, corr, gain, scale),
+        [SMEM] * 3 + [VMEM] * 10,
+        [f32(slabs, *kept.shape), halo],
         [kept],
         10_000_000,
     )
     grads = lax.all_to_all(grads, "space", 0, 0, tiled=True)
-    grads, mu, v = lax.optimization_barrier((grads, mu, v))
-    return tuple(last_call(mu, v, coef, gain, got_a, got_b, edge, corr, grads))
+    grads, ve = lax.optimization_barrier((grads, ve))
+    return tuple(last_call(base, ve, coef, gain, scale, got_a, got_b, edge, corr, grads))
 
 
 def solution(mesh):

time: 63.7 us -> 60.7 us (0.953)
  local copies, waits for them, and re-layouts: 2.74 us -> 0.05 us
    unnamed x22 -> x20, local copies, waits for them, and re-layouts: 2.74 us -> 0.05 us
    pallas_call x3, Pallas kernels: 9.49 us -> 10.7 us  [field_call(): pl.pallas_call(kernel, in_specs=specs, out_specs=[VMEM] * len(outs) + [SM...]
    pallas_call x1, Pallas kernels: 3.32 us -> 2.34 us  [last_call(): pl.pallas_call(last_kernel, in_specs=[VMEM] * 10, out_specs=[ANY, VMEM],...]
  transfers between devices with their start and end apart: 12 -> 12, of which waited for: 2 -> 2; matrix products, arithmetic and copies ran while one was open for 0% -> 0% of each run, Pallas kernels for 30% -> 33%
where the time goes in v3:
time: 60.7 us; the launch traced here: 60.6 us
  Pallas kernels  22.5 us (37%)
  starting transfers between devices  17.7 us (29%)
  blocking collectives  13 us (21%)
  waiting for transfers between devices  6.47 us (11%)
  between operations  0.89 us (1%)
    ppermute x4, starting transfers between devices, swap_a(): return lax.ppermute(x, 'space', pairs_a)  13.8 us
    all_to_all x1, blocking collectives, body(): grads = lax.all_to_all(grads, 'space', 0, 0, tiled=True)  13 us
    pallas_call x3, Pallas kernels, field_call(): pl.pallas_call(kernel, in_specs=specs, out_specs=[VMEM] * len(outs) + [SM...  10.7 us
    ppermute x4, waiting for transfers between devices, swap_a(): return lax.ppermute(x, 'space', pairs_a)  6.45 us
    pallas_call x4, Pallas kernels, rim(): pl.pallas_call(functools.partial(rim_kernel, step, late), in_specs=[SMEM]...  3.62 us
    pallas_call x1, Pallas kernels, pack(): pl.pallas_call(pack_kernel, in_specs=[SMEM] * 3 + [ANY] * 3, out_specs=[V...  2.86 us
    ppermute x4, starting transfers between devices, swap_b(): return lax.ppermute(x, 'space', pairs_b)  2.82 us
    pallas_call x1, Pallas kernels, last_call(): pl.pallas_call(last_kernel, in_specs=[VMEM] * 10, out_specs=[ANY, VMEM],...  2.34 us
  transfers between devices with their start and end apart: 12, of which 2 were waited for; matrix products, arithmetic and copies ran while one was open for 0% of the time, Pallas kernels for 33%

profile of v3, /device:TPU:0, one launch (start us, length us, event | category | flops | bytes accessed | tf_op | source)
XLA Modules:
  0.0 60.6 jit_solution(621358826620254777)
XLA Ops:
  0.6 0.5 collective-permute-start.2
  1.1 0.1 collective-permute-start.3
  1.2 2.9 %pack.1 = (f32[8,64,128]{2,1,0:T(8,128)}, f32[8,64,128]{2,1,0:T(8,128)}, f32[224,128]{1,0:T(8,128)}, f32[224,128]{1,0:T(8,128)}) custom-call(s32[3]{0:T(128)} %refs_0_.3, s32[8]{0:T(128)} %sensors.13, f32[3,8]{1,0:T(4,128)} %bitcast.1, f32[8,4,64,128]{3,2,1,0:T(8,128)} %lam.1, f32[4,4,64,128]{3,2,1,0:T(8,128)} %refs_3_, f32[6,4,32,128]{3,2,1,0:T(8,128)} %refs_1_), custom_call_target="tpu_custom_call" | custom-call | flops 20000000000 | bytes 60000000 | tf_op jit(solution)/shard_map/pack/pallas_call | solution.py:102
  4.1 3.0 %collective-permute-start = (f32[224,128]{1,0:T(8,128)}, f32[224,128]{1,0:T(8,128)S(1)}, u32[]{:S(2)}, u32[]{:S(2)}) collective-permute-start(f32[224,128]{1,0:T(8,128)} %get-tuple-element.46), channel_id=1, source_target_pairs={{0,2},{2,0},{4,6},{6,4},{8,10},{10,8},{12,14},{14,12},{16,18},{18,... | collective-permute-start | bytes 344072 | tf_op jit(solution)/shard_map/ppermute | solution.py:730
  7.1 0.7 %collective-permute-start.1 = (f32[224,128]{1,0:T(8,128)}, f32[224,128]{1,0:T(8,128)S(1)}, u32[]{:S(2)}, u32[]{:S(2)}) collective-permute-start(f32[224,128]{1,0:T(8,128)} %get-tuple-element.47), channel_id=1, source_target_pairs={{2,4},{4,2},{6,8},{8,6},{10,12},{12,10},{14,16},{16,14},{18,20},{2... | collective-permute-start | bytes 344072 | tf_op jit(solution)/shard_map/ppermute | solution.py:733
  7.8 0.0 collective-permute-done.3.refs_4_
  7.8 0.0 copy-start
  7.8 0.0 copy-start.3
  7.8 0.0 copy-start.4
  7.8 0.8 %collective-permute-start.7 = (f32[8,64,128]{2,1,0:T(8,128)}, f32[8,64,128]{2,1,0:T(8,128)S(1)}, u32[]{:S(2)}, u32[]{:S(2)}) collective-permute-start(f32[8,64,128]{2,1,0:T(8,128)} %get-tuple-element.73.sent), channel_id=1, source_target_pairs={{2,4},{4,2},{6,8},{8,6},{10,12},{12,10},{14,16},{16,14},{18,20},{2... | collective-permute-start | bytes 786440 | tf_op jit(solution)/shard_map/ppermute | solution.py:733
  8.6 5.5 %collective-permute-start.6 = (f32[8,64,128]{2,1,0:T(8,128)}, f32[8,64,128]{2,1,0:T(8,128)S(1)}, u32[]{:S(2)}, u32[]{:S(2)}) collective-permute-start(f32[8,64,128]{2,1,0:T(8,128)} %get-tuple-element.64.sent), channel_id=1, source_target_pairs={{0,2},{2,0},{4,6},{6,4},{8,10},{10,8},{12,14},{14,12},{16,18},{18,... | collective-permute-start | bytes 786440 | tf_op jit(solution)/shard_map/ppermute | solution.py:730
  14.2 0.5 collective-permute-start.5
  14.7 2.0 %planes.1 = (f32[19,4,64,128]{3,2,1,0:T(8,128)S(1)}, f32[3,4,64,128]{3,2,1,0:T(8,128)S(1)}, f32[3,4,64,128]{3,2,1,0:T(8,128)S(1)}, f32[3,2,64,128]{3,2,1,0:T(8,128)S(1)}) custom-call(s32[3]{0:T(128)S(1)} %copy-done.7, f32[6,4,32,128]{3,2,1,0:T(8,128)S(1)} %copy-done.9, f32[6,4,32,128]{3,2,1,0:T(8,128)S(1)} %collective-permute-done.2.refs_2_, ...), custom_call_target="tpu_custom_call" | custom-call | flops 2000000000 | bytes 60000000 | tf_op jit(solution)/shard_map/planes/pallas_call | solution.py:244
  16.8 2.4 %step2.1 = (f32[8,4,64,128]{3,2,1,0:T(8,128)S(1)}, f32[2,8,64,128]{3,2,1,0:T(8,128)S(1)}) custom-call(s32[8]{0:T(128)S(1)} %copy-done.4, f32[3,8]{1,0:T(4,128)S(1)} %bitcast.2, f32[8,4,64,128]{3,2,1,0:T(8,128)S(1)} %copy-done, f32[19,4,64,128]{3,2,1,0:T(8,128)S(1)} %get-tuple-element.56.coef.refs_1_, f32[3,4,64,128]{3,2,1,0:T(8,128)S(1)} %get-tuple-element.57.gain, ...), custom_call_target="tpu_custom_call" | custom-call | flops 40000000 | bytes 4000000 | tf_op jit(solution)/shard_map/step2/pallas_call | solution.py:580
  19.3 0.0 copy-start.1
  19.3 1.0 %ends.1 = (f32[2,5,64,128]{3,2,1,0:T(8,128)S(1)}, f32[2,5,64,128]{3,2,1,0:T(8,128)S(1)}, f32[3,2,64,128]{3,2,1,0:T(8,128)S(1)}) custom-call(s32[3]{0:T(128)S(1)} %copy-done.7, f32[19,4,64,128]{3,2,1,0:T(8,128)S(1)} %get-tuple-element.56.coef.refs_1_, f32[3,2,64,128]{3,2,1,0:T(8,128)S(1)} %get-tuple-element.65.refs_2_, ...), custom_call_target="tpu_custom_call" | custom-call | flops 1000000 | bytes 1000000 | tf_op jit(solution)/shard_map/ends/pallas_call | solution.py:340
  20.2 0.0 copy-start.5
  20.3 0.0 copy-start.6
  20.3 0.9 %rim2b.1 = (f32[8,64,128]{2,1,0:T(8,128)S(1)}, f32[8,64,128]{2,1,0:T(8,128)S(1)}) custom-call(s32[8]{0:T(128)S(1)} %copy-done.4, f32[3,8]{1,0:T(4,128)S(1)} %bitcast.3, f32[2,8,64,128]{3,2,1,0:T(8,128)S(1)} %get-tuple-element.63.part_edges, f32[8,64,128]{2,1,0:T(8,128)S(1)} %collective-permute-done.7.got, f32[8,64,128]{2,1,0:T(8,128)S(1)} %copy-done.2, ...), custom_call_target="tpu_custom_call" | custom-call | flops 2000000 | bytes 1500000 | tf_op jit(solution)/shard_map/rim2b/pallas_call | solution.py:642
  21.2 0.7 %collective-permute-start.9 = (f32[8,64,128]{2,1,0:T(8,128)S(1)}, f32[8,64,128]{2,1,0:T(8,128)S(1)}, u32[]{:S(2)}, u32[]{:S(2)}) collective-permute-start(f32[8,64,128]{2,1,0:T(8,128)S(1)} %get-tuple-element.82.sent), channel_id=1, source_target_pairs={{2,4},{4,2},{6,8},{8,6},{10,12},{12,10},{14,16},{16,14},{18,20},{2... | collective-permute-start | bytes 786440 | tf_op jit(solution)/shard_map/ppermute | solution.py:733
  21.9 4.3 %collective-permute-done.6.got = f32[8,64,128]{2,1,0:T(8,128)S(1)} collective-permute-done((f32[8,64,128]{2,1,0:T(8,128)}, f32[8,64,128]{2,1,0:T(8,128)S(1)}, u32[]{:S(2)}, u32[]{:S(2)}) %collective-permute-start.6) | collective-permute-done | bytes 262176 | tf_op jit(solution)/shard_map/ppermute | solution.py:730
  26.2 0.9 %rim2a.1 = (f32[8,64,128]{2,1,0:T(8,128)S(1)}, f32[8,64,128]{2,1,0:T(8,128)S(1)}) custom-call(s32[8]{0:T(128)S(1)} %copy-done.4, f32[3,8]{1,0:T(4,128)S(1)} %bitcast.4, f32[2,8,64,128]{3,2,1,0:T(8,128)S(1)} %get-tuple-element.63.part_edges, f32[8,64,128]{2,1,0:T(8,128)S(1)} %collective-permute-done.6.got, f32[8,64,128]{2,1,0:T(8,128)S(1)} %copy-done.1, ...), custom_call_target="tpu_custom_call" | custom-call | flops 2000000 | bytes 1500000 | tf_op jit(solution)/shard_map/rim2a/pallas_call | solution.py:642
  27.1 1.6 %collective-permute-start.8 = (f32[8,64,128]{2,1,0:T(8,128)S(1)}, f32[8,64,128]{2,1,0:T(8,128)S(1)}, u32[]{:S(2)}, u32[]{:S(2)}) collective-permute-start(f32[8,64,128]{2,1,0:T(8,128)S(1)} %get-tuple-element.79.sent), channel_id=1, source_target_pairs={{0,2},{2,0},{4,6},{6,4},{8,10},{10,8},{12,14},{14,12},{16,18},{18,... | collective-permute-start | bytes 786440 | tf_op jit(solution)/shard_map/ppermute | solution.py:730
  28.7 6.9 %step1.1 = (f32[8,4,64,128]{3,2,1,0:T(8,128)S(1)}, f32[2,8,64,128]{3,2,1,0:T(8,128)S(1)}, f32[8,128]{1,0:T(8,128)S(1)}, s32[129]{0:T(256)S(1)}) custom-call(s32[8]{0:T(128)S(1)} %copy-done.4, f32[3,8]{1,0:T(4,128)S(1)} %bitcast.5, s32[128]{0:T(128)S(1)} %copy-done.5, s32[128]{0:T(128)S(1)} %copy-done.6, f32[8,4,64,128]{3,2,1,0:T(8,128)S(1)} %get-tuple-element.59.lam, ...), custom_call_target="tpu_custom_call" | custom-call | flops 40000000 | bytes 4000000 | tf_op jit(solution)/shard_map/step1/pallas_call | solution.py:580
  35.6 0.9 %rim1b.1 = (f32[8,64,128]{2,1,0:T(8,128)S(1)}, f32[8,64,128]{2,1,0:T(8,128)S(1)}) custom-call(s32[8]{0:T(128)S(1)} %copy-done.4, f32[3,8]{1,0:T(4,128)S(1)} %bitcast.6, f32[2,8,64,128]{3,2,1,0:T(8,128)S(1)} %get-tuple-element.78.part_edges, f32[8,64,128]{2,1,0:T(8,128)S(1)} %collective-permute-done.9.got, f32[8,64,128]{2,1,0:T(8,128)S(1)} %get-tuple-element.82.sent, ...), custom_call_target="tpu_custom_call" | custom-call | flops 2000000 | bytes 1500000 | tf_op jit(solution)/shard_map/rim1b/pallas_call | solution.py:642
  36.5 0.7 %collective-permute-start.11 = (f32[8,64,128]{2,1,0:T(8,128)S(1)}, f32[8,64,128]{2,1,0:T(8,128)S(1)}, u32[]{:S(2)}, u32[]{:S(2)}) collective-permute-start(f32[8,64,128]{2,1,0:T(8,128)S(1)} %get-tuple-element.85.sent_b), channel_id=1, source_target_pairs={{2,4},{4,2},{6,8},{8,6},{10,12},{12,10},{14,16},{16,14},{18,20},{2... | collective-permute-start | bytes 786440 | tf_op jit(solution)/shard_map/ppermute | solution.py:733
  37.2 2.1 %collective-permute-done.8.got = f32[8,64,128]{2,1,0:T(8,128)S(1)} collective-permute-done((f32[8,64,128]{2,1,0:T(8,128)S(1)}, f32[8,64,128]{2,1,0:T(8,128)S(1)}, u32[]{:S(2)}, u32[]{:S(2)}) %collective-permute-start.8) | collective-permute-done | bytes 262176 | tf_op jit(solution)/shard_map/ppermute | solution.py:730
  39.3 0.9 %rim1a.1 = (f32[8,64,128]{2,1,0:T(8,128)S(1)}, f32[8,64,128]{2,1,0:T(8,128)S(1)}) custom-call(s32[8]{0:T(128)S(1)} %copy-done.4, f32[3,8]{1,0:T(4,128)S(1)} %bitcast.7, f32[2,8,64,128]{3,2,1,0:T(8,128)S(1)} %get-tuple-element.78.part_edges, f32[8,64,128]{2,1,0:T(8,128)S(1)} %collective-permute-done.8.got, f32[8,64,128]{2,1,0:T(8,128)S(1)} %get-tuple-element.79.sent, ...), custom_call_target="tpu_custom_call" | custom-call | flops 2000000 | bytes 1500000 | tf_op jit(solution)/shard_map/rim1a/pallas_call | solution.py:642
  40.2 3.7 %collective-permute-start.10 = (f32[8,64,128]{2,1,0:T(8,128)S(1)}, f32[8,64,128]{2,1,0:T(8,128)S(1)}, u32[]{:S(2)}, u32[]{:S(2)}) collective-permute-start(f32[8,64,128]{2,1,0:T(8,128)S(1)} %get-tuple-element.84.sent_a), channel_id=1, source_target_pairs={{0,2},{2,0},{4,6},{6,4},{8,10},{10,8},{12,14},{14,12},{16,18},{18,... | collective-permute-start | bytes 786440 | tf_op jit(solution)/shard_map/ppermute | solution.py:730
  43.9 1.3 %front0.1 = (f32[16,8,128]{2,1,0:T(8,128)S(1)}, f32[2,8,80,128]{3,2,1,0:T(8,128)S(1)}) custom-call(s32[128]{0:T(128)S(1)} %copy-done.5, s32[128]{0:T(128)S(1)} %copy-done.6, s32[129]{0:T(256)S(1)} %get-tuple-element.76.inside, f32[8,128]{1,0:T(8,128)S(1)} %get-tuple-element.77.grad_in, f32[8,64,128]{2,1,0:T(8,128)S(1)} %get-tuple-element.81.lam_a, ...), custom_call_target="tpu_custom_call" | custom-call | flops 10000000 | bytes 4000000 | tf_op jit(solution)/shard_map/front0/pallas_call | solution.py:580
  45.3 13.0 %all_to_all.5.grads = f32[16,8,128]{2,1,0:T(8,128)S(1)} all-to-all(f32[16,8,128]{2,1,0:T(8,128)S(1)} %get-tuple-element.86), channel_id=1, replica_groups=mesh['space'=16,'sens'=2] {'space'}, dimensions={0} | all-to-all | bytes 131072 | tf_op jit(solution)/shard_map/all_to_all | solution.py:795
  58.3 2.3 %step0.1 = (f32[8,4,64,128]{3,2,1,0:T(8,128)}, f32[8,128]{1,0:T(8,128)}) custom-call(f32[8,4,64,128]{3,2,1,0:T(8,128)S(1)} %get-tuple-element.75.base, f32[2,8,80,128]{3,2,1,0:T(8,128)S(1)} %get-tuple-element.88.ve, f32[19,4,64,128]{3,2,1,0:T(8,128)S(1)} %get-tuple-element.56.coef.refs_1_, f32[3,4,64,128]{3,2,1,0:T(8,128)S(1)} %get-tuple-element.57.gain, ...), custom_call_target="tpu_custom_call" | custom-call | flops 10000000 | bytes 6000000 | tf_op jit(solution)/shard_map/step0/pallas_call | solution.py:690
  (24 shorter events, 0.1 us)
Async XLA Ops:
  0.6 7.1 %collective-permute-start.2 = (f32[6,4,32,128]{3,2,1,0:T(8,128)}, f32[6,4,32,128]{3,2,1,0:T(8,128)S(1)}, u32[]{:S(2)}, u32[]{:S(2)}) collective-permute-start(f32[6,4,32,128]{3,2,1,0:T(8,128)} %refs_1_), channel_id=1, source_target_pairs={{0,1},{1,0},{2,3},{3,2},{4,5},{5,4},{6,7},{7,6},{8,9},{9,8},{10,11... | collective-permute-start | bytes 1179656 | tf_op jit(solution)/shard_map/ppermute | solution.py:708
  1.1 6.6 %collective-permute-start.3 = (f32[4,4,64,128]{3,2,1,0:T(8,128)}, f32[4,4,64,128]{3,2,1,0:T(8,128)S(1)}, u32[]{:S(2)}, u32[]{:S(2)}) collective-permute-start(f32[4,4,64,128]{3,2,1,0:T(8,128)} %refs_3_), channel_id=1, source_target_pairs={{0,1},{1,0},{2,3},{3,2},{4,5},{5,4},{6,7},{7,6},{8,9},{9,8},{10,11... | collective-permute-start | bytes 1572872 | tf_op jit(solution)/shard_map/ppermute | solution.py:708
  1.2 13.5 %copy-start.7 = (s32[3]{0:T(128)S(1)}, s32[3]{0:T(128)}, u32[]{:S(2)}) copy-start(s32[3]{0:T(128)} %refs_0_.3) | copy-start | bytes 40
  1.2 13.5 %copy-start.8 = (f32[4,4,64,128]{3,2,1,0:T(8,128)S(1)}, f32[4,4,64,128]{3,2,1,0:T(8,128)}, u32[]{:S(2)}) copy-start(f32[4,4,64,128]{3,2,1,0:T(8,128)} %refs_3_) | copy-start | bytes 1572868
  1.2 13.5 %copy-start.9 = (f32[6,4,32,128]{3,2,1,0:T(8,128)S(1)}, f32[6,4,32,128]{3,2,1,0:T(8,128)}, u32[]{:S(2)}) copy-start(f32[6,4,32,128]{3,2,1,0:T(8,128)} %refs_1_) | copy-start | bytes 1179652
  4.1 10.1 %collective-permute-start = (f32[224,128]{1,0:T(8,128)}, f32[224,128]{1,0:T(8,128)S(1)}, u32[]{:S(2)}, u32[]{:S(2)}) collective-permute-start(f32[224,128]{1,0:T(8,128)} %get-tuple-element.46), channel_id=1, source_target_pairs={{0,2},{2,0},{4,6},{6,4},{8,10},{10,8},{12,14},{14,12},{16,18},{18,... | collective-permute-start | bytes 344072 | tf_op jit(solution)/shard_map/ppermute | solution.py:730
  7.1 7.1 %collective-permute-start.1 = (f32[224,128]{1,0:T(8,128)}, f32[224,128]{1,0:T(8,128)S(1)}, u32[]{:S(2)}, u32[]{:S(2)}) collective-permute-start(f32[224,128]{1,0:T(8,128)} %get-tuple-element.47), channel_id=1, source_target_pairs={{2,4},{4,2},{6,8},{8,6},{10,12},{12,10},{14,16},{16,14},{18,20},{2... | collective-permute-start | bytes 344072 | tf_op jit(solution)/shard_map/ppermute | solution.py:733
  7.8 9.0 %copy-start = (f32[8,4,64,128]{3,2,1,0:T(8,128)S(1)}, f32[8,4,64,128]{3,2,1,0:T(8,128)}, u32[]{:S(2)}) copy-start(f32[8,4,64,128]{3,2,1,0:T(8,128)} %lam.1) | copy-start | bytes 3145732
  7.8 9.0 %copy-start.3 = (f32[8,3]{0,1:T(4,128)S(1)}, f32[8,3]{0,1:T(4,128)}, u32[]{:S(2)}) copy-start(f32[8,3]{0,1:T(4,128)} %param.13) | copy-start | bytes 292
  7.8 9.0 %copy-start.4 = (s32[8]{0:T(128)S(1)}, s32[8]{0:T(128)}, u32[]{:S(2)}) copy-start(s32[8]{0:T(128)} %sensors.13) | copy-start | bytes 100
  7.8 12.5 %collective-permute-start.7 = (f32[8,64,128]{2,1,0:T(8,128)}, f32[8,64,128]{2,1,0:T(8,128)S(1)}, u32[]{:S(2)}, u32[]{:S(2)}) collective-permute-start(f32[8,64,128]{2,1,0:T(8,128)} %get-tuple-element.73.sent), channel_id=1, source_target_pairs={{2,4},{4,2},{6,8},{8,6},{10,12},{12,10},{14,16},{16,14},{18,20},{2... | collective-permute-start | bytes 786440 | tf_op jit(solution)/shard_map/ppermute | solution.py:733
  8.6 17.6 %collective-permute-start.6 = (f32[8,64,128]{2,1,0:T(8,128)}, f32[8,64,128]{2,1,0:T(8,128)S(1)}, u32[]{:S(2)}, u32[]{:S(2)}) collective-permute-start(f32[8,64,128]{2,1,0:T(8,128)} %get-tuple-element.64.sent), channel_id=1, source_target_pairs={{0,2},{2,0},{4,6},{6,4},{8,10},{10,8},{12,14},{14,12},{16,18},{18,... | collective-permute-start | bytes 786440 | tf_op jit(solution)/shard_map/ppermute | solution.py:730
  14.2 5.1 %collective-permute-start.4 = (f32[224,128]{1,0:T(8,128)S(1)}, f32[224,128]{1,0:T(8,128)S(1)}, u32[]{:S(2)}, u32[]{:S(2)}) collective-permute-start(f32[224,128]{1,0:T(8,128)S(1)} %collective-permute-done.refs_3_), channel_id=1, source_target_pairs={{0,1},{1,0},{2,3},{3,2},{4,5},{5,4},{6,7},{7,6},{8,9},{9,8},{10,11... | collective-permute-start | bytes 344072 | tf_op jit(solution)/shard_map/ppermute | solution.py:708
  14.2 5.1 %collective-permute-start.5 = (f32[224,128]{1,0:T(8,128)S(1)}, f32[224,128]{1,0:T(8,128)S(1)}, u32[]{:S(2)}, u32[]{:S(2)}) collective-permute-start(f32[224,128]{1,0:T(8,128)S(1)} %collective-permute-done.1.refs_5_), channel_id=1, source_target_pairs={{0,1},{1,0},{2,3},{3,2},{4,5},{5,4},{6,7},{7,6},{8,9},{9,8},{10,11... | collective-permute-start | bytes 344072 | tf_op jit(solution)/shard_map/ppermute | solution.py:708
  19.2 1.1 %copy-start.2 = (f32[8,64,128]{2,1,0:T(8,128)S(1)}, f32[8,64,128]{2,1,0:T(8,128)}, u32[]{:S(2)}) copy-start(f32[8,64,128]{2,1,0:T(8,128)} %get-tuple-element.73.sent) | copy-start | bytes 786436
  19.3 7.0 %copy-start.1 = (f32[8,64,128]{2,1,0:T(8,128)S(1)}, f32[8,64,128]{2,1,0:T(8,128)}, u32[]{:S(2)}) copy-start(f32[8,64,128]{2,1,0:T(8,128)} %get-tuple-element.64.sent) | copy-start | bytes 786436
  20.2 8.5 %copy-start.5 = (s32[128]{0:T(128)S(1)}, s32[128]{0:T(128)}, u32[]{:S(2)}) copy-start(s32[128]{0:T(128)} %cells.3) | copy-start | bytes 1540
  20.3 8.5 %copy-start.6 = (s32[128]{0:T(128)S(1)}, s32[128]{0:T(128)}, u32[]{:S(2)}) copy-start(s32[128]{0:T(128)} %steps.3) | copy-start | bytes 1540
  21.2 14.4 %collective-permute-start.9 = (f32[8,64,128]{2,1,0:T(8,128)S(1)}, f32[8,64,128]{2,1,0:T(8,128)S(1)}, u32[]{:S(2)}, u32[]{:S(2)}) collective-permute-start(f32[8,64,128]{2,1,0:T(8,128)S(1)} %get-tuple-element.82.sent), channel_id=1, source_target_pairs={{2,4},{4,2},{6,8},{8,6},{10,12},{12,10},{14,16},{16,14},{18,20},{2... | collective-permute-start | bytes 786440 | tf_op jit(solution)/shard_map/ppermute | solution.py:733
  27.1 12.2 %collective-permute-start.8 = (f32[8,64,128]{2,1,0:T(8,128)S(1)}, f32[8,64,128]{2,1,0:T(8,128)S(1)}, u32[]{:S(2)}, u32[]{:S(2)}) collective-permute-start(f32[8,64,128]{2,1,0:T(8,128)S(1)} %get-tuple-element.79.sent), channel_id=1, source_target_pairs={{0,2},{2,0},{4,6},{6,4},{8,10},{10,8},{12,14},{14,12},{16,18},{18,... | collective-permute-start | bytes 786440 | tf_op jit(solution)/shard_map/ppermute | solution.py:730
  36.5 21.8 %collective-permute-start.11 = (f32[8,64,128]{2,1,0:T(8,128)S(1)}, f32[8,64,128]{2,1,0:T(8,128)S(1)}, u32[]{:S(2)}, u32[]{:S(2)}) collective-permute-start(f32[8,64,128]{2,1,0:T(8,128)S(1)} %get-tuple-element.85.sent_b), channel_id=1, source_target_pairs={{2,4},{4,2},{6,8},{8,6},{10,12},{12,10},{14,16},{16,14},{18,20},{2... | collective-permute-start | bytes 786440 | tf_op jit(solution)/shard_map/ppermute | solution.py:733
  40.2 18.0 %collective-permute-start.10 = (f32[8,64,128]{2,1,0:T(8,128)S(1)}, f32[8,64,128]{2,1,0:T(8,128)S(1)}, u32[]{:S(2)}, u32[]{:S(2)}) collective-permute-start(f32[8,64,128]{2,1,0:T(8,128)S(1)} %get-tuple-element.84.sent_a), channel_id=1, source_target_pairs={{0,2},{2,0},{4,6},{6,4},{8,10},{10,8},{12,14},{14,12},{16,18},{18,... | collective-permute-start | bytes 786440 | tf_op jit(solution)/shard_map/ppermute | solution.py:730

commit v4 on v3

--- a/solution.py
+++ b/solution.py
@@ -16,6 +16,21 @@
 PLANES = 19
 LOW = (ZM, ZMYP, ZMYM, XPZM, XMZM)
 HIGH = (ZP, ZPYP, ZPYM, XPZP, XMZP)
+GROUPS = (
+    (
+        (CENTRE, 0, 0),
+        (ZP, 1, 0),
+        (ZM, -1, 0),
+        (YP, 0, 1),
+        (YM, 0, -1),
+        (ZPYP, 1, 1),
+        (ZPYM, 1, -1),
+        (ZMYP, -1, 1),
+        (ZMYM, -1, -1),
+    ),
+    ((XP, 0, 0), (XPZP, 1, 0), (XPZM, -1, 0), (XPYP, 0, 1), (XPYM, 0, -1)),
+    ((XM, 0, 0), (XMZP, 1, 0), (XMZM, -1, 0), (XMYP, 0, 1), (XMYM, 0, -1)),
+)
 IN_LAYER = (CENTRE, YP, YM, XP, XPYP, XPYM, XM, XMYP, XMYM)
 
 VMEM = pl.BlockSpec(memory_space=pltpu.VMEM)
@@ -152,16 +167,17 @@
     return c
 
 
-def stencil(c, u):
-    near = {(dz, dy): u(dz, dy) for dz in (-1, 0, 1) for dy in (-1, 0, 1)}
-    here = c[CENTRE] * near[0, 0] + c[ZP] * near[1, 0] + c[ZM] * near[-1, 0]
-    here += c[YP] * near[0, 1] + c[YM] * near[0, -1]
-    here += c[ZPYP] * near[1, 1] + c[ZPYM] * near[1, -1]
-    here += c[ZMYP] * near[-1, 1] + c[ZMYM] * near[-1, -1]
-    right = c[XP] * near[0, 0] + c[XPZP] * near[1, 0] + c[XPZM] * near[-1, 0]
-    right += c[XPYP] * near[0, 1] + c[XPYM] * near[0, -1]
-    left = c[XM] * near[0, 0] + c[XMZP] * near[1, 0] + c[XMZM] * near[-1, 0]
-    left += c[XMYP] * near[0, 1] + c[XMYM] * near[0, -1]
+def stencil(c, u, reach=(-1, 0, 1)):
+    near = {(dz, dy): u(dz, dy) for dz in reach for dy in (-1, 0, 1)}
+    sums = []
+    for group in GROUPS:
+        value = None
+        for j, dz, dy in group:
+            if dz in reach:
+                term = c[j] * near[dz, dy]
+                value = term if value is None else value + term
+        sums.append(value)
+    here, right, left = sums
     width = here.shape[-1]
     return here + pltpu.roll(right, width - 1, axis=1) + pltpu.roll(left, 1, axis=1)
 
@@ -395,22 +411,22 @@
             v[k, z + 1, pl.ds(PAD, rows_y)] = scale[step, z] * mu[k, z]
 
 
-def spread_field(coef, gain, step, mu, v, part, part_edges=None):
+def spread_field(coef, gain, step, mu, v, part, part_edges=None, skip=0):
     own, depth, rows_y, rows_x = mu.shape
-
-    def layer(z, carry):
+    for z in range(depth):
+        reach = [dz for dz in (-1, 0, 1) if skip <= z + dz < depth - skip]
+        used = {j for group in GROUPS for j, dz, _ in group if dz in reach}
         for tile in range(rows_y // TILE):
             at = pl.ds(tile * TILE, TILE)
-            c = [coef[j, z, at] for j in range(PLANES)]
+            c = {j: coef[j, z, at] for j in sorted(used)}
             keep = gain[step, z, at]
             for k in range(own):
-                spread = stencil(
-                    c, lambda dz, dy: v[k, z + 1 + dz, pl.ds(PAD + tile * TILE + dy, TILE)]
+                value = stencil(
+                    c, lambda dz, dy: v[k, z + 1 + dz, pl.ds(PAD + tile * TILE + dy, TILE)], reach
                 )
-                part[k, z, at] = mu[k, z, at] * keep + spread
-        return carry
-
-    lax.fori_loop(0, depth, layer, 0)
+                if 0 in reach:
+                    value += mu[k, z, at] * keep
+                part[k, z, at] = value
     if part_edges is not None:
         for k in range(own):
             part_edges[0, k] = part[k, 0]
@@ -494,7 +510,7 @@
     collect(1, release, mu.shape, grad, lambda z, y: rows_of(mu, z, pl.ds(y, 1)))
     add_misfit(0, sensors, misfit, mu, 1)
     scale_field(scale, 0, mu, v)
-    spread_field(coef, gain, 0, mu, v, base)
+    spread_field(coef, gain, 0, mu, v, base, skip=1)
 
     def own_row(z, y):
         at = pl.ds(y, 1)
@@ -626,14 +642,14 @@
             lam[k, at] = value
             send[k, at] = gain * value
     plane = rows_y * rows_x
-    start = lax.axis_index("space") * (depth * plane)
+    first = (lax.axis_index("space") * depth + z) * plane
     lanes = lax.broadcasted_iota(jnp.int32, (1, rows_x), 1)
     for k in range(own):
-        lifted, at_z, y, x = spot(sensors[k], start, rows_y, rows_x)
-        here = (lifted >= plane) & (lifted < (depth + 1) * plane)
-
-        @pl.when(here & (at_z == z))
-        def _(k=k, y=y, x=x):
+        local = sensors[k] - first
+
+        @pl.when((local >= 0) & (local < plane))
+        def _(k=k, local=local):
+            y, x = lax.div(local, rows_x), lax.rem(local, rows_x)
             add = jnp.where(lanes == x, misfit[step - 1, k], 0.0)
             send[k, pl.ds(y, 1), :] += add * scale[step - 1, z, pl.ds(y, 1), :]
 

time: 60.7 us -> 60.1 us (level)
  starting transfers between devices: 17.7 us -> 16 us
  blocking collectives: 13 us -> 14 us
  waiting for transfers between devices: 6.47 us -> 7.1 us
    ppermute x4, starting transfers between devices: 13.8 us -> 12.1 us  [swap_a(): return lax.ppermute(x, 'space', pairs_a)]
    all_to_all x1, blocking collectives: 13 us -> 14 us  [body(): grads = lax.all_to_all(grads, 'space', 0, 0, tiled=True)]
    ppermute x4, waiting for transfers between devices: 6.45 us -> 7.08 us  [swap_a(): return lax.ppermute(x, 'space', pairs_a)]
where the time goes in v4:
time: 60.1 us
  Pallas kernels  22 us (37%)
  starting transfers between devices  16 us (27%)
  blocking collectives  14 us (23%)
  waiting for transfers between devices  7.1 us (12%)
  between operations  0.88 us (1%)
    all_to_all x1, blocking collectives, body(): grads = lax.all_to_all(grads, 'space', 0, 0, tiled=True)  14 us
    ppermute x4, starting transfers between devices, swap_a(): return lax.ppermute(x, 'space', pairs_a)  12.1 us
    pallas_call x3, Pallas kernels, field_call(): pl.pallas_call(kernel, in_specs=specs, out_specs=[VMEM] * len(outs) + [SM...  10.3 us
    ppermute x4, waiting for transfers between devices, swap_a(): return lax.ppermute(x, 'space', pairs_a)  7.08 us
    pallas_call x4, Pallas kernels, rim(): pl.pallas_call(functools.partial(rim_kernel, step, late), in_specs=[SMEM]...  3.43 us
    pallas_call x1, Pallas kernels, pack(): pl.pallas_call(pack_kernel, in_specs=[SMEM] * 3 + [ANY] * 3, out_specs=[V...  2.86 us
    ppermute x4, starting transfers between devices, swap_b(): return lax.ppermute(x, 'space', pairs_b)  2.82 us
    pallas_call x1, Pallas kernels, last_call(): pl.pallas_call(last_kernel, in_specs=[VMEM] * 10, out_specs=[ANY, VMEM],...  2.34 us
  transfers between devices with their start and end apart: 12, of which 2 were waited for; matrix products, arithmetic and copies ran while one was open for 0% of the time, Pallas kernels for 33%

profile of v4, /device:TPU:0, one launch (start us, length us, event | category | flops | bytes accessed | tf_op | source)
XLA Modules:
  0.0 60.1 jit_solution(3097411093223039748)
XLA Ops:
  0.6 0.5 collective-permute-start.2
  1.1 0.1 collective-permute-start.3
  1.2 2.9 %pack.1 = (f32[8,64,128]{2,1,0:T(8,128)}, f32[8,64,128]{2,1,0:T(8,128)}, f32[224,128]{1,0:T(8,128)}, f32[224,128]{1,0:T(8,128)}) custom-call(s32[3]{0:T(128)} %refs_0_.3, s32[8]{0:T(128)} %sensors.13, f32[3,8]{1,0:T(4,128)} %bitcast.1, f32[8,4,64,128]{3,2,1,0:T(8,128)} %lam.1, f32[4,4,64,128]{3,2,1,0:T(8,128)} %refs_3_, f32[6,4,32,128]{3,2,1,0:T(8,128)} %refs_1_), custom_call_target="tpu_custom_call" | custom-call | flops 20000000000 | bytes 60000000 | tf_op jit(solution)/shard_map/pack/pallas_call | solution.py:117
  4.1 3.0 %collective-permute-start = (f32[224,128]{1,0:T(8,128)}, f32[224,128]{1,0:T(8,128)S(1)}, u32[]{:S(2)}, u32[]{:S(2)}) collective-permute-start(f32[224,128]{1,0:T(8,128)} %get-tuple-element.46), channel_id=1, source_target_pairs={{0,2},{2,0},{4,6},{6,4},{8,10},{10,8},{12,14},{14,12},{16,18},{18,... | collective-permute-start | bytes 344072 | tf_op jit(solution)/shard_map/ppermute | solution.py:746
  7.1 0.7 %collective-permute-start.1 = (f32[224,128]{1,0:T(8,128)}, f32[224,128]{1,0:T(8,128)S(1)}, u32[]{:S(2)}, u32[]{:S(2)}) collective-permute-start(f32[224,128]{1,0:T(8,128)} %get-tuple-element.47), channel_id=1, source_target_pairs={{2,4},{4,2},{6,8},{8,6},{10,12},{12,10},{14,16},{16,14},{18,20},{2... | collective-permute-start | bytes 344072 | tf_op jit(solution)/shard_map/ppermute | solution.py:749
  7.8 0.0 collective-permute-done.2.refs_2_
  7.8 0.0 copy-start
  7.8 0.0 copy-start.3
  7.8 0.0 copy-start.4
  7.8 0.8 %collective-permute-start.7 = (f32[8,64,128]{2,1,0:T(8,128)}, f32[8,64,128]{2,1,0:T(8,128)S(1)}, u32[]{:S(2)}, u32[]{:S(2)}) collective-permute-start(f32[8,64,128]{2,1,0:T(8,128)} %get-tuple-element.73.sent), channel_id=1, source_target_pairs={{2,4},{4,2},{6,8},{8,6},{10,12},{12,10},{14,16},{16,14},{18,20},{2... | collective-permute-start | bytes 786440 | tf_op jit(solution)/shard_map/ppermute | solution.py:749
  8.6 5.5 %collective-permute-start.6 = (f32[8,64,128]{2,1,0:T(8,128)}, f32[8,64,128]{2,1,0:T(8,128)S(1)}, u32[]{:S(2)}, u32[]{:S(2)}) collective-permute-start(f32[8,64,128]{2,1,0:T(8,128)} %get-tuple-element.64.sent), channel_id=1, source_target_pairs={{0,2},{2,0},{4,6},{6,4},{8,10},{10,8},{12,14},{14,12},{16,18},{18,... | collective-permute-start | bytes 786440 | tf_op jit(solution)/shard_map/ppermute | solution.py:746
  14.2 0.5 collective-permute-start.5
  14.7 2.1 %planes.1 = (f32[19,4,64,128]{3,2,1,0:T(8,128)S(1)}, f32[3,4,64,128]{3,2,1,0:T(8,128)S(1)}, f32[3,4,64,128]{3,2,1,0:T(8,128)S(1)}, f32[3,2,64,128]{3,2,1,0:T(8,128)S(1)}) custom-call(s32[3]{0:T(128)S(1)} %copy-done.7, f32[6,4,32,128]{3,2,1,0:T(8,128)S(1)} %copy-done.9, f32[6,4,32,128]{3,2,1,0:T(8,128)S(1)} %collective-permute-done.2.refs_2_, ...), custom_call_target="tpu_custom_call" | custom-call | flops 2000000000 | bytes 60000000 | tf_op jit(solution)/shard_map/planes/pallas_call | solution.py:260
  16.8 2.2 %step2.1 = (f32[8,4,64,128]{3,2,1,0:T(8,128)S(1)}, f32[2,8,64,128]{3,2,1,0:T(8,128)S(1)}) custom-call(s32[8]{0:T(128)S(1)} %copy-done.4, f32[3,8]{1,0:T(4,128)S(1)} %bitcast.2, f32[8,4,64,128]{3,2,1,0:T(8,128)S(1)} %copy-done, f32[19,4,64,128]{3,2,1,0:T(8,128)S(1)} %get-tuple-element.56.coef.refs_1_, f32[3,4,64,128]{3,2,1,0:T(8,128)S(1)} %get-tuple-element.57.gain, ...), custom_call_target="tpu_custom_call" | custom-call | flops 40000000 | bytes 4000000 | tf_op jit(solution)/shard_map/step2/pallas_call | solution.py:596
  19.0 0.0 copy-start.1
  19.0 1.0 %ends.1 = (f32[2,5,64,128]{3,2,1,0:T(8,128)S(1)}, f32[2,5,64,128]{3,2,1,0:T(8,128)S(1)}, f32[3,2,64,128]{3,2,1,0:T(8,128)S(1)}) custom-call(s32[3]{0:T(128)S(1)} %copy-done.7, f32[19,4,64,128]{3,2,1,0:T(8,128)S(1)} %get-tuple-element.56.coef.refs_1_, f32[3,2,64,128]{3,2,1,0:T(8,128)S(1)} %get-tuple-element.65.refs_2_, ...), custom_call_target="tpu_custom_call" | custom-call | flops 1000000 | bytes 1000000 | tf_op jit(solution)/shard_map/ends/pallas_call | solution.py:356
  20.0 0.0 copy-start.5
  20.0 0.0 copy-start.6
  20.1 0.9 %rim2b.1 = (f32[8,64,128]{2,1,0:T(8,128)S(1)}, f32[8,64,128]{2,1,0:T(8,128)S(1)}) custom-call(s32[8]{0:T(128)S(1)} %copy-done.4, f32[3,8]{1,0:T(4,128)S(1)} %bitcast.3, f32[2,8,64,128]{3,2,1,0:T(8,128)S(1)} %get-tuple-element.63.part_edges, f32[8,64,128]{2,1,0:T(8,128)S(1)} %collective-permute-done.7.got, f32[8,64,128]{2,1,0:T(8,128)S(1)} %copy-done.2, ...), custom_call_target="tpu_custom_call" | custom-call | flops 2000000 | bytes 1500000 | tf_op jit(solution)/shard_map/rim2b/pallas_call | solution.py:658
  20.9 0.7 %collective-permute-start.9 = (f32[8,64,128]{2,1,0:T(8,128)S(1)}, f32[8,64,128]{2,1,0:T(8,128)S(1)}, u32[]{:S(2)}, u32[]{:S(2)}) collective-permute-start(f32[8,64,128]{2,1,0:T(8,128)S(1)} %get-tuple-element.82.sent), channel_id=1, source_target_pairs={{2,4},{4,2},{6,8},{8,6},{10,12},{12,10},{14,16},{16,14},{18,20},{2... | collective-permute-start | bytes 786440 | tf_op jit(solution)/shard_map/ppermute | solution.py:749
  21.6 4.6 %collective-permute-done.6.got = f32[8,64,128]{2,1,0:T(8,128)S(1)} collective-permute-done((f32[8,64,128]{2,1,0:T(8,128)}, f32[8,64,128]{2,1,0:T(8,128)S(1)}, u32[]{:S(2)}, u32[]{:S(2)}) %collective-permute-start.6) | collective-permute-done | bytes 262176 | tf_op jit(solution)/shard_map/ppermute | solution.py:746
  26.2 0.9 %rim2a.1 = (f32[8,64,128]{2,1,0:T(8,128)S(1)}, f32[8,64,128]{2,1,0:T(8,128)S(1)}) custom-call(s32[8]{0:T(128)S(1)} %copy-done.4, f32[3,8]{1,0:T(4,128)S(1)} %bitcast.4, f32[2,8,64,128]{3,2,1,0:T(8,128)S(1)} %get-tuple-element.63.part_edges, f32[8,64,128]{2,1,0:T(8,128)S(1)} %collective-permute-done.6.got, f32[8,64,128]{2,1,0:T(8,128)S(1)} %copy-done.1, ...), custom_call_target="tpu_custom_call" | custom-call | flops 2000000 | bytes 1500000 | tf_op jit(solution)/shard_map/rim2a/pallas_call | solution.py:658
  27.1 1.6 %collective-permute-start.8 = (f32[8,64,128]{2,1,0:T(8,128)S(1)}, f32[8,64,128]{2,1,0:T(8,128)S(1)}, u32[]{:S(2)}, u32[]{:S(2)}) collective-permute-start(f32[8,64,128]{2,1,0:T(8,128)S(1)} %get-tuple-element.79.sent), channel_id=1, source_target_pairs={{0,2},{2,0},{4,6},{6,4},{8,10},{10,8},{12,14},{14,12},{16,18},{18,... | collective-permute-start | bytes 786440 | tf_op jit(solution)/shard_map/ppermute | solution.py:746
  28.7 6.4 %step1.1 = (f32[8,4,64,128]{3,2,1,0:T(8,128)S(1)}, f32[2,8,64,128]{3,2,1,0:T(8,128)S(1)}, f32[8,128]{1,0:T(8,128)S(1)}, s32[129]{0:T(256)S(1)}) custom-call(s32[8]{0:T(128)S(1)} %copy-done.4, f32[3,8]{1,0:T(4,128)S(1)} %bitcast.5, s32[128]{0:T(128)S(1)} %copy-done.5, s32[128]{0:T(128)S(1)} %copy-done.6, f32[8,4,64,128]{3,2,1,0:T(8,128)S(1)} %get-tuple-element.59.lam, ...), custom_call_target="tpu_custom_call" | custom-call | flops 40000000 | bytes 4000000 | tf_op jit(solution)/shard_map/step1/pallas_call | solution.py:596
  35.0 0.9 %rim1b.1 = (f32[8,64,128]{2,1,0:T(8,128)S(1)}, f32[8,64,128]{2,1,0:T(8,128)S(1)}) custom-call(s32[8]{0:T(128)S(1)} %copy-done.4, f32[3,8]{1,0:T(4,128)S(1)} %bitcast.6, f32[2,8,64,128]{3,2,1,0:T(8,128)S(1)} %get-tuple-element.78.part_edges, f32[8,64,128]{2,1,0:T(8,128)S(1)} %collective-permute-done.9.got, f32[8,64,128]{2,1,0:T(8,128)S(1)} %get-tuple-element.82.sent, ...), custom_call_target="tpu_custom_call" | custom-call | flops 2000000 | bytes 1500000 | tf_op jit(solution)/shard_map/rim1b/pallas_call | solution.py:658
  35.9 0.7 %collective-permute-start.11 = (f32[8,64,128]{2,1,0:T(8,128)S(1)}, f32[8,64,128]{2,1,0:T(8,128)S(1)}, u32[]{:S(2)}, u32[]{:S(2)}) collective-permute-start(f32[8,64,128]{2,1,0:T(8,128)S(1)} %get-tuple-element.85.sent_b), channel_id=1, source_target_pairs={{2,4},{4,2},{6,8},{8,6},{10,12},{12,10},{14,16},{16,14},{18,20},{2... | collective-permute-start | bytes 786440 | tf_op jit(solution)/shard_map/ppermute | solution.py:749
  36.6 2.5 %collective-permute-done.8.got = f32[8,64,128]{2,1,0:T(8,128)S(1)} collective-permute-done((f32[8,64,128]{2,1,0:T(8,128)S(1)}, f32[8,64,128]{2,1,0:T(8,128)S(1)}, u32[]{:S(2)}, u32[]{:S(2)}) %collective-permute-start.8) | collective-permute-done | bytes 262176 | tf_op jit(solution)/shard_map/ppermute | solution.py:746
  39.1 0.9 %rim1a.1 = (f32[8,64,128]{2,1,0:T(8,128)S(1)}, f32[8,64,128]{2,1,0:T(8,128)S(1)}) custom-call(s32[8]{0:T(128)S(1)} %copy-done.4, f32[3,8]{1,0:T(4,128)S(1)} %bitcast.7, f32[2,8,64,128]{3,2,1,0:T(8,128)S(1)} %get-tuple-element.78.part_edges, f32[8,64,128]{2,1,0:T(8,128)S(1)} %collective-permute-done.8.got, f32[8,64,128]{2,1,0:T(8,128)S(1)} %get-tuple-element.79.sent, ...), custom_call_target="tpu_custom_call" | custom-call | flops 2000000 | bytes 1500000 | tf_op jit(solution)/shard_map/rim1a/pallas_call | solution.py:658
  39.9 2.0 %collective-permute-start.10 = (f32[8,64,128]{2,1,0:T(8,128)S(1)}, f32[8,64,128]{2,1,0:T(8,128)S(1)}, u32[]{:S(2)}, u32[]{:S(2)}) collective-permute-start(f32[8,64,128]{2,1,0:T(8,128)S(1)} %get-tuple-element.84.sent_a), channel_id=1, source_target_pairs={{0,2},{2,0},{4,6},{6,4},{8,10},{10,8},{12,14},{14,12},{16,18},{18,... | collective-permute-start | bytes 786440 | tf_op jit(solution)/shard_map/ppermute | solution.py:746
  41.9 1.8 %front0.1 = (f32[16,8,128]{2,1,0:T(8,128)S(1)}, f32[2,8,80,128]{3,2,1,0:T(8,128)S(1)}) custom-call(s32[128]{0:T(128)S(1)} %copy-done.5, s32[128]{0:T(128)S(1)} %copy-done.6, s32[129]{0:T(256)S(1)} %get-tuple-element.76.inside, f32[8,128]{1,0:T(8,128)S(1)} %get-tuple-element.77.grad_in, f32[8,64,128]{2,1,0:T(8,128)S(1)} %get-tuple-element.81.lam_a, ...), custom_call_target="tpu_custom_call" | custom-call | flops 10000000 | bytes 4000000 | tf_op jit(solution)/shard_map/front0/pallas_call | solution.py:596
  43.7 14.0 %all_to_all.5.grads = f32[16,8,128]{2,1,0:T(8,128)S(1)} all-to-all(f32[16,8,128]{2,1,0:T(8,128)S(1)} %get-tuple-element.86), channel_id=1, replica_groups=mesh['space'=16,'sens'=2] {'space'}, dimensions={0} | all-to-all | bytes 131072 | tf_op jit(solution)/shard_map/all_to_all | solution.py:811
  57.7 2.3 %step0.1 = (f32[8,4,64,128]{3,2,1,0:T(8,128)}, f32[8,128]{1,0:T(8,128)}) custom-call(f32[8,4,64,128]{3,2,1,0:T(8,128)S(1)} %get-tuple-element.75.base, f32[2,8,80,128]{3,2,1,0:T(8,128)S(1)} %get-tuple-element.88.ve, f32[19,4,64,128]{3,2,1,0:T(8,128)S(1)} %get-tuple-element.56.coef.refs_1_, f32[3,4,64,128]{3,2,1,0:T(8,128)S(1)} %get-tuple-element.57.gain, ...), custom_call_target="tpu_custom_call" | custom-call | flops 10000000 | bytes 6000000 | tf_op jit(solution)/shard_map/step0/pallas_call | solution.py:706
  (24 shorter events, 0.1 us)
Async XLA Ops:
  0.6 7.1 %collective-permute-start.2 = (f32[6,4,32,128]{3,2,1,0:T(8,128)}, f32[6,4,32,128]{3,2,1,0:T(8,128)S(1)}, u32[]{:S(2)}, u32[]{:S(2)}) collective-permute-start(f32[6,4,32,128]{3,2,1,0:T(8,128)} %refs_1_), channel_id=1, source_target_pairs={{0,1},{1,0},{2,3},{3,2},{4,5},{5,4},{6,7},{7,6},{8,9},{9,8},{10,11... | collective-permute-start | bytes 1179656 | tf_op jit(solution)/shard_map/ppermute | solution.py:724
  1.1 6.6 %collective-permute-start.3 = (f32[4,4,64,128]{3,2,1,0:T(8,128)}, f32[4,4,64,128]{3,2,1,0:T(8,128)S(1)}, u32[]{:S(2)}, u32[]{:S(2)}) collective-permute-start(f32[4,4,64,128]{3,2,1,0:T(8,128)} %refs_3_), channel_id=1, source_target_pairs={{0,1},{1,0},{2,3},{3,2},{4,5},{5,4},{6,7},{7,6},{8,9},{9,8},{10,11... | collective-permute-start | bytes 1572872 | tf_op jit(solution)/shard_map/ppermute | solution.py:724
  1.2 13.5 %copy-start.7 = (s32[3]{0:T(128)S(1)}, s32[3]{0:T(128)}, u32[]{:S(2)}) copy-start(s32[3]{0:T(128)} %refs_0_.3) | copy-start | bytes 40
  1.2 13.5 %copy-start.8 = (f32[4,4,64,128]{3,2,1,0:T(8,128)S(1)}, f32[4,4,64,128]{3,2,1,0:T(8,128)}, u32[]{:S(2)}) copy-start(f32[4,4,64,128]{3,2,1,0:T(8,128)} %refs_3_) | copy-start | bytes 1572868
  1.2 13.5 %copy-start.9 = (f32[6,4,32,128]{3,2,1,0:T(8,128)S(1)}, f32[6,4,32,128]{3,2,1,0:T(8,128)}, u32[]{:S(2)}) copy-start(f32[6,4,32,128]{3,2,1,0:T(8,128)} %refs_1_) | copy-start | bytes 1179652
  4.1 10.1 %collective-permute-start = (f32[224,128]{1,0:T(8,128)}, f32[224,128]{1,0:T(8,128)S(1)}, u32[]{:S(2)}, u32[]{:S(2)}) collective-permute-start(f32[224,128]{1,0:T(8,128)} %get-tuple-element.46), channel_id=1, source_target_pairs={{0,2},{2,0},{4,6},{6,4},{8,10},{10,8},{12,14},{14,12},{16,18},{18,... | collective-permute-start | bytes 344072 | tf_op jit(solution)/shard_map/ppermute | solution.py:746
  7.1 7.1 %collective-permute-start.1 = (f32[224,128]{1,0:T(8,128)}, f32[224,128]{1,0:T(8,128)S(1)}, u32[]{:S(2)}, u32[]{:S(2)}) collective-permute-start(f32[224,128]{1,0:T(8,128)} %get-tuple-element.47), channel_id=1, source_target_pairs={{2,4},{4,2},{6,8},{8,6},{10,12},{12,10},{14,16},{16,14},{18,20},{2... | collective-permute-start | bytes 344072 | tf_op jit(solution)/shard_map/ppermute | solution.py:749
  7.8 9.0 %copy-start = (f32[8,4,64,128]{3,2,1,0:T(8,128)S(1)}, f32[8,4,64,128]{3,2,1,0:T(8,128)}, u32[]{:S(2)}) copy-start(f32[8,4,64,128]{3,2,1,0:T(8,128)} %lam.1) | copy-start | bytes 3145732
  7.8 9.0 %copy-start.3 = (f32[8,3]{0,1:T(4,128)S(1)}, f32[8,3]{0,1:T(4,128)}, u32[]{:S(2)}) copy-start(f32[8,3]{0,1:T(4,128)} %param.13) | copy-start | bytes 292
  7.8 9.0 %copy-start.4 = (s32[8]{0:T(128)S(1)}, s32[8]{0:T(128)}, u32[]{:S(2)}) copy-start(s32[8]{0:T(128)} %sensors.13) | copy-start | bytes 100
  7.8 12.2 %collective-permute-start.7 = (f32[8,64,128]{2,1,0:T(8,128)}, f32[8,64,128]{2,1,0:T(8,128)S(1)}, u32[]{:S(2)}, u32[]{:S(2)}) collective-permute-start(f32[8,64,128]{2,1,0:T(8,128)} %get-tuple-element.73.sent), channel_id=1, source_target_pairs={{2,4},{4,2},{6,8},{8,6},{10,12},{12,10},{14,16},{16,14},{18,20},{2... | collective-permute-start | bytes 786440 | tf_op jit(solution)/shard_map/ppermute | solution.py:749
  8.6 17.6 %collective-permute-start.6 = (f32[8,64,128]{2,1,0:T(8,128)}, f32[8,64,128]{2,1,0:T(8,128)S(1)}, u32[]{:S(2)}, u32[]{:S(2)}) collective-permute-start(f32[8,64,128]{2,1,0:T(8,128)} %get-tuple-element.64.sent), channel_id=1, source_target_pairs={{0,2},{2,0},{4,6},{6,4},{8,10},{10,8},{12,14},{14,12},{16,18},{18,... | collective-permute-start | bytes 786440 | tf_op jit(solution)/shard_map/ppermute | solution.py:746
  14.2 4.9 %collective-permute-start.4 = (f32[224,128]{1,0:T(8,128)S(1)}, f32[224,128]{1,0:T(8,128)S(1)}, u32[]{:S(2)}, u32[]{:S(2)}) collective-permute-start(f32[224,128]{1,0:T(8,128)S(1)} %collective-permute-done.refs_3_), channel_id=1, source_target_pairs={{0,1},{1,0},{2,3},{3,2},{4,5},{5,4},{6,7},{7,6},{8,9},{9,8},{10,11... | collective-permute-start | bytes 344072 | tf_op jit(solution)/shard_map/ppermute | solution.py:724
  14.2 4.9 %collective-permute-start.5 = (f32[224,128]{1,0:T(8,128)S(1)}, f32[224,128]{1,0:T(8,128)S(1)}, u32[]{:S(2)}, u32[]{:S(2)}) collective-permute-start(f32[224,128]{1,0:T(8,128)S(1)} %collective-permute-done.1.refs_5_), channel_id=1, source_target_pairs={{0,1},{1,0},{2,3},{3,2},{4,5},{5,4},{6,7},{7,6},{8,9},{9,8},{10,11... | collective-permute-start | bytes 344072 | tf_op jit(solution)/shard_map/ppermute | solution.py:724
  19.0 1.1 %copy-start.2 = (f32[8,64,128]{2,1,0:T(8,128)S(1)}, f32[8,64,128]{2,1,0:T(8,128)}, u32[]{:S(2)}) copy-start(f32[8,64,128]{2,1,0:T(8,128)} %get-tuple-element.73.sent) | copy-start | bytes 786436
  19.0 7.2 %copy-start.1 = (f32[8,64,128]{2,1,0:T(8,128)S(1)}, f32[8,64,128]{2,1,0:T(8,128)}, u32[]{:S(2)}) copy-start(f32[8,64,128]{2,1,0:T(8,128)} %get-tuple-element.64.sent) | copy-start | bytes 786436
  20.0 8.6 %copy-start.5 = (s32[128]{0:T(128)S(1)}, s32[128]{0:T(128)}, u32[]{:S(2)}) copy-start(s32[128]{0:T(128)} %cells.3) | copy-start | bytes 1540
  20.0 8.6 %copy-start.6 = (s32[128]{0:T(128)S(1)}, s32[128]{0:T(128)}, u32[]{:S(2)}) copy-start(s32[128]{0:T(128)} %steps.3) | copy-start | bytes 1540
  20.9 14.1 %collective-permute-start.9 = (f32[8,64,128]{2,1,0:T(8,128)S(1)}, f32[8,64,128]{2,1,0:T(8,128)S(1)}, u32[]{:S(2)}, u32[]{:S(2)}) collective-permute-start(f32[8,64,128]{2,1,0:T(8,128)S(1)} %get-tuple-element.82.sent), channel_id=1, source_target_pairs={{2,4},{4,2},{6,8},{8,6},{10,12},{12,10},{14,16},{16,14},{18,20},{2... | collective-permute-start | bytes 786440 | tf_op jit(solution)/shard_map/ppermute | solution.py:749
  27.1 12.0 %collective-permute-start.8 = (f32[8,64,128]{2,1,0:T(8,128)S(1)}, f32[8,64,128]{2,1,0:T(8,128)S(1)}, u32[]{:S(2)}, u32[]{:S(2)}) collective-permute-start(f32[8,64,128]{2,1,0:T(8,128)S(1)} %get-tuple-element.79.sent), channel_id=1, source_target_pairs={{0,2},{2,0},{4,6},{6,4},{8,10},{10,8},{12,14},{14,12},{16,18},{18,... | collective-permute-start | bytes 786440 | tf_op jit(solution)/shard_map/ppermute | solution.py:746
  35.9 21.8 %collective-permute-start.11 = (f32[8,64,128]{2,1,0:T(8,128)S(1)}, f32[8,64,128]{2,1,0:T(8,128)S(1)}, u32[]{:S(2)}, u32[]{:S(2)}) collective-permute-start(f32[8,64,128]{2,1,0:T(8,128)S(1)} %get-tuple-element.85.sent_b), channel_id=1, source_target_pairs={{2,4},{4,2},{6,8},{8,6},{10,12},{12,10},{14,16},{16,14},{18,20},{2... | collective-permute-start | bytes 786440 | tf_op jit(solution)/shard_map/ppermute | solution.py:749
  39.9 17.8 %collective-permute-start.10 = (f32[8,64,128]{2,1,0:T(8,128)S(1)}, f32[8,64,128]{2,1,0:T(8,128)S(1)}, u32[]{:S(2)}, u32[]{:S(2)}) collective-permute-start(f32[8,64,128]{2,1,0:T(8,128)S(1)} %get-tuple-element.84.sent_a), channel_id=1, source_target_pairs={{0,2},{2,0},{4,6},{6,4},{8,10},{10,8},{12,14},{14,12},{16,18},{18,... | collective-permute-start | bytes 786440 | tf_op jit(solution)/shard_map/ppermute | solution.py:746

commit v5 on v4

--- a/solution.py
+++ b/solution.py
@@ -120,7 +120,7 @@
         out_specs=[VMEM] * 4,
         out_shape=[f32(own, rows_y, rows_x)] * 2 + [small, small],
         scratch_shapes=[pltpu.SemaphoreType.DMA((12,))],
-        compiler_params=params(60),
+        compiler_params=params(56),
         cost_estimate=cost(20_000_000_000, 60_000_000),
         name="pack",
     )(owner, sensors, misfit, adj, ckpt, disp)
@@ -278,9 +278,9 @@
 
 
 def ends_kernel(count, slots, *refs):
-    owner, coef, ends = refs[:3]
-    small = refs[3 : 3 + count], refs[3 + count : 3 + 2 * count]
-    edge, edge_raw, corr, tensor, conc = refs[3 + 2 * count :]
+    owner, coef, gains, scales, ends = refs[:5]
+    small = refs[5 : 5 + count], refs[5 + count : 5 + 2 * count]
+    edge, edge_raw, corr, tail, tensor, conc = refs[5 + 2 * count :]
     depth, rows_y, rows_x = coef.shape[1:]
     rows = rows_y // count
     me = lax.axis_index("sens")
@@ -348,19 +348,31 @@
                     corr[i, side, at] = gain - 0.5 * zz * scale
                 else:
                     corr[i, side, at] = gain / scale - 0.5 * zz
-
-
-def ends_call(owner, coef, ends, small_a, small_b, slots):
+                    if i == 0:
+                        keep = gains[0, z, at] / scales[0, z, at]
+                        tail[side, 14, at] = keep + (gain / scale - 0.5 * zz)
+            rows_in = [(name, z) for name in IN_LAYER] + [(name, z - sign) for name in names]
+            for j, (name, layer) in enumerate(rows_in):
+                value = coef[name, layer, at]
+                if tile == rows_y // TILE - 1 and j in (1, 4, 7, 10):
+                    value = jnp.where(ys < TILE - 1, value, 0.0)
+                if tile == 0 and j in (2, 5, 8, 11):
+                    value = jnp.where(ys > 0, value, 0.0)
+                tail[side, j, at] = value
+
+
+def ends_call(owner, coef, gain, scale, ends, small_a, small_b, slots):
     count = len(small_a)
     _, _, rows_y, rows_x = coef.shape
     return pl.pallas_call(
         functools.partial(ends_kernel, count, slots),
-        in_specs=[SMEM] + [VMEM] * (2 + 2 * count),
-        out_specs=[VMEM] * 3,
+        in_specs=[SMEM] + [VMEM] * (4 + 2 * count),
+        out_specs=[VMEM] * 4,
         out_shape=[
             f32(2, 5, rows_y, rows_x),
             f32(2, 5, rows_y, rows_x),
             f32(STEPS, 2, rows_y, rows_x),
+            f32(2, 15, rows_y, rows_x),
         ],
         scratch_shapes=[
             pltpu.VMEM((2, 3, rows_y, rows_x), jnp.float32),
@@ -369,7 +381,7 @@
         compiler_params=params(16),
         cost_estimate=cost(1_000_000, 1_000_000),
         name="ends",
-    )(owner, coef, ends, *small_a, *small_b)
+    )(owner, coef, gain, scale, ends, *small_a, *small_b)
 
 
 def gather_field(first, lam, lam_a, lam_b, mu):
@@ -530,7 +542,7 @@
 
 
 def front_kernel(
-    cells, steps, inside, grad_in, lam_a, lam_b, sent_a, sent_b, coef, edge, corr, gain, scale, grads, ve, total
+    cells, steps, inside, grad_in, lam_a, lam_b, sent_a, sent_b, coef, edge, corr, gain, scale, grads, total, ve
 ):
     own, rows_y, rows_x = lam_a.shape
     depth = coef.shape[1]
@@ -666,7 +678,7 @@
     )(sensors, misfit, part_edges, got, sent, edge, corr, scale)
 
 
-def last_kernel(base, ve, coef, gain, scale, got_a, got_b, edge, corr, grads, out, grad, part, sems):
+def last_kernel(base, sent_a, sent_b, tail, got_a, got_b, edge, out, part, sems):
     own, depth, rows_y, rows_x = base.shape
     tiles = rows_y // TILE
     copies = [
@@ -675,39 +687,34 @@
     for c in copies:
         c.start()
     side_a = 1 - parity()
-    for turn, (got, side) in enumerate(((got_b, 1 - side_a), (got_a, side_a))):
+    pairs = ((got_b, sent_b, 1 - side_a), (got_a, sent_a, side_a))
+    for turn, (got, sent, side) in enumerate(pairs):
         end = side * (depth - 1)
         inner = end + 1 - 2 * side
         for tile in range(tiles):
             at = pl.ds(tile * TILE, TILE)
-            ce = [coef[j, end, at] for j in IN_LAYER]
-            ci = [coef[jnp.where(side == 0, low, high), inner, at] for low, high in zip(LOW, HIGH)]
+            ce = [tail[side, j, at] for j in range(9)]
+            ci = [tail[side, 9 + j, at] for j in range(5)]
             cm = [edge[side, j, at] for j in range(5)]
-            keep = gain[0, end, at] / scale[0, end, at] + corr[0, side, at]
+            keep = tail[side, 14, at]
             for k in range(own):
-                here, up, down = (
-                    ve[side, k, pl.ds(PAD + tile * TILE + d, TILE)] for d in (0, 1, -1)
-                )
+                here, up, down = met(sent, k, tile, tiles)
                 value = base[k, end, at] + keep * here + in_layer(ce, here, up, down)
                 part[k, end, at] = value + from_met(cm, *met(got, k, tile, tiles))
                 part[k, inner, at] = base[k, inner, at] + from_met(ci, here, up, down)
         for z, sem in ((end, turn), (inner, depth - 1 - turn)):
             copies.append(pltpu.make_async_copy(part.at[:, z], out.at[:, z], sems.at[sem]))
             copies[-1].start()
-    total = grads[0]
-    for i in range(1, grads.shape[0]):
-        total += grads[i]
-    grad[...] = total
     for c in copies:
         c.wait()
 
 
-def last_call(base, ve, coef, gain, scale, got_a, got_b, edge, corr, grads):
+def last_call(base, sent_a, sent_b, tail, got_a, got_b, edge):
     return pl.pallas_call(
         last_kernel,
-        in_specs=[VMEM] * 10,
-        out_specs=[ANY, VMEM],
-        out_shape=[f32(*base.shape), f32(*grads.shape[1:])],
+        in_specs=[VMEM] * 7,
+        out_specs=ANY,
+        out_shape=f32(*base.shape),
         scratch_shapes=[
             pltpu.VMEM(base.shape, jnp.float32),
             pltpu.SemaphoreType.DMA((base.shape[1],)),
@@ -715,7 +722,7 @@
         compiler_params=params(16),
         cost_estimate=cost(10_000_000, 6_000_000),
         name="step0",
-    )(base, ve, coef, gain, scale, got_a, got_b, edge, corr, grads)
+    )(base, sent_a, sent_b, tail, got_a, got_b, edge)
 
 
 def turned(array, axis):
@@ -776,8 +783,8 @@
         40_000_000,
     )
     small_a, small_b, part_edges = lax.optimization_barrier((small_a, small_b, part_edges))
-    edge, edge_raw, corr = ends_call(
-        owner_steps, coef, ends, small_a, small_b, checkpoints.shape[0]
+    edge, edge_raw, corr, tail = ends_call(
+        owner_steps, coef, gain, scale, ends, small_a, small_b, checkpoints.shape[0]
     )
     lam_b, send_b = rim(2, True, *sensors, part_edges, got_b, sent_b, edge_raw, corr, scale)
     got_b = swap_b(send_b)
@@ -799,18 +806,19 @@
     lam_a, send_a = rim(1, False, *sensors, part_edges, got_a, sent_a, edge, corr, scale)
     got_a = swap_a(send_a)
     halo = f32(2, own, rows_y + 2 * PAD, rows_x)
-    grads, ve = field_call(
+    (grads,) = field_call(
         front_kernel,
         "front0",
         (*release, inside, grad, lam_a, lam_b, send_a, send_b, coef, edge, corr, gain, scale),
         [SMEM] * 3 + [VMEM] * 10,
-        [f32(slabs, *kept.shape), halo],
-        [kept],
+        [f32(slabs, *kept.shape)],
+        [kept, halo],
         10_000_000,
     )
     grads = lax.all_to_all(grads, "space", 0, 0, tiled=True)
-    grads, ve = lax.optimization_barrier((grads, ve))
-    return tuple(last_call(base, ve, coef, gain, scale, got_a, got_b, edge, corr, grads))
+    lam = last_call(base, send_a, send_b, tail, got_a, got_b, edge)
+    lam, grads = lax.optimization_barrier((lam, grads))
+    return lam, jnp.sum(grads, axis=0)
 
 
 def solution(mesh):

time: 60.1 us -> 59 us (0.982)
  blocking collectives: 14 us -> 0 us
  starting transfers between devices: 16 us -> 21.5 us
  waiting for transfers between devices: 7.1 us -> 12.3 us
  Pallas kernels: 22 us -> 23 us
  other arithmetic: 0 us -> 0.61 us
    all_to_all x1 -> x0, blocking collectives: 14 us -> none  [body(): grads = lax.all_to_all(grads, 'space', 0, 0, tiled=True)]
    all_to_all x0 -> x1, starting transfers between devices: none -> 5.38 us  [body(): grads = lax.all_to_all(grads, 'space', 0, 0, tiled=True)]
    all_to_all x0 -> x1, waiting for transfers between devices: none -> 4.09 us  [body(): grads = lax.all_to_all(grads, 'space', 0, 0, tiled=True)]
    pallas_call x3, Pallas kernels: 10.3 us -> 11.8 us  [field_call(): pl.pallas_call(kernel, in_specs=specs, out_specs=[VMEM] * len(outs) + [SM...]
    ppermute x4, waiting for transfers between devices: 7.08 us -> 8.22 us  [swap_a(): return lax.ppermute(x, 'space', pairs_a)]
    pallas_call x1, Pallas kernels: 2.34 us -> 1.71 us  [last_call(): pl.pallas_call(last_kernel, in_specs=[VMEM] * 7, out_specs=ANY, out_shape...]
    reduce_sum x0 -> x1, other arithmetic: none -> 0.61 us  [body(): return (lam, jnp.sum(grads, axis=0))]
  transfers between devices with their start and end apart: 12 -> 13, of which waited for: 2 -> 4; matrix products, arithmetic and copies ran while one was open for 0% -> 0% of each run, Pallas kernels for 33% -> 39%
where the time goes in v5:
time: 59 us; the launch traced here: 58.4 us
  Pallas kernels  23 us (39%)
  starting transfers between devices  21.5 us (36%)
  waiting for transfers between devices  12.3 us (21%)
  between operations  0.9 us (2%)
  other arithmetic  0.61 us (1%)
    ppermute x4, starting transfers between devices, swap_a(): return lax.ppermute(x, 'space', pairs_a)  12.2 us
    pallas_call x3, Pallas kernels, field_call(): pl.pallas_call(kernel, in_specs=specs, out_specs=[VMEM] * len(outs) + [SM...  11.8 us
    ppermute x4, waiting for transfers between devices, swap_a(): return lax.ppermute(x, 'space', pairs_a)  8.22 us
    all_to_all x1, starting transfers between devices, body(): grads = lax.all_to_all(grads, 'space', 0, 0, tiled=True)  5.38 us
    all_to_all x1, waiting for transfers between devices, body(): grads = lax.all_to_all(grads, 'space', 0, 0, tiled=True)  4.09 us
    pallas_call x4, Pallas kernels, rim(): pl.pallas_call(functools.partial(rim_kernel, step, late), in_specs=[SMEM]...  3.44 us
    pallas_call x1, Pallas kernels, pack(): pl.pallas_call(pack_kernel, in_specs=[SMEM] * 3 + [ANY] * 3, out_specs=[V...  2.86 us
    ppermute x4, starting transfers between devices, swap_b(): return lax.ppermute(x, 'space', pairs_b)  2.82 us
  transfers between devices with their start and end apart: 13, of which 4 were waited for; matrix products, arithmetic and copies ran while one was open for 0% of the time, Pallas kernels for 39%

profile of v5, /device:TPU:0, one launch (start us, length us, event | category | flops | bytes accessed | tf_op | source)
XLA Modules:
  0.0 58.4 jit_solution(9668893827330411436)
XLA Ops:
  0.6 0.5 collective-permute-start.2
  1.1 0.1 collective-permute-start.3
  1.2 2.9 %pack.1 = (f32[8,64,128]{2,1,0:T(8,128)}, f32[8,64,128]{2,1,0:T(8,128)}, f32[224,128]{1,0:T(8,128)}, f32[224,128]{1,0:T(8,128)}) custom-call(s32[3]{0:T(128)} %refs_0_.3, s32[8]{0:T(128)} %sensors.13, f32[3,8]{1,0:T(4,128)} %bitcast.1, f32[8,4,64,128]{3,2,1,0:T(8,128)} %lam.1, f32[4,4,64,128]{3,2,1,0:T(8,128)} %refs_3_, f32[6,4,32,128]{3,2,1,0:T(8,128)} %refs_1_), custom_call_target="tpu_custom_call" | custom-call | flops 20000000000 | bytes 60000000 | tf_op jit(solution)/shard_map/pack/pallas_call | solution.py:117
  4.1 3.0 %collective-permute-start = (f32[224,128]{1,0:T(8,128)}, f32[224,128]{1,0:T(8,128)S(1)}, u32[]{:S(2)}, u32[]{:S(2)}) collective-permute-start(f32[224,128]{1,0:T(8,128)} %get-tuple-element.45), channel_id=1, source_target_pairs={{0,2},{2,0},{4,6},{6,4},{8,10},{10,8},{12,14},{14,12},{16,18},{18,... | collective-permute-start | bytes 344072 | tf_op jit(solution)/shard_map/ppermute | solution.py:753
  7.1 0.7 %collective-permute-start.1 = (f32[224,128]{1,0:T(8,128)}, f32[224,128]{1,0:T(8,128)S(1)}, u32[]{:S(2)}, u32[]{:S(2)}) collective-permute-start(f32[224,128]{1,0:T(8,128)} %get-tuple-element.46), channel_id=1, source_target_pairs={{2,4},{4,2},{6,8},{8,6},{10,12},{12,10},{14,16},{16,14},{18,20},{2... | collective-permute-start | bytes 344072 | tf_op jit(solution)/shard_map/ppermute | solution.py:756
  7.8 0.0 copy-start
  7.8 0.0 copy-start.3
  7.8 0.0 copy-start.4
  7.8 0.8 %collective-permute-start.7 = (f32[8,64,128]{2,1,0:T(8,128)}, f32[8,64,128]{2,1,0:T(8,128)S(1)}, u32[]{:S(2)}, u32[]{:S(2)}) collective-permute-start(f32[8,64,128]{2,1,0:T(8,128)} %get-tuple-element.72.sent), channel_id=1, source_target_pairs={{2,4},{4,2},{6,8},{8,6},{10,12},{12,10},{14,16},{16,14},{18,20},{2... | collective-permute-start | bytes 786440 | tf_op jit(solution)/shard_map/ppermute | solution.py:756
  8.6 5.5 %collective-permute-start.6 = (f32[8,64,128]{2,1,0:T(8,128)}, f32[8,64,128]{2,1,0:T(8,128)S(1)}, u32[]{:S(2)}, u32[]{:S(2)}) collective-permute-start(f32[8,64,128]{2,1,0:T(8,128)} %get-tuple-element.63.sent), channel_id=1, source_target_pairs={{0,2},{2,0},{4,6},{6,4},{8,10},{10,8},{12,14},{14,12},{16,18},{18,... | collective-permute-start | bytes 786440 | tf_op jit(solution)/shard_map/ppermute | solution.py:753
  14.2 0.5 collective-permute-start.5
  14.7 2.1 %planes.1 = (f32[19,4,64,128]{3,2,1,0:T(8,128)S(1)}, f32[3,4,64,128]{3,2,1,0:T(8,128)S(1)}, f32[3,4,64,128]{3,2,1,0:T(8,128)S(1)}, f32[3,2,64,128]{3,2,1,0:T(8,128)S(1)}) custom-call(s32[3]{0:T(128)S(1)} %copy-done.7, f32[6,4,32,128]{3,2,1,0:T(8,128)S(1)} %copy-done.9, f32[6,4,32,128]{3,2,1,0:T(8,128)S(1)} %collective-permute-done.2.refs_2_, ...), custom_call_target="tpu_custom_call" | custom-call | flops 2000000000 | bytes 60000000 | tf_op jit(solution)/shard_map/planes/pallas_call | solution.py:260
  16.8 2.2 %step2.1 = (f32[8,4,64,128]{3,2,1,0:T(8,128)S(1)}, f32[2,8,64,128]{3,2,1,0:T(8,128)S(1)}) custom-call(s32[8]{0:T(128)S(1)} %copy-done.4, f32[3,8]{1,0:T(4,128)S(1)} %bitcast.2, f32[8,4,64,128]{3,2,1,0:T(8,128)S(1)} %copy-done, f32[19,4,64,128]{3,2,1,0:T(8,128)S(1)} %get-tuple-element.55.coef.refs_1_, f32[3,4,64,128]{3,2,1,0:T(8,128)S(1)} %get-tuple-element.56.gain.refs_2_, ...), custom_call_target="tpu_custom_call" | custom-call | flops 40000000 | bytes 4000000 | tf_op jit(solution)/shard_map/step2/pallas_call | solution.py:608
  19.0 1.0 %ends.1 = (f32[2,5,64,128]{3,2,1,0:T(8,128)S(1)}, f32[2,5,64,128]{3,2,1,0:T(8,128)S(1)}, f32[3,2,64,128]{3,2,1,0:T(8,128)S(1)}, f32[2,15,64,128]{3,2,1,0:T(8,128)S(1)}) custom-call(s32[3]{0:T(128)S(1)} %copy-done.7, f32[19,4,64,128]{3,2,1,0:T(8,128)S(1)} %get-tuple-element.55.coef.refs_1_, f32[3,4,64,128]{3,2,1,0:T(8,128)S(1)} %get-tuple-element.56.gain.refs_2_, ...), custom_call_target="tpu_custom_call" | custom-call | flops 1000000 | bytes 1000000 | tf_op jit(solution)/shard_map/ends/pallas_call | solution.py:367
  20.1 0.0 copy-start.5
  20.1 0.9 %rim2b.1 = (f32[8,64,128]{2,1,0:T(8,128)S(1)}, f32[8,64,128]{2,1,0:T(8,128)S(1)}) custom-call(s32[8]{0:T(128)S(1)} %copy-done.4, f32[3,8]{1,0:T(4,128)S(1)} %bitcast.3, f32[2,8,64,128]{3,2,1,0:T(8,128)S(1)} %get-tuple-element.62.part_edges, f32[8,64,128]{2,1,0:T(8,128)S(1)} %collective-permute-done.7.got, f32[8,64,128]{2,1,0:T(8,128)S(1)} %copy-done.2, ...), custom_call_target="tpu_custom_call" | custom-call | flops 2000000 | bytes 1500000 | tf_op jit(solution)/shard_map/rim2b/pallas_call | solution.py:670
  21.0 0.7 %collective-permute-start.9 = (f32[8,64,128]{2,1,0:T(8,128)S(1)}, f32[8,64,128]{2,1,0:T(8,128)S(1)}, u32[]{:S(2)}, u32[]{:S(2)}) collective-permute-start(f32[8,64,128]{2,1,0:T(8,128)S(1)} %get-tuple-element.79.sent), channel_id=1, source_target_pairs={{2,4},{4,2},{6,8},{8,6},{10,12},{12,10},{14,16},{16,14},{18,20},{2... | collective-permute-start | bytes 786440 | tf_op jit(solution)/shard_map/ppermute | solution.py:756
  21.7 4.6 %collective-permute-done.6.got = f32[8,64,128]{2,1,0:T(8,128)S(1)} collective-permute-done((f32[8,64,128]{2,1,0:T(8,128)}, f32[8,64,128]{2,1,0:T(8,128)S(1)}, u32[]{:S(2)}, u32[]{:S(2)}) %collective-permute-start.6) | collective-permute-done | bytes 262176 | tf_op jit(solution)/shard_map/ppermute | solution.py:753
  26.2 0.9 %rim2a.1 = (f32[8,64,128]{2,1,0:T(8,128)S(1)}, f32[8,64,128]{2,1,0:T(8,128)S(1)}) custom-call(s32[8]{0:T(128)S(1)} %copy-done.4, f32[3,8]{1,0:T(4,128)S(1)} %bitcast.4, f32[2,8,64,128]{3,2,1,0:T(8,128)S(1)} %get-tuple-element.62.part_edges, f32[8,64,128]{2,1,0:T(8,128)S(1)} %collective-permute-done.6.got, f32[8,64,128]{2,1,0:T(8,128)S(1)} %copy-done.1, ...), custom_call_target="tpu_custom_call" | custom-call | flops 2000000 | bytes 1500000 | tf_op jit(solution)/shard_map/rim2a/pallas_call | solution.py:670
  27.1 1.6 %collective-permute-start.8 = (f32[8,64,128]{2,1,0:T(8,128)S(1)}, f32[8,64,128]{2,1,0:T(8,128)S(1)}, u32[]{:S(2)}, u32[]{:S(2)}) collective-permute-start(f32[8,64,128]{2,1,0:T(8,128)S(1)} %get-tuple-element.76.sent), channel_id=1, source_target_pairs={{0,2},{2,0},{4,6},{6,4},{8,10},{10,8},{12,14},{14,12},{16,18},{18,... | collective-permute-start | bytes 786440 | tf_op jit(solution)/shard_map/ppermute | solution.py:753
  28.7 6.9 %step1.1 = (f32[8,4,64,128]{3,2,1,0:T(8,128)S(1)}, f32[2,8,64,128]{3,2,1,0:T(8,128)S(1)}, f32[8,128]{1,0:T(8,128)S(1)}, s32[129]{0:T(256)S(1)}) custom-call(s32[8]{0:T(128)S(1)} %copy-done.4, f32[3,8]{1,0:T(4,128)S(1)} %bitcast.5, s32[128]{0:T(128)S(1)} %copy-done.5, s32[128]{0:T(128)S(1)} %copy-done.6, f32[8,4,64,128]{3,2,1,0:T(8,128)S(1)} %get-tuple-element.58.lam, ...), custom_call_target="tpu_custom_call" | custom-call | flops 40000000 | bytes 4000000 | tf_op jit(solution)/shard_map/step1/pallas_call | solution.py:608
  35.6 0.9 %rim1b.1 = (f32[8,64,128]{2,1,0:T(8,128)S(1)}, f32[8,64,128]{2,1,0:T(8,128)S(1)}) custom-call(s32[8]{0:T(128)S(1)} %copy-done.4, f32[3,8]{1,0:T(4,128)S(1)} %bitcast.6, f32[2,8,64,128]{3,2,1,0:T(8,128)S(1)} %get-tuple-element.75.part_edges, f32[8,64,128]{2,1,0:T(8,128)S(1)} %collective-permute-done.9.got, f32[8,64,128]{2,1,0:T(8,128)S(1)} %get-tuple-element.79.sent, ...), custom_call_target="tpu_custom_call" | custom-call | flops 2000000 | bytes 1500000 | tf_op jit(solution)/shard_map/rim1b/pallas_call | solution.py:670
  36.5 0.7 %collective-permute-start.11 = (f32[8,64,128]{2,1,0:T(8,128)S(1)}, f32[8,64,128]{2,1,0:T(8,128)S(1)}, u32[]{:S(2)}, u32[]{:S(2)}) collective-permute-start(f32[8,64,128]{2,1,0:T(8,128)S(1)} %get-tuple-element.80.sent_b), channel_id=1, source_target_pairs={{2,4},{4,2},{6,8},{8,6},{10,12},{12,10},{14,16},{16,14},{18,20},{2... | collective-permute-start | bytes 786440 | tf_op jit(solution)/shard_map/ppermute | solution.py:756
  37.1 1.9 %collective-permute-done.8.got = f32[8,64,128]{2,1,0:T(8,128)S(1)} collective-permute-done((f32[8,64,128]{2,1,0:T(8,128)S(1)}, f32[8,64,128]{2,1,0:T(8,128)S(1)}, u32[]{:S(2)}, u32[]{:S(2)}) %collective-permute-start.8) | collective-permute-done | bytes 262176 | tf_op jit(solution)/shard_map/ppermute | solution.py:753
  39.1 0.9 %rim1a.1 = (f32[8,64,128]{2,1,0:T(8,128)S(1)}, f32[8,64,128]{2,1,0:T(8,128)S(1)}) custom-call(s32[8]{0:T(128)S(1)} %copy-done.4, f32[3,8]{1,0:T(4,128)S(1)} %bitcast.7, f32[2,8,64,128]{3,2,1,0:T(8,128)S(1)} %get-tuple-element.75.part_edges, f32[8,64,128]{2,1,0:T(8,128)S(1)} %collective-permute-done.8.got, f32[8,64,128]{2,1,0:T(8,128)S(1)} %get-tuple-element.76.sent, ...), custom_call_target="tpu_custom_call" | custom-call | flops 2000000 | bytes 1500000 | tf_op jit(solution)/shard_map/rim1a/pallas_call | solution.py:670
  40.0 2.2 %collective-permute-start.10 = (f32[8,64,128]{2,1,0:T(8,128)S(1)}, f32[8,64,128]{2,1,0:T(8,128)S(1)}, u32[]{:S(2)}, u32[]{:S(2)}) collective-permute-start(f32[8,64,128]{2,1,0:T(8,128)S(1)} %get-tuple-element.78.sent_a), channel_id=1, source_target_pairs={{0,2},{2,0},{4,6},{6,4},{8,10},{10,8},{12,14},{14,12},{16,18},{18,... | collective-permute-start | bytes 786440 | tf_op jit(solution)/shard_map/ppermute | solution.py:753
  42.1 2.7 %front0.1 = f32[16,8,128]{2,1,0:T(8,128)} custom-call(s32[128]{0:T(128)S(1)} %copy-done.5, s32[128]{0:T(128)S(1)} %copy-done.6, s32[129]{0:T(256)S(1)} %get-tuple-element.82.inside, f32[8,128]{1,0:T(8,128)S(1)} %get-tuple-element.83.grad_in, f32[8,64,128]{2,1,0:T(8,128)S(1)} %get-tuple-element.84.lam_a, f32[8,64,128]{2,1,0:T(8,128)S(1)} %get-tuple-element.85.lam_b, ...), custom_call_target="tpu_custom_call" | custom-call | flops 10000000 | bytes 4000000 | tf_op jit(solution)/shard_map/front0/pallas_call | solution.py:608
  44.9 5.4 %all-to-all-start = ((f32[16,8,128]{2,1,0:T(8,128)}), f32[16,8,128]{2,1,0:T(8,128)S(1)}, u32[]{:S(2)}, u32[]{:S(2)}) async-start(f32[16,8,128]{2,1,0:T(8,128)} %front0.1), calls=%async_computation | async-start | bytes 131072 | tf_op jit(solution)/shard_map/all_to_all | solution.py:818
  50.3 1.7 %collective-permute-done.10.got_a = f32[8,64,128]{2,1,0:T(8,128)S(1)} collective-permute-done((f32[8,64,128]{2,1,0:T(8,128)S(1)}, f32[8,64,128]{2,1,0:T(8,128)S(1)}, u32[]{:S(2)}, u32[]{:S(2)}) %collective-permute-start.10) | collective-permute-done | bytes 262176 | tf_op jit(solution)/shard_map/ppermute | solution.py:753
  52.0 1.7 %step0.1 = f32[8,4,64,128]{3,2,1,0:T(8,128)} custom-call(f32[8,4,64,128]{3,2,1,0:T(8,128)S(1)} %get-tuple-element.74.base, f32[8,64,128]{2,1,0:T(8,128)S(1)} %get-tuple-element.78.sent_a, f32[8,64,128]{2,1,0:T(8,128)S(1)} %get-tuple-element.80.sent_b, f32[2,15,64,128]{3,2,1,0:T(8,128)S(1)} %get-tuple-element.81.tail, ...), custom_call_target="tpu_custom_call" | custom-call | flops 10000000 | bytes 6000000 | tf_op jit(solution)/shard_map/step0/pallas_call | solution.py:713
  53.7 4.1 %all-to-all-done = f32[16,8,128]{2,1,0:T(8,128)S(1)} async-done(((f32[16,8,128]{2,1,0:T(8,128)}), f32[16,8,128]{2,1,0:T(8,128)S(1)}, u32[]{:S(2)}, u32[]{:S(2)}) %all-to-all-start) | async-done | bytes 65568 | tf_op jit(solution)/shard_map/all_to_all | solution.py:818
  57.8 0.6 %reduce_sum.9 = f32[8,128]{1,0:T(8,128)} reduce(f32[16,8,128]{2,1,0:T(8,128)S(1)} %all-to-all-done, f32[]{:T(128)} %constant.0.clone.1), dimensions={0}, to_apply=%region_0.0 | reduce | flops 15360 | bytes 69636 | tf_op jit(solution)/shard_map/reduce_sum | solution.py:821
  (26 shorter events, 0.1 us)
Async XLA Ops:
  0.6 7.1 %collective-permute-start.2 = (f32[6,4,32,128]{3,2,1,0:T(8,128)}, f32[6,4,32,128]{3,2,1,0:T(8,128)S(1)}, u32[]{:S(2)}, u32[]{:S(2)}) collective-permute-start(f32[6,4,32,128]{3,2,1,0:T(8,128)} %refs_1_), channel_id=1, source_target_pairs={{0,1},{1,0},{2,3},{3,2},{4,5},{5,4},{6,7},{7,6},{8,9},{9,8},{10,11... | collective-permute-start | bytes 1179656 | tf_op jit(solution)/shard_map/ppermute | solution.py:731
  1.1 6.6 %collective-permute-start.3 = (f32[4,4,64,128]{3,2,1,0:T(8,128)}, f32[4,4,64,128]{3,2,1,0:T(8,128)S(1)}, u32[]{:S(2)}, u32[]{:S(2)}) collective-permute-start(f32[4,4,64,128]{3,2,1,0:T(8,128)} %refs_3_), channel_id=1, source_target_pairs={{0,1},{1,0},{2,3},{3,2},{4,5},{5,4},{6,7},{7,6},{8,9},{9,8},{10,11... | collective-permute-start | bytes 1572872 | tf_op jit(solution)/shard_map/ppermute | solution.py:731
  1.2 13.4 %copy-start.7 = (s32[3]{0:T(128)S(1)}, s32[3]{0:T(128)}, u32[]{:S(2)}) copy-start(s32[3]{0:T(128)} %refs_0_.3) | copy-start | bytes 40
  1.2 13.4 %copy-start.8 = (f32[4,4,64,128]{3,2,1,0:T(8,128)S(1)}, f32[4,4,64,128]{3,2,1,0:T(8,128)}, u32[]{:S(2)}) copy-start(f32[4,4,64,128]{3,2,1,0:T(8,128)} %refs_3_) | copy-start | bytes 1572868
  1.2 13.4 %copy-start.9 = (f32[6,4,32,128]{3,2,1,0:T(8,128)S(1)}, f32[6,4,32,128]{3,2,1,0:T(8,128)}, u32[]{:S(2)}) copy-start(f32[6,4,32,128]{3,2,1,0:T(8,128)} %refs_1_) | copy-start | bytes 1179652
  4.1 10.1 %collective-permute-start = (f32[224,128]{1,0:T(8,128)}, f32[224,128]{1,0:T(8,128)S(1)}, u32[]{:S(2)}, u32[]{:S(2)}) collective-permute-start(f32[224,128]{1,0:T(8,128)} %get-tuple-element.45), channel_id=1, source_target_pairs={{0,2},{2,0},{4,6},{6,4},{8,10},{10,8},{12,14},{14,12},{16,18},{18,... | collective-permute-start | bytes 344072 | tf_op jit(solution)/shard_map/ppermute | solution.py:753
  7.1 7.1 %collective-permute-start.1 = (f32[224,128]{1,0:T(8,128)}, f32[224,128]{1,0:T(8,128)S(1)}, u32[]{:S(2)}, u32[]{:S(2)}) collective-permute-start(f32[224,128]{1,0:T(8,128)} %get-tuple-element.46), channel_id=1, source_target_pairs={{2,4},{4,2},{6,8},{8,6},{10,12},{12,10},{14,16},{16,14},{18,20},{2... | collective-permute-start | bytes 344072 | tf_op jit(solution)/shard_map/ppermute | solution.py:756
  7.8 9.0 %copy-start = (f32[8,4,64,128]{3,2,1,0:T(8,128)S(1)}, f32[8,4,64,128]{3,2,1,0:T(8,128)}, u32[]{:S(2)}) copy-start(f32[8,4,64,128]{3,2,1,0:T(8,128)} %lam.1) | copy-start | bytes 3145732
  7.8 9.0 %copy-start.3 = (f32[8,3]{0,1:T(4,128)S(1)}, f32[8,3]{0,1:T(4,128)}, u32[]{:S(2)}) copy-start(f32[8,3]{0,1:T(4,128)} %param.13) | copy-start | bytes 292
  7.8 9.0 %copy-start.4 = (s32[8]{0:T(128)S(1)}, s32[8]{0:T(128)}, u32[]{:S(2)}) copy-start(s32[8]{0:T(128)} %sensors.13) | copy-start | bytes 100
  7.8 12.3 %collective-permute-start.7 = (f32[8,64,128]{2,1,0:T(8,128)}, f32[8,64,128]{2,1,0:T(8,128)S(1)}, u32[]{:S(2)}, u32[]{:S(2)}) collective-permute-start(f32[8,64,128]{2,1,0:T(8,128)} %get-tuple-element.72.sent), channel_id=1, source_target_pairs={{2,4},{4,2},{6,8},{8,6},{10,12},{12,10},{14,16},{16,14},{18,20},{2... | collective-permute-start | bytes 786440 | tf_op jit(solution)/shard_map/ppermute | solution.py:756
  8.6 17.6 %collective-permute-start.6 = (f32[8,64,128]{2,1,0:T(8,128)}, f32[8,64,128]{2,1,0:T(8,128)S(1)}, u32[]{:S(2)}, u32[]{:S(2)}) collective-permute-start(f32[8,64,128]{2,1,0:T(8,128)} %get-tuple-element.63.sent), channel_id=1, source_target_pairs={{0,2},{2,0},{4,6},{6,4},{8,10},{10,8},{12,14},{14,12},{16,18},{18,... | collective-permute-start | bytes 786440 | tf_op jit(solution)/shard_map/ppermute | solution.py:753
  14.2 4.8 %collective-permute-start.4 = (f32[224,128]{1,0:T(8,128)S(1)}, f32[224,128]{1,0:T(8,128)S(1)}, u32[]{:S(2)}, u32[]{:S(2)}) collective-permute-start(f32[224,128]{1,0:T(8,128)S(1)} %collective-permute-done.refs_5_), channel_id=1, source_target_pairs={{0,1},{1,0},{2,3},{3,2},{4,5},{5,4},{6,7},{7,6},{8,9},{9,8},{10,11... | collective-permute-start | bytes 344072 | tf_op jit(solution)/shard_map/ppermute | solution.py:731
  14.2 4.9 %collective-permute-start.5 = (f32[224,128]{1,0:T(8,128)S(1)}, f32[224,128]{1,0:T(8,128)S(1)}, u32[]{:S(2)}, u32[]{:S(2)}) collective-permute-start(f32[224,128]{1,0:T(8,128)S(1)} %collective-permute-done.1.refs_7_), channel_id=1, source_target_pairs={{0,1},{1,0},{2,3},{3,2},{4,5},{5,4},{6,7},{7,6},{8,9},{9,8},{10,11... | collective-permute-start | bytes 344072 | tf_op jit(solution)/shard_map/ppermute | solution.py:731
  19.0 1.1 %copy-start.2 = (f32[8,64,128]{2,1,0:T(8,128)S(1)}, f32[8,64,128]{2,1,0:T(8,128)}, u32[]{:S(2)}) copy-start(f32[8,64,128]{2,1,0:T(8,128)} %get-tuple-element.72.sent) | copy-start | bytes 786436
  19.0 7.2 %copy-start.1 = (f32[8,64,128]{2,1,0:T(8,128)S(1)}, f32[8,64,128]{2,1,0:T(8,128)}, u32[]{:S(2)}) copy-start(f32[8,64,128]{2,1,0:T(8,128)} %get-tuple-element.63.sent) | copy-start | bytes 786436
  20.1 8.6 %copy-start.5 = (s32[128]{0:T(128)S(1)}, s32[128]{0:T(128)}, u32[]{:S(2)}) copy-start(s32[128]{0:T(128)} %cells.3) | copy-start | bytes 1540
  20.1 8.6 %copy-start.6 = (s32[128]{0:T(128)S(1)}, s32[128]{0:T(128)}, u32[]{:S(2)}) copy-start(s32[128]{0:T(128)} %steps.3) | copy-start | bytes 1540
  21.0 14.6 %collective-permute-start.9 = (f32[8,64,128]{2,1,0:T(8,128)S(1)}, f32[8,64,128]{2,1,0:T(8,128)S(1)}, u32[]{:S(2)}, u32[]{:S(2)}) collective-permute-start(f32[8,64,128]{2,1,0:T(8,128)S(1)} %get-tuple-element.79.sent), channel_id=1, source_target_pairs={{2,4},{4,2},{6,8},{8,6},{10,12},{12,10},{14,16},{16,14},{18,20},{2... | collective-permute-start | bytes 786440 | tf_op jit(solution)/shard_map/ppermute | solution.py:756
  27.1 12.0 %collective-permute-start.8 = (f32[8,64,128]{2,1,0:T(8,128)S(1)}, f32[8,64,128]{2,1,0:T(8,128)S(1)}, u32[]{:S(2)}, u32[]{:S(2)}) collective-permute-start(f32[8,64,128]{2,1,0:T(8,128)S(1)} %get-tuple-element.76.sent), channel_id=1, source_target_pairs={{0,2},{2,0},{4,6},{6,4},{8,10},{10,8},{12,14},{14,12},{16,18},{18,... | collective-permute-start | bytes 786440 | tf_op jit(solution)/shard_map/ppermute | solution.py:753
  36.5 13.8 %collective-permute-start.11 = (f32[8,64,128]{2,1,0:T(8,128)S(1)}, f32[8,64,128]{2,1,0:T(8,128)S(1)}, u32[]{:S(2)}, u32[]{:S(2)}) collective-permute-start(f32[8,64,128]{2,1,0:T(8,128)S(1)} %get-tuple-element.80.sent_b), channel_id=1, source_target_pairs={{2,4},{4,2},{6,8},{8,6},{10,12},{12,10},{14,16},{16,14},{18,20},{2... | collective-permute-start | bytes 786440 | tf_op jit(solution)/shard_map/ppermute | solution.py:756
  40.0 12.0 %collective-permute-start.10 = (f32[8,64,128]{2,1,0:T(8,128)S(1)}, f32[8,64,128]{2,1,0:T(8,128)S(1)}, u32[]{:S(2)}, u32[]{:S(2)}) collective-permute-start(f32[8,64,128]{2,1,0:T(8,128)S(1)} %get-tuple-element.78.sent_a), channel_id=1, source_target_pairs={{0,2},{2,0},{4,6},{6,4},{8,10},{10,8},{12,14},{14,12},{16,18},{18,... | collective-permute-start | bytes 786440 | tf_op jit(solution)/shard_map/ppermute | solution.py:753
  44.9 12.9 %all-to-all-start = ((f32[16,8,128]{2,1,0:T(8,128)}), f32[16,8,128]{2,1,0:T(8,128)S(1)}, u32[]{:S(2)}, u32[]{:S(2)}) async-start(f32[16,8,128]{2,1,0:T(8,128)} %front0.1), calls=%async_computation | async-start | bytes 131072 | tf_op jit(solution)/shard_map/all_to_all | solution.py:818

commit v6 on v5

--- a/solution.py
+++ b/solution.py
@@ -480,12 +480,18 @@
     plane = rows_y * rows_x
     start = lax.axis_index("space") * (depth * plane)
 
-    def note(r, found):
-        local = cells[r] - start
-        inside[found] = r
-        return found + jnp.where((local >= -plane) & (local < (depth + 1) * plane), 1, 0)
-
-    inside[inside.shape[0] - 1] = lax.fori_loop(0, cells.shape[0], note, jnp.int32(0))
+    count = cells.shape[0]
+    many = 8 if count % 8 == 0 else 1
+
+    def note(i, found):
+        for j in range(many):
+            r = i * many + j
+            local = cells[r] - start
+            inside[found] = r
+            found += jnp.where((local >= -plane) & (local < (depth + 1) * plane), 1, 0)
+        return found
+
+    inside[count] = lax.fori_loop(0, count // many, note, jnp.int32(0))
 
 
 def rows_of(ref, *index):

time: 59 us -> 58.9 us (level)
  Pallas kernels: 23 us -> 22.1 us
  waiting for transfers between devices: 12.3 us -> 13 us
    all_to_all x1, waiting for transfers between devices: 4.09 us -> 5.19 us  [body(): grads = lax.all_to_all(grads, 'space', 0, 0, tiled=True)]
    pallas_call x3, Pallas kernels: 11.8 us -> 10.9 us  [field_call(): pl.pallas_call(kernel, in_specs=specs, out_specs=[VMEM] * len(outs) + [SM...]
    all_to_all x1, starting transfers between devices: 5.38 us -> 5.99 us  [body(): grads = lax.all_to_all(grads, 'space', 0, 0, tiled=True)]
  transfers between devices with their start and end apart: 13 -> 13, of which waited for: 4 -> 4; matrix products, arithmetic and copies ran while one was open for 0% -> 0% of each run, Pallas kernels for 39% -> 38%
where the time goes in v6:
time: 58.9 us; the launch traced here: 58.5 us
  Pallas kernels  22.1 us (38%)
  starting transfers between devices  21.9 us (37%)
  waiting for transfers between devices  13 us (22%)
  between operations  0.9 us (2%)
  other arithmetic  0.61 us (1%)
    ppermute x4, starting transfers between devices, swap_a(): return lax.ppermute(x, 'space', pairs_a)  12 us
    pallas_call x3, Pallas kernels, field_call(): pl.pallas_call(kernel, in_specs=specs, out_specs=[VMEM] * len(outs) + [SM...  10.9 us
    ppermute x4, waiting for transfers between devices, swap_a(): return lax.ppermute(x, 'space', pairs_a)  7.82 us
    all_to_all x1, starting transfers between devices, body(): grads = lax.all_to_all(grads, 'space', 0, 0, tiled=True)  5.99 us
    all_to_all x1, waiting for transfers between devices, body(): grads = lax.all_to_all(grads, 'space', 0, 0, tiled=True)  5.19 us
    pallas_call x4, Pallas kernels, rim(): pl.pallas_call(functools.partial(rim_kernel, step, late), in_specs=[SMEM]...  3.45 us
    pallas_call x1, Pallas kernels, pack(): pl.pallas_call(pack_kernel, in_specs=[SMEM] * 3 + [ANY] * 3, out_specs=[V...  2.86 us
    ppermute x4, starting transfers between devices, swap_b(): return lax.ppermute(x, 'space', pairs_b)  2.82 us
  transfers between devices with their start and end apart: 13, of which 4 were waited for; matrix products, arithmetic and copies ran while one was open for 0% of the time, Pallas kernels for 38%

profile of v6, /device:TPU:0, one launch (start us, length us, event | category | flops | bytes accessed | tf_op | source)
XLA Modules:
  0.0 58.5 jit_solution(2125427769957861378)
XLA Ops:
  0.6 0.5 collective-permute-start.2
  1.1 0.1 collective-permute-start.3
  1.2 2.9 %pack.1 = (f32[8,64,128]{2,1,0:T(8,128)}, f32[8,64,128]{2,1,0:T(8,128)}, f32[224,128]{1,0:T(8,128)}, f32[224,128]{1,0:T(8,128)}) custom-call(s32[3]{0:T(128)} %refs_0_.3, s32[8]{0:T(128)} %sensors.13, f32[3,8]{1,0:T(4,128)} %bitcast.1, f32[8,4,64,128]{3,2,1,0:T(8,128)} %lam.1, f32[4,4,64,128]{3,2,1,0:T(8,128)} %refs_3_, f32[6,4,32,128]{3,2,1,0:T(8,128)} %refs_1_), custom_call_target="tpu_custom_call" | custom-call | flops 20000000000 | bytes 60000000 | tf_op jit(solution)/shard_map/pack/pallas_call | solution.py:117
  4.1 3.0 %collective-permute-start = (f32[224,128]{1,0:T(8,128)}, f32[224,128]{1,0:T(8,128)S(1)}, u32[]{:S(2)}, u32[]{:S(2)}) collective-permute-start(f32[224,128]{1,0:T(8,128)} %get-tuple-element.45), channel_id=1, source_target_pairs={{0,2},{2,0},{4,6},{6,4},{8,10},{10,8},{12,14},{14,12},{16,18},{18,... | collective-permute-start | bytes 344072 | tf_op jit(solution)/shard_map/ppermute | solution.py:759
  7.1 0.7 %collective-permute-start.1 = (f32[224,128]{1,0:T(8,128)}, f32[224,128]{1,0:T(8,128)S(1)}, u32[]{:S(2)}, u32[]{:S(2)}) collective-permute-start(f32[224,128]{1,0:T(8,128)} %get-tuple-element.46), channel_id=1, source_target_pairs={{2,4},{4,2},{6,8},{8,6},{10,12},{12,10},{14,16},{16,14},{18,20},{2... | collective-permute-start | bytes 344072 | tf_op jit(solution)/shard_map/ppermute | solution.py:762
  7.8 0.0 copy-start.4
  7.8 0.8 %collective-permute-start.7 = (f32[8,64,128]{2,1,0:T(8,128)}, f32[8,64,128]{2,1,0:T(8,128)S(1)}, u32[]{:S(2)}, u32[]{:S(2)}) collective-permute-start(f32[8,64,128]{2,1,0:T(8,128)} %get-tuple-element.72.sent), channel_id=1, source_target_pairs={{2,4},{4,2},{6,8},{8,6},{10,12},{12,10},{14,16},{16,14},{18,20},{2... | collective-permute-start | bytes 786440 | tf_op jit(solution)/shard_map/ppermute | solution.py:762
  8.6 5.5 %collective-permute-start.6 = (f32[8,64,128]{2,1,0:T(8,128)}, f32[8,64,128]{2,1,0:T(8,128)S(1)}, u32[]{:S(2)}, u32[]{:S(2)}) collective-permute-start(f32[8,64,128]{2,1,0:T(8,128)} %get-tuple-element.63.sent), channel_id=1, source_target_pairs={{0,2},{2,0},{4,6},{6,4},{8,10},{10,8},{12,14},{14,12},{16,18},{18,... | collective-permute-start | bytes 786440 | tf_op jit(solution)/shard_map/ppermute | solution.py:759
  14.2 0.5 collective-permute-start.5
  14.7 2.1 %planes.1 = (f32[19,4,64,128]{3,2,1,0:T(8,128)S(1)}, f32[3,4,64,128]{3,2,1,0:T(8,128)S(1)}, f32[3,4,64,128]{3,2,1,0:T(8,128)S(1)}, f32[3,2,64,128]{3,2,1,0:T(8,128)S(1)}) custom-call(s32[3]{0:T(128)S(1)} %copy-done.7, f32[6,4,32,128]{3,2,1,0:T(8,128)S(1)} %copy-done.9, f32[6,4,32,128]{3,2,1,0:T(8,128)S(1)} %collective-permute-done.2.refs_2_, ...), custom_call_target="tpu_custom_call" | custom-call | flops 2000000000 | bytes 60000000 | tf_op jit(solution)/shard_map/planes/pallas_call | solution.py:260
  16.8 2.2 %step2.1 = (f32[8,4,64,128]{3,2,1,0:T(8,128)S(1)}, f32[2,8,64,128]{3,2,1,0:T(8,128)S(1)}) custom-call(s32[8]{0:T(128)S(1)} %copy-done.4, f32[3,8]{1,0:T(4,128)S(1)} %bitcast.2, f32[8,4,64,128]{3,2,1,0:T(8,128)S(1)} %copy-done, f32[19,4,64,128]{3,2,1,0:T(8,128)S(1)} %get-tuple-element.55.coef.refs_1_, f32[3,4,64,128]{3,2,1,0:T(8,128)S(1)} %get-tuple-element.56.gain.refs_2_, ...), custom_call_target="tpu_custom_call" | custom-call | flops 40000000 | bytes 4000000 | tf_op jit(solution)/shard_map/step2/pallas_call | solution.py:614
  19.0 0.0 copy-start.1
  19.0 1.0 %ends.1 = (f32[2,5,64,128]{3,2,1,0:T(8,128)S(1)}, f32[2,5,64,128]{3,2,1,0:T(8,128)S(1)}, f32[3,2,64,128]{3,2,1,0:T(8,128)S(1)}, f32[2,15,64,128]{3,2,1,0:T(8,128)S(1)}) custom-call(s32[3]{0:T(128)S(1)} %copy-done.7, f32[19,4,64,128]{3,2,1,0:T(8,128)S(1)} %get-tuple-element.55.coef.refs_1_, f32[3,4,64,128]{3,2,1,0:T(8,128)S(1)} %get-tuple-element.56.gain.refs_2_, ...), custom_call_target="tpu_custom_call" | custom-call | flops 1000000 | bytes 1000000 | tf_op jit(solution)/shard_map/ends/pallas_call | solution.py:367
  20.1 0.0 copy-start.5
  20.1 0.0 copy-start.6
  20.1 0.9 %rim2b.1 = (f32[8,64,128]{2,1,0:T(8,128)S(1)}, f32[8,64,128]{2,1,0:T(8,128)S(1)}) custom-call(s32[8]{0:T(128)S(1)} %copy-done.4, f32[3,8]{1,0:T(4,128)S(1)} %bitcast.3, f32[2,8,64,128]{3,2,1,0:T(8,128)S(1)} %get-tuple-element.62.part_edges, f32[8,64,128]{2,1,0:T(8,128)S(1)} %collective-permute-done.7.got, f32[8,64,128]{2,1,0:T(8,128)S(1)} %copy-done.2, ...), custom_call_target="tpu_custom_call" | custom-call | flops 2000000 | bytes 1500000 | tf_op jit(solution)/shard_map/rim2b/pallas_call | solution.py:676
  21.0 0.7 %collective-permute-start.9 = (f32[8,64,128]{2,1,0:T(8,128)S(1)}, f32[8,64,128]{2,1,0:T(8,128)S(1)}, u32[]{:S(2)}, u32[]{:S(2)}) collective-permute-start(f32[8,64,128]{2,1,0:T(8,128)S(1)} %get-tuple-element.79.sent), channel_id=1, source_target_pairs={{2,4},{4,2},{6,8},{8,6},{10,12},{12,10},{14,16},{16,14},{18,20},{2... | collective-permute-start | bytes 786440 | tf_op jit(solution)/shard_map/ppermute | solution.py:762
  21.7 4.6 %collective-permute-done.6.got = f32[8,64,128]{2,1,0:T(8,128)S(1)} collective-permute-done((f32[8,64,128]{2,1,0:T(8,128)}, f32[8,64,128]{2,1,0:T(8,128)S(1)}, u32[]{:S(2)}, u32[]{:S(2)}) %collective-permute-start.6) | collective-permute-done | bytes 262176 | tf_op jit(solution)/shard_map/ppermute | solution.py:759
  26.2 0.9 %rim2a.1 = (f32[8,64,128]{2,1,0:T(8,128)S(1)}, f32[8,64,128]{2,1,0:T(8,128)S(1)}) custom-call(s32[8]{0:T(128)S(1)} %copy-done.4, f32[3,8]{1,0:T(4,128)S(1)} %bitcast.4, f32[2,8,64,128]{3,2,1,0:T(8,128)S(1)} %get-tuple-element.62.part_edges, f32[8,64,128]{2,1,0:T(8,128)S(1)} %collective-permute-done.6.got, f32[8,64,128]{2,1,0:T(8,128)S(1)} %copy-done.1, ...), custom_call_target="tpu_custom_call" | custom-call | flops 2000000 | bytes 1500000 | tf_op jit(solution)/shard_map/rim2a/pallas_call | solution.py:676
  27.1 1.6 %collective-permute-start.8 = (f32[8,64,128]{2,1,0:T(8,128)S(1)}, f32[8,64,128]{2,1,0:T(8,128)S(1)}, u32[]{:S(2)}, u32[]{:S(2)}) collective-permute-start(f32[8,64,128]{2,1,0:T(8,128)S(1)} %get-tuple-element.76.sent), channel_id=1, source_target_pairs={{0,2},{2,0},{4,6},{6,4},{8,10},{10,8},{12,14},{14,12},{16,18},{18,... | collective-permute-start | bytes 786440 | tf_op jit(solution)/shard_map/ppermute | solution.py:759
  28.7 6.2 %step1.1 = (f32[8,4,64,128]{3,2,1,0:T(8,128)S(1)}, f32[2,8,64,128]{3,2,1,0:T(8,128)S(1)}, f32[8,128]{1,0:T(8,128)S(1)}, s32[129]{0:T(256)S(1)}) custom-call(s32[8]{0:T(128)S(1)} %copy-done.4, f32[3,8]{1,0:T(4,128)S(1)} %bitcast.5, s32[128]{0:T(128)S(1)} %copy-done.5, s32[128]{0:T(128)S(1)} %copy-done.6, f32[8,4,64,128]{3,2,1,0:T(8,128)S(1)} %get-tuple-element.58.lam, ...), custom_call_target="tpu_custom_call" | custom-call | flops 40000000 | bytes 4000000 | tf_op jit(solution)/shard_map/step1/pallas_call | solution.py:614
  34.9 0.9 %rim1b.1 = (f32[8,64,128]{2,1,0:T(8,128)S(1)}, f32[8,64,128]{2,1,0:T(8,128)S(1)}) custom-call(s32[8]{0:T(128)S(1)} %copy-done.4, f32[3,8]{1,0:T(4,128)S(1)} %bitcast.6, f32[2,8,64,128]{3,2,1,0:T(8,128)S(1)} %get-tuple-element.75.part_edges, f32[8,64,128]{2,1,0:T(8,128)S(1)} %collective-permute-done.9.got, f32[8,64,128]{2,1,0:T(8,128)S(1)} %get-tuple-element.79.sent, ...), custom_call_target="tpu_custom_call" | custom-call | flops 2000000 | bytes 1500000 | tf_op jit(solution)/shard_map/rim1b/pallas_call | solution.py:676
  35.8 0.7 %collective-permute-start.11 = (f32[8,64,128]{2,1,0:T(8,128)S(1)}, f32[8,64,128]{2,1,0:T(8,128)S(1)}, u32[]{:S(2)}, u32[]{:S(2)}) collective-permute-start(f32[8,64,128]{2,1,0:T(8,128)S(1)} %get-tuple-element.80.sent_b), channel_id=1, source_target_pairs={{2,4},{4,2},{6,8},{8,6},{10,12},{12,10},{14,16},{16,14},{18,20},{2... | collective-permute-start | bytes 786440 | tf_op jit(solution)/shard_map/ppermute | solution.py:762
  36.4 2.7 %collective-permute-done.8.got = f32[8,64,128]{2,1,0:T(8,128)S(1)} collective-permute-done((f32[8,64,128]{2,1,0:T(8,128)S(1)}, f32[8,64,128]{2,1,0:T(8,128)S(1)}, u32[]{:S(2)}, u32[]{:S(2)}) %collective-permute-start.8) | collective-permute-done | bytes 262176 | tf_op jit(solution)/shard_map/ppermute | solution.py:759
  39.1 0.9 %rim1a.1 = (f32[8,64,128]{2,1,0:T(8,128)S(1)}, f32[8,64,128]{2,1,0:T(8,128)S(1)}) custom-call(s32[8]{0:T(128)S(1)} %copy-done.4, f32[3,8]{1,0:T(4,128)S(1)} %bitcast.7, f32[2,8,64,128]{3,2,1,0:T(8,128)S(1)} %get-tuple-element.75.part_edges, f32[8,64,128]{2,1,0:T(8,128)S(1)} %collective-permute-done.8.got, f32[8,64,128]{2,1,0:T(8,128)S(1)} %get-tuple-element.76.sent, ...), custom_call_target="tpu_custom_call" | custom-call | flops 2000000 | bytes 1500000 | tf_op jit(solution)/shard_map/rim1a/pallas_call | solution.py:676
  40.0 1.9 %collective-permute-start.10 = (f32[8,64,128]{2,1,0:T(8,128)S(1)}, f32[8,64,128]{2,1,0:T(8,128)S(1)}, u32[]{:S(2)}, u32[]{:S(2)}) collective-permute-start(f32[8,64,128]{2,1,0:T(8,128)S(1)} %get-tuple-element.78.sent_a), channel_id=1, source_target_pairs={{0,2},{2,0},{4,6},{6,4},{8,10},{10,8},{12,14},{14,12},{16,18},{18,... | collective-permute-start | bytes 786440 | tf_op jit(solution)/shard_map/ppermute | solution.py:759
  41.9 2.5 %front0.1 = f32[16,8,128]{2,1,0:T(8,128)} custom-call(s32[128]{0:T(128)S(1)} %copy-done.5, s32[128]{0:T(128)S(1)} %copy-done.6, s32[129]{0:T(256)S(1)} %get-tuple-element.82.inside, f32[8,128]{1,0:T(8,128)S(1)} %get-tuple-element.83.grad_in, f32[8,64,128]{2,1,0:T(8,128)S(1)} %get-tuple-element.84.lam_a, f32[8,64,128]{2,1,0:T(8,128)S(1)} %get-tuple-element.85.lam_b, ...), custom_call_target="tpu_custom_call" | custom-call | flops 10000000 | bytes 4000000 | tf_op jit(solution)/shard_map/front0/pallas_call | solution.py:614
  44.4 6.0 %all-to-all-start = ((f32[16,8,128]{2,1,0:T(8,128)}), f32[16,8,128]{2,1,0:T(8,128)S(1)}, u32[]{:S(2)}, u32[]{:S(2)}) async-start(f32[16,8,128]{2,1,0:T(8,128)} %front0.1), calls=%async_computation | async-start | bytes 131072 | tf_op jit(solution)/shard_map/all_to_all | solution.py:824
  50.4 0.6 %collective-permute-done.10.got_a = f32[8,64,128]{2,1,0:T(8,128)S(1)} collective-permute-done((f32[8,64,128]{2,1,0:T(8,128)S(1)}, f32[8,64,128]{2,1,0:T(8,128)S(1)}, u32[]{:S(2)}, u32[]{:S(2)}) %collective-permute-start.10) | collective-permute-done | bytes 262176 | tf_op jit(solution)/shard_map/ppermute | solution.py:759
  51.0 1.7 %step0.1 = f32[8,4,64,128]{3,2,1,0:T(8,128)} custom-call(f32[8,4,64,128]{3,2,1,0:T(8,128)S(1)} %get-tuple-element.74.base, f32[8,64,128]{2,1,0:T(8,128)S(1)} %get-tuple-element.78.sent_a, f32[8,64,128]{2,1,0:T(8,128)S(1)} %get-tuple-element.80.sent_b, f32[2,15,64,128]{3,2,1,0:T(8,128)S(1)} %get-tuple-element.81.tail, ...), custom_call_target="tpu_custom_call" | custom-call | flops 10000000 | bytes 6000000 | tf_op jit(solution)/shard_map/step0/pallas_call | solution.py:719
  52.7 5.2 %all-to-all-done = f32[16,8,128]{2,1,0:T(8,128)S(1)} async-done(((f32[16,8,128]{2,1,0:T(8,128)}), f32[16,8,128]{2,1,0:T(8,128)S(1)}, u32[]{:S(2)}, u32[]{:S(2)}) %all-to-all-start) | async-done | bytes 65568 | tf_op jit(solution)/shard_map/all_to_all | solution.py:824
  57.9 0.6 %reduce_sum.9 = f32[8,128]{1,0:T(8,128)} reduce(f32[16,8,128]{2,1,0:T(8,128)S(1)} %all-to-all-done, f32[]{:T(128)} %constant.0.clone.1), dimensions={0}, to_apply=%region_0.0 | reduce | flops 15360 | bytes 69636 | tf_op jit(solution)/shard_map/reduce_sum | solution.py:827
  (26 shorter events, 0.1 us)
Async XLA Ops:
  0.6 7.1 %collective-permute-start.2 = (f32[6,4,32,128]{3,2,1,0:T(8,128)}, f32[6,4,32,128]{3,2,1,0:T(8,128)S(1)}, u32[]{:S(2)}, u32[]{:S(2)}) collective-permute-start(f32[6,4,32,128]{3,2,1,0:T(8,128)} %refs_1_), channel_id=1, source_target_pairs={{0,1},{1,0},{2,3},{3,2},{4,5},{5,4},{6,7},{7,6},{8,9},{9,8},{10,11... | collective-permute-start | bytes 1179656 | tf_op jit(solution)/shard_map/ppermute | solution.py:737
  1.1 6.6 %collective-permute-start.3 = (f32[4,4,64,128]{3,2,1,0:T(8,128)}, f32[4,4,64,128]{3,2,1,0:T(8,128)S(1)}, u32[]{:S(2)}, u32[]{:S(2)}) collective-permute-start(f32[4,4,64,128]{3,2,1,0:T(8,128)} %refs_3_), channel_id=1, source_target_pairs={{0,1},{1,0},{2,3},{3,2},{4,5},{5,4},{6,7},{7,6},{8,9},{9,8},{10,11... | collective-permute-start | bytes 1572872 | tf_op jit(solution)/shard_map/ppermute | solution.py:737
  1.2 13.4 %copy-start.7 = (s32[3]{0:T(128)S(1)}, s32[3]{0:T(128)}, u32[]{:S(2)}) copy-start(s32[3]{0:T(128)} %refs_0_.3) | copy-start | bytes 40
  1.2 13.4 %copy-start.8 = (f32[4,4,64,128]{3,2,1,0:T(8,128)S(1)}, f32[4,4,64,128]{3,2,1,0:T(8,128)}, u32[]{:S(2)}) copy-start(f32[4,4,64,128]{3,2,1,0:T(8,128)} %refs_3_) | copy-start | bytes 1572868
  1.2 13.4 %copy-start.9 = (f32[6,4,32,128]{3,2,1,0:T(8,128)S(1)}, f32[6,4,32,128]{3,2,1,0:T(8,128)}, u32[]{:S(2)}) copy-start(f32[6,4,32,128]{3,2,1,0:T(8,128)} %refs_1_) | copy-start | bytes 1179652
  4.1 10.1 %collective-permute-start = (f32[224,128]{1,0:T(8,128)}, f32[224,128]{1,0:T(8,128)S(1)}, u32[]{:S(2)}, u32[]{:S(2)}) collective-permute-start(f32[224,128]{1,0:T(8,128)} %get-tuple-element.45), channel_id=1, source_target_pairs={{0,2},{2,0},{4,6},{6,4},{8,10},{10,8},{12,14},{14,12},{16,18},{18,... | collective-permute-start | bytes 344072 | tf_op jit(solution)/shard_map/ppermute | solution.py:759
  7.1 7.1 %collective-permute-start.1 = (f32[224,128]{1,0:T(8,128)}, f32[224,128]{1,0:T(8,128)S(1)}, u32[]{:S(2)}, u32[]{:S(2)}) collective-permute-start(f32[224,128]{1,0:T(8,128)} %get-tuple-element.46), channel_id=1, source_target_pairs={{2,4},{4,2},{6,8},{8,6},{10,12},{12,10},{14,16},{16,14},{18,20},{2... | collective-permute-start | bytes 344072 | tf_op jit(solution)/shard_map/ppermute | solution.py:762
  7.8 9.0 %copy-start = (f32[8,4,64,128]{3,2,1,0:T(8,128)S(1)}, f32[8,4,64,128]{3,2,1,0:T(8,128)}, u32[]{:S(2)}) copy-start(f32[8,4,64,128]{3,2,1,0:T(8,128)} %lam.1) | copy-start | bytes 3145732
  7.8 9.0 %copy-start.3 = (f32[8,3]{0,1:T(4,128)S(1)}, f32[8,3]{0,1:T(4,128)}, u32[]{:S(2)}) copy-start(f32[8,3]{0,1:T(4,128)} %param.13) | copy-start | bytes 292
  7.8 9.0 %copy-start.4 = (s32[8]{0:T(128)S(1)}, s32[8]{0:T(128)}, u32[]{:S(2)}) copy-start(s32[8]{0:T(128)} %sensors.13) | copy-start | bytes 100
  7.8 12.3 %collective-permute-start.7 = (f32[8,64,128]{2,1,0:T(8,128)}, f32[8,64,128]{2,1,0:T(8,128)S(1)}, u32[]{:S(2)}, u32[]{:S(2)}) collective-permute-start(f32[8,64,128]{2,1,0:T(8,128)} %get-tuple-element.72.sent), channel_id=1, source_target_pairs={{2,4},{4,2},{6,8},{8,6},{10,12},{12,10},{14,16},{16,14},{18,20},{2... | collective-permute-start | bytes 786440 | tf_op jit(solution)/shard_map/ppermute | solution.py:762
  8.6 17.6 %collective-permute-start.6 = (f32[8,64,128]{2,1,0:T(8,128)}, f32[8,64,128]{2,1,0:T(8,128)S(1)}, u32[]{:S(2)}, u32[]{:S(2)}) collective-permute-start(f32[8,64,128]{2,1,0:T(8,128)} %get-tuple-element.63.sent), channel_id=1, source_target_pairs={{0,2},{2,0},{4,6},{6,4},{8,10},{10,8},{12,14},{14,12},{16,18},{18,... | collective-permute-start | bytes 786440 | tf_op jit(solution)/shard_map/ppermute | solution.py:759
  14.2 4.9 %collective-permute-start.4 = (f32[224,128]{1,0:T(8,128)S(1)}, f32[224,128]{1,0:T(8,128)S(1)}, u32[]{:S(2)}, u32[]{:S(2)}) collective-permute-start(f32[224,128]{1,0:T(8,128)S(1)} %collective-permute-done.refs_5_), channel_id=1, source_target_pairs={{0,1},{1,0},{2,3},{3,2},{4,5},{5,4},{6,7},{7,6},{8,9},{9,8},{10,11... | collective-permute-start | bytes 344072 | tf_op jit(solution)/shard_map/ppermute | solution.py:737
  14.2 4.9 %collective-permute-start.5 = (f32[224,128]{1,0:T(8,128)S(1)}, f32[224,128]{1,0:T(8,128)S(1)}, u32[]{:S(2)}, u32[]{:S(2)}) collective-permute-start(f32[224,128]{1,0:T(8,128)S(1)} %collective-permute-done.1.refs_7_), channel_id=1, source_target_pairs={{0,1},{1,0},{2,3},{3,2},{4,5},{5,4},{6,7},{7,6},{8,9},{9,8},{10,11... | collective-permute-start | bytes 344072 | tf_op jit(solution)/shard_map/ppermute | solution.py:737
  19.0 1.1 %copy-start.2 = (f32[8,64,128]{2,1,0:T(8,128)S(1)}, f32[8,64,128]{2,1,0:T(8,128)}, u32[]{:S(2)}) copy-start(f32[8,64,128]{2,1,0:T(8,128)} %get-tuple-element.72.sent) | copy-start | bytes 786436
  19.0 7.2 %copy-start.1 = (f32[8,64,128]{2,1,0:T(8,128)S(1)}, f32[8,64,128]{2,1,0:T(8,128)}, u32[]{:S(2)}) copy-start(f32[8,64,128]{2,1,0:T(8,128)} %get-tuple-element.63.sent) | copy-start | bytes 786436
  20.1 8.6 %copy-start.5 = (s32[128]{0:T(128)S(1)}, s32[128]{0:T(128)}, u32[]{:S(2)}) copy-start(s32[128]{0:T(128)} %cells.3) | copy-start | bytes 1540
  20.1 8.6 %copy-start.6 = (s32[128]{0:T(128)S(1)}, s32[128]{0:T(128)}, u32[]{:S(2)}) copy-start(s32[128]{0:T(128)} %steps.3) | copy-start | bytes 1540
  21.0 13.9 %collective-permute-start.9 = (f32[8,64,128]{2,1,0:T(8,128)S(1)}, f32[8,64,128]{2,1,0:T(8,128)S(1)}, u32[]{:S(2)}, u32[]{:S(2)}) collective-permute-start(f32[8,64,128]{2,1,0:T(8,128)S(1)} %get-tuple-element.79.sent), channel_id=1, source_target_pairs={{2,4},{4,2},{6,8},{8,6},{10,12},{12,10},{14,16},{16,14},{18,20},{2... | collective-permute-start | bytes 786440 | tf_op jit(solution)/shard_map/ppermute | solution.py:762
  27.1 12.0 %collective-permute-start.8 = (f32[8,64,128]{2,1,0:T(8,128)S(1)}, f32[8,64,128]{2,1,0:T(8,128)S(1)}, u32[]{:S(2)}, u32[]{:S(2)}) collective-permute-start(f32[8,64,128]{2,1,0:T(8,128)S(1)} %get-tuple-element.76.sent), channel_id=1, source_target_pairs={{0,2},{2,0},{4,6},{6,4},{8,10},{10,8},{12,14},{14,12},{16,18},{18,... | collective-permute-start | bytes 786440 | tf_op jit(solution)/shard_map/ppermute | solution.py:759
  35.8 14.6 %collective-permute-start.11 = (f32[8,64,128]{2,1,0:T(8,128)S(1)}, f32[8,64,128]{2,1,0:T(8,128)S(1)}, u32[]{:S(2)}, u32[]{:S(2)}) collective-permute-start(f32[8,64,128]{2,1,0:T(8,128)S(1)} %get-tuple-element.80.sent_b), channel_id=1, source_target_pairs={{2,4},{4,2},{6,8},{8,6},{10,12},{12,10},{14,16},{16,14},{18,20},{2... | collective-permute-start | bytes 786440 | tf_op jit(solution)/shard_map/ppermute | solution.py:762
  40.0 11.1 %collective-permute-start.10 = (f32[8,64,128]{2,1,0:T(8,128)S(1)}, f32[8,64,128]{2,1,0:T(8,128)S(1)}, u32[]{:S(2)}, u32[]{:S(2)}) collective-permute-start(f32[8,64,128]{2,1,0:T(8,128)S(1)} %get-tuple-element.78.sent_a), channel_id=1, source_target_pairs={{0,2},{2,0},{4,6},{6,4},{8,10},{10,8},{12,14},{14,12},{16,18},{18,... | collective-permute-start | bytes 786440 | tf_op jit(solution)/shard_map/ppermute | solution.py:759
  44.4 13.5 %all-to-all-start = ((f32[16,8,128]{2,1,0:T(8,128)}), f32[16,8,128]{2,1,0:T(8,128)S(1)}, u32[]{:S(2)}, u32[]{:S(2)}) async-start(f32[16,8,128]{2,1,0:T(8,128)} %front0.1), calls=%async_computation | async-start | bytes 131072 | tf_op jit(solution)/shard_map/all_to_all | solution.py:824
